TPU v7x, 128 devices: a whole 4x4x4 slice. The times are simulated.
128 devices in a mesh: ta: 8 (over y_lo, z), gz: 4 (over x), xy: 4 (over y_hi, core).
Axes of the slice: x: 4, y: 4 (y_hi: 2, y_lo: 2; y = y_hi * 2 + y_lo), z: 4, core: 2. Of those that a mesh axis runs over, the one named last changes fastest.
Arguments:
- fine_solution: bfloat16 [2, 4, 12, 32, 16, 512], P(None, None, None, 'ta', 'gz', 'xy'), may hold values from -6 to 6
- links: bfloat16 [8, 2, 3, 3, 32, 16, 512], P(None, None, None, None, 'ta', 'gz', 'xy'), may hold values from -3.5 to 3.5
- clover: bfloat16 [2, 2, 6, 6, 32, 16, 512], P(None, None, None, None, 'ta', 'gz', 'xy'), may hold values from -1.796875 to 1.796875
- near_null: bfloat16 [12, 2, 12, 32, 16, 512], P(None, None, None, 'ta', 'gz', 'xy'), may hold values from -0.15625 to 0.15625
- coarse_links: float32 [9, 2, 24, 24, 8, 4, 32], P(None, None, None, None, 'ta', 'gz', 'xy'), may hold values from -0.15 to 0.15
- wall_time: int32 [4], replicated, may hold values from 0 to 31
- spin_index: int32 [4], replicated, may hold values from 0 to 3, each once
- wall_colour: float32 [2, 4, 3], replicated, may hold values from -18 to 18
Outputs:
- corrected: float32 [2, 4, 12, 32, 16, 512], P(None, None, None, 'ta', 'gz', 'xy')
Inputs may be any that keep to these rules, and one draw needn't show every extreme that they name: `spin_index`: each right-hand side has its own spin.
All inputs are finite; a program needn't handle non-finite values.
Results may differ from a plain program's by a relative error of at most 0.0003.
Values may be sent and summed in bfloat16 or wider, within the bound.
No kernel may reach another device: no remote copies, remote signals or barrier semaphores. Data moves between devices by JAX's collectives and lax.ppermute only.
A program may use at most 192 MiB of HBM per device.

v0:
```python
import jax
import jax.numpy as jnp
from jax import lax
from jax.sharding import PartitionSpec as P

BLOCK = 4
ITERS = 4
NY = 32


gammas = [
    [[0j, 0j, 1 + 0j, 0j], [0j, 0j, 0j, 1 + 0j], [1 + 0j, 0j, 0j, 0j], [0j, 1 + 0j, 0j, 0j]],
    [[0j, 0j, 1j, 0j], [0j, 0j, 0j, -1j], [-1j, 0j, 0j, 0j], [0j, 1j, 0j, 0j]],
    [[0j, 0j, 0j, 1j], [0j, 0j, 1j, 0j], [0j, -1j, 0j, 0j], [-1j, 0j, 0j, 0j]],
    [[0j, 0j, 0j, -1 + 0j], [0j, 0j, 1 + 0j, 0j], [0j, 1 + 0j, 0j, 0j], [-1 + 0j, 0j, 0j, 0j]],
]
mass_term = 4.1


def extended(block, sides, width):
    for axis, dim in sides:
        count = lax.axis_size(axis)
        forward = [(i, i + 1) for i in range(count - 1)]
        forward.append((count - 1, 0))
        backward = [(target, source) for source, target in forward]
        low = lax.ppermute(
            lax.slice_in_dim(block, block.shape[dim] - width, None, axis=dim), axis, forward
        )
        high = lax.ppermute(lax.slice_in_dim(block, 0, width, axis=dim), axis, backward)
        block = jnp.concatenate([low, block, high], axis=dim)
    return block


def project(sign, direction, field):
    field_re, field_im = field
    out_re = []
    out_im = []
    for spin_out in range(4):
        total_re = field_re[:, spin_out]
        total_im = field_im[:, spin_out]
        for spin_in in range(4):
            entry = gammas[direction][spin_out][spin_in] * sign
            if entry.real != 0:
                total_re = total_re + entry.real * field_re[:, spin_in]
                total_im = total_im + entry.real * field_im[:, spin_in]
            if entry.imag != 0:
                total_re = total_re - entry.imag * field_im[:, spin_in]
                total_im = total_im + entry.imag * field_re[:, spin_in]
        out_re.append(total_re)
        out_im.append(total_im)
    return (jnp.stack(out_re, axis=1), jnp.stack(out_im, axis=1))


def color_apply(link, field):
    total_re = None
    total_im = None
    for colour_in in range(3):
        link_re = link[0][:, colour_in][None, None]
        link_im = link[1][:, colour_in][None, None]
        field_re = field[0][:, :, colour_in][:, :, None]
        field_im = field[1][:, :, colour_in][:, :, None]
        term_re = link_re * field_re - link_im * field_im
        term_im = link_re * field_im + link_im * field_re
        total_re = term_re if total_re is None else total_re + term_re
        total_im = term_im if total_im is None else total_im + term_im
    return (total_re, total_im)


def link_pair(links, which):
    return (links[which, 0].astype(jnp.float32), links[which, 1].astype(jnp.float32))


def clover_apply(clover_blocks, field):
    rows = field[0].shape[0]
    sites = field[0].shape[3:]
    flat_re = field[0].reshape((rows, 12) + sites)
    flat_im = field[1].reshape((rows, 12) + sites)
    parts_re = []
    parts_im = []
    for chirality in range(2):
        block_re = flat_re[:, 6 * chirality : 6 * chirality + 6][:, None]
        block_im = flat_im[:, 6 * chirality : 6 * chirality + 6][:, None]
        entry_re = clover_blocks[chirality, 0].astype(jnp.float32)[None]
        entry_im = clover_blocks[chirality, 1].astype(jnp.float32)[None]
        parts_re.append(jnp.sum(entry_re * block_re - entry_im * block_im, axis=2))
        parts_im.append(jnp.sum(entry_re * block_im + entry_im * block_re, axis=2))
    return (
        jnp.concatenate(parts_re, axis=1).reshape((rows, 4, 3) + sites),
        jnp.concatenate(parts_im, axis=1).reshape((rows, 4, 3) + sites),
    )


def wilson(center, uppers, lowers, links, clover_blocks):
    extra = clover_apply(clover_blocks, center)
    total_re = mass_term * center[0] + extra[0]
    total_im = mass_term * center[1] + extra[1]
    for direction in range(4):
        ahead = color_apply(
            link_pair(links, 2 * direction), project(-1.0, direction, uppers[direction])
        )
        behind = color_apply(
            link_pair(links, 2 * direction + 1), project(1.0, direction, lowers[direction])
        )
        total_re = total_re - 0.5 * (ahead[0] + behind[0])
        total_im = total_im - 0.5 * (ahead[1] + behind[1])
    return (total_re, total_im)


def along_rows(values, row_length, step):
    shape = values.shape
    shaped = values.reshape(shape[:-1] + (shape[-1] // row_length, row_length))
    return jnp.roll(shaped, -step, axis=-1).reshape(shape)


def local_source(wall_time, spin_index, wall_colour, offset, site_shape):
    rows = wall_time.shape[0]
    times = offset + jnp.arange(site_shape[0], dtype=jnp.int32)
    time_mask = (times[None, :] == wall_time[:, None]).astype(jnp.float32)
    spin_mask = (jnp.arange(4, dtype=jnp.int32)[None, :] == spin_index[:, None]).astype(jnp.float32)
    weight = (spin_mask[:, :, None, None] * time_mask[:, None, None, :])[..., None, None]
    full = (rows, 4, 3) + tuple(site_shape)
    source_re = jnp.broadcast_to(weight * wall_colour[0][:, None, :, None, None, None], full)
    source_im = jnp.broadcast_to(weight * wall_colour[1][:, None, :, None, None, None], full)
    return (source_re, source_im)


def block_reduce(values):
    lead = values.shape[:-3]
    ext_t, ext_z, extent = values.shape[-3:]
    ext_x = extent // NY
    shaped = values.reshape(
        lead
        + (ext_t // BLOCK, BLOCK, ext_z // BLOCK, BLOCK, ext_x // BLOCK, BLOCK, NY // BLOCK, BLOCK)
    )
    start = len(lead)
    summed = jnp.sum(shaped, axis=(start + 1, start + 3, start + 5, start + 7))
    return summed.reshape(lead + (ext_t // BLOCK, ext_z // BLOCK, ext_x // BLOCK * (NY // BLOCK)))


def restrict(near_vectors, residual):
    halves_re = []
    halves_im = []
    for chirality in range(2):
        total_re = None
        total_im = None
        for component in range(6):
            position = 6 * chirality + component
            near_re = near_vectors[:, 0, position].astype(jnp.float32)[:, None]
            near_im = near_vectors[:, 1, position].astype(jnp.float32)[:, None]
            res_re = residual[0][:, position][None]
            res_im = residual[1][:, position][None]
            term_re = near_re * res_re + near_im * res_im
            term_im = near_re * res_im - near_im * res_re
            total_re = term_re if total_re is None else total_re + term_re
            total_im = term_im if total_im is None else total_im + term_im
        halves_re.append(block_reduce(total_re))
        halves_im.append(block_reduce(total_im))
    coarse_re = jnp.swapaxes(jnp.concatenate(halves_re, axis=0), 0, 1)
    coarse_im = jnp.swapaxes(jnp.concatenate(halves_im, axis=0), 0, 1)
    return jnp.stack((coarse_re, coarse_im))


def real_stencil(stencil):
    part_re = stencil[:, 0]
    part_im = stencil[:, 1]
    upper = jnp.stack((part_re, -part_im), axis=2)
    lower = jnp.stack((part_im, part_re), axis=2)
    return jnp.stack((upper, lower), axis=1)


def coarse_apply(estimate, uppers, lowers, operator):
    members = [estimate]
    for direction in range(4):
        members.append(uppers[direction])
        members.append(lowers[direction])
    stacked = jnp.stack(members)
    return jnp.einsum(
        "kqipjtza,kprjtza->qritza", operator, stacked, precision=lax.Precision.HIGHEST
    )


def prolong(near_vectors, coarse, site_shape):
    count = near_vectors.shape[0]
    rows = coarse.shape[1]
    agg_t, agg_z, agg_flat = coarse.shape[3:]
    agg_y = NY // BLOCK
    agg_x = agg_flat // agg_y
    shaped = coarse.reshape((2, rows, 2 * count, agg_t, 1, agg_z, 1, agg_x, 1, agg_y, 1))
    shaped = jnp.broadcast_to(
        shaped, (2, rows, 2 * count, agg_t, BLOCK, agg_z, BLOCK, agg_x, BLOCK, agg_y, BLOCK)
    )
    expanded = shaped.reshape((2, rows, 2, count) + tuple(site_shape))
    out_re = []
    out_im = []
    for position in range(12):
        chirality = position // 6
        near_re = near_vectors[:, 0, position].astype(jnp.float32)[None]
        near_im = near_vectors[:, 1, position].astype(jnp.float32)[None]
        coarse_re = expanded[0][:, chirality]
        coarse_im = expanded[1][:, chirality]
        out_re.append(jnp.sum(near_re * coarse_re - near_im * coarse_im, axis=1))
        out_im.append(jnp.sum(near_re * coarse_im + near_im * coarse_re, axis=1))
    return (jnp.stack(out_re, axis=1), jnp.stack(out_im, axis=1))


def local(
    fine_solution, links, clover, near_null, coarse_links, wall_time, spin_index, wall_colour
):
    count_rhs = fine_solution.shape[1]
    local_t = fine_solution.shape[3]
    local_z = fine_solution.shape[4]
    local_sites = fine_solution.shape[5]
    site_shape = (local_t, local_z, local_sites)
    agg_y = NY // BLOCK
    agg_flat = local_sites // NY // BLOCK * agg_y
    folded = fine_solution.reshape((2, count_rhs, 4, 3) + site_shape)
    framed = extended(folded, (("ta", 4), ("gz", 5)), 1)
    widened = extended(folded, (("xy", 6),), NY)
    middle = folded.astype(jnp.float32)
    ahead_list = [
        framed[:, :, :, :, 2:, 1:-1].astype(jnp.float32),
        framed[:, :, :, :, 1:-1, 2:].astype(jnp.float32),
        widened[..., 2 * NY :].astype(jnp.float32),
        along_rows(middle, NY, 1),
    ]
    behind_list = [
        framed[:, :, :, :, :-2, 1:-1].astype(jnp.float32),
        framed[:, :, :, :, 1:-1, :-2].astype(jnp.float32),
        widened[..., :local_sites].astype(jnp.float32),
        along_rows(middle, NY, -1),
    ]
    center = (middle[0], middle[1])
    uppers = [(item[0], item[1]) for item in ahead_list]
    lowers = [(item[0], item[1]) for item in behind_list]
    source = local_source(
        wall_time, spin_index, wall_colour, lax.axis_index("ta") * local_t, site_shape
    )
    applied = wilson(center, uppers, lowers, links, clover)
    residual = (
        (source[0] - applied[0]).reshape((count_rhs, 12) + site_shape),
        (source[1] - applied[1]).reshape((count_rhs, 12) + site_shape),
    )
    restricted = restrict(near_null, residual)
    group_rhs, stencil = (
        lax.all_gather(restricted, "xy", axis=5, tiled=True),
        lax.all_gather(coarse_links, "xy", axis=6, tiled=True),
    )
    operator = real_stencil(stencil)
    estimate = group_rhs
    for step in range(ITERS):
        edged = extended(estimate, (("ta", 3), ("gz", 4)), 1)
        coarse_up = [
            edged[:, :, :, 2:, 1:-1],
            edged[:, :, :, 1:-1, 2:],
            jnp.roll(estimate, -agg_y, axis=5),
            along_rows(estimate, agg_y, 1),
        ]
        coarse_down = [
            edged[:, :, :, :-2, 1:-1],
            edged[:, :, :, 1:-1, :-2],
            jnp.roll(estimate, agg_y, axis=5),
            along_rows(estimate, agg_y, -1),
        ]
        estimate = group_rhs + coarse_apply(estimate, coarse_up, coarse_down, operator)
    estimate = lax.dynamic_slice_in_dim(estimate, lax.axis_index("xy") * agg_flat, agg_flat, axis=5)
    correction = prolong(near_null, estimate, site_shape)
    base = fine_solution.astype(jnp.float32)
    return base + jnp.stack(correction)


def solution(mesh):
    placed = (
        P(None, None, None, "ta", "gz", "xy"),
        P(None, None, None, None, "ta", "gz", "xy"),
        P(None, None, None, None, "ta", "gz", "xy"),
        P(None, None, None, "ta", "gz", "xy"),
        P(None, None, None, None, "ta", "gz", "xy"),
        P(),
        P(),
        P(),
    )
    return jax.shard_map(
        local,
        mesh=mesh,
        in_specs=placed,
        out_specs=P(None, None, None, "ta", "gz", "xy"),
        check_vma=False,
    )
```

profile of v0, /device:TPU:0, one launch (start us, length us, event | category | flops | bytes accessed | tf_op | source)
XLA Modules:
  0.0 773.4 jit_solution(6708579174771712050)
XLA Ops:
  8.3 5.1 collective-permute-start
  32.9 4.7 pad_maximum_fusion
  282.2 9.9 %fusion.29 = f32[4,12,4,4,128]{4,3,2,1,0:T(4,128)S(1)} fusion(f32[4,6,4,4,128]{4,3,2,1,0:T(4,128)S(1)} %copy-done.130, f32[4,6,4,4,128]{4,3,2,1,0:T(4,128)S(1)} %copy-done.131, f32[4,12,4,4,128]{4,3,2,1,0:T(4,128)} %bitcast.245, f32[4,12,4,4,128]{4,3,2,1,0:T(4,128)} %bitcast.241, f32[4,12,4,4,128]{4,3,2,1,0:T(4,128)} %bitcast.237, ...), kind=kLoop, calls=%fused_computation.69 | loop fusion | flops 10223616 | bytes 24773376 | tf_op jit(solution)/shard_map/sub | solution.py:240
  327.8 3.6 copy.370
  331.4 12.1 %fusion.34 = f32[4,12,4,4,128]{4,3,2,1,0:T(4,128)S(1)} fusion(f32[4,6,4,4,128]{4,3,2,1,0:T(4,128)} %get-tuple-element.8, f32[4,6,4,4,128]{4,3,2,1,0:T(4,128)} %get-tuple-element.375, f32[4,12,4,4,128]{4,3,2,1,0:T(4,128)} %bitcast.241, f32[4,12,4,4,128]{4,3,2,1,0:T(4,128)} %bitcast.245, f32[4,12,4,4,128]{4,3,2,1,0:T(4,128)} %bitcast.232, ...), kind=kLoop, calls=%fused_computation.91 | loop fusion | flops 10223616 | bytes 24773376 | tf_op jit(solution)/shard_map/sub | solution.py:241
  359.9 3.6 copy.355
  383.0 18.3 %add_reduce_fusion.3 = f32[12,4,8]{0,2,1:T(8,128)} fusion(f32[4,4,4,4,8,4]{4,5,3,2,1,0:T(4,128)} %copy.373, f32[12,4,4,4,8,4]{0,4,5,3,2,1:T(8,128)} %copy.372, f32[4,4,4,4,8,4]{4,5,3,2,1,0:T(4,128)} %copy.370, f32[12,4,4,4,8,4]{0,4,5,3,2,1:T(8,128)} %copy.369, f32[4,4,4,4,8,4]{4,5,3,2,1,0:T(4,128)} %copy.367, f32[12,4,4,4,8,4]{0,4,5,3,2,1:T(8,128)} %copy.366, ...), kind=kLoop, calls=%fused_computation.12 | loop fusion | flops 2358912 | bytes 1574400 | tf_op jit(solution)/shard_map/reduce_sum | solution.py:136
  401.5 14.6 %add_reduce_fusion.1 = f32[12,4,8]{0,2,1:T(8,128)S(1)} fusion(f32[4,4,4,4,8,4]{4,5,3,2,1,0:T(4,128)S(1)} %copy-done.45, f32[12,4,4,4,8,4]{0,4,5,3,2,1:T(8,128)S(1)} %copy-done.19, f32[4,4,4,4,8,4]{4,5,3,2,1,0:T(4,128)S(1)} %copy-done.28, f32[12,4,4,4,8,4]{0,4,5,3,2,1:T(8,128)S(1)} %copy-done.18, f32[4,4,4,4,8,4]{4,5,3,2,1,0:T(4,128)S(1)} %copy-done.44, ...), kind=kLoop, calls=%fused_computation.10 | loop fusion | flops 2358912 | bytes 1574400 | tf_op jit(solution)/shard_map/reduce_sum | solution.py:136
  438.3 3.6 copy.394
  444.8 3.6 copy.400
  494.1 17.5 %add_reduce_fusion.2 = f32[12,4,8]{0,2,1:T(8,128)S(1)} fusion(f32[4,4,4,4,8,4]{4,5,3,2,1,0:T(4,128)} %copy.409, f32[12,4,4,4,8,4]{0,4,5,3,2,1:T(8,128)} %copy.408, f32[4,4,4,4,8,4]{4,5,3,2,1,0:T(4,128)} %copy.406, f32[12,4,4,4,8,4]{0,4,5,3,2,1:T(8,128)} %copy.405, f32[4,4,4,4,8,4]{4,5,3,2,1,0:T(4,128)} %copy.403, f32[12,4,4,4,8,4]{0,4,5,3,2,1:T(8,128)} %copy.402, ...), kind=kLoop, calls=%fused_computation.11 | loop fusion | flops 2358912 | bytes 1574400 | tf_op jit(solution)/shard_map/reduce_sum | solution.py:136
  511.8 14.4 %add_reduce_fusion = f32[12,4,8]{0,2,1:T(8,128)S(1)} fusion(f32[4,4,4,4,8,4]{4,5,3,2,1,0:T(4,128)S(1)} %copy-done.46, f32[12,4,4,4,8,4]{0,4,5,3,2,1:T(8,128)S(1)} %copy-done.10, f32[4,4,4,4,8,4]{4,5,3,2,1,0:T(4,128)S(1)} %copy-done.34, f32[12,4,4,4,8,4]{0,4,5,3,2,1:T(8,128)S(1)} %copy-done.9, f32[4,4,4,4,8,4]{4,5,3,2,1,0:T(4,128)S(1)} %copy-done.43, ...), kind=kLoop, calls=%fused_computation.9 | loop fusion | flops 2358912 | bytes 1574400 | tf_op jit(solution)/shard_map/reduce_sum | solution.py:136
  526.4 7.0 all_gather.6
  533.4 3.6 collective-permute-start.6
  540.3 4.3 collective-permute-done.7
  547.8 7.7 collective-permute-done.8
  559.1 3.7 slice_bitcast_fusion
  565.5 34.8 %bitcast_dynamic-update-slice_fusion.10 = (f32[9,2,4,24,1,1,32]{3,2,1,6,5,4,0:T(4,128)S(1)}, f32[2,4,24,1,1,32]{2,1,0,5,4,3:T(4,128)S(1)}) fusion(f32[9,1,24,2,24,1,1,32]{4,2,3,0,1,7,6,5:T(8,128)S(1)} %get-tuple-element.64, f32[9,1,24,2,24,1,1,32]{4,2,3,0,1,7,6,5:T(8,128)S(1)} %get-tuple-element.63, ...), kind=kOutput, calls=%fused_computation.249 | convolution fusion | flops 32520192 | bytes 3162112 | tf_op jit(solution)/shard_map/kqipjtza,kprjtza->qritza/dot_general | solution.py:177
  610.4 5.9 collective-permute-done.12
  617.9 35.2 %fusion.4 = f32[32,4,2,24,1,1]{3,1,5,0,2,4:T(4,128)S(1)} fusion(f32[9,2,4,24,1,1,32]{3,2,1,6,5,4,0:T(4,128)S(1)} %constant_dynamic-update-slice_fusion.2, f32[9,1,24,2,24,1,1,32]{4,2,3,0,1,7,6,5:T(8,128)S(1)} %get-tuple-element.64, f32[9,1,24,2,24,1,1,32]{4,2,3,0,1,7,6,5:T(8,128)S(1)} %get-tuple-element.63), kind=kOutput, calls=%fused_computation.5 | convolution fusion | flops 32514048 | bytes 2899968 | tf_op jit(solution)/shard_map/kqipjtza,kprjtza->qritza/dot_general | solution.py:177
  663.0 5.7 collective-permute-done.16
  670.4 35.0 %fusion.2 = f32[32,4,2,24,1,1]{3,1,5,0,2,4:T(4,128)S(1)} fusion(f32[9,2,4,24,1,1,32]{3,2,1,6,5,4,0:T(4,128)S(1)} %constant_dynamic-update-slice_fusion.4, f32[9,1,24,2,24,1,1,32]{4,2,3,0,1,7,6,5:T(8,128)S(1)} %get-tuple-element.64, f32[9,1,24,2,24,1,1,32]{4,2,3,0,1,7,6,5:T(8,128)S(1)} %get-tuple-element.63), kind=kOutput, calls=%fused_computation.3 | convolution fusion | flops 32514048 | bytes 2899968 | tf_op jit(solution)/shard_map/kqipjtza,kprjtza->qritza/dot_general | solution.py:177
  715.2 5.7 collective-permute-done.20
  722.4 35.1 %fusion = f32[32,4,2,24,1,1]{3,1,5,0,2,4:T(4,128)S(1)} fusion(f32[9,2,4,24,1,1,32]{3,2,1,6,5,4,0:T(4,128)S(1)} %constant_dynamic-update-slice_fusion.6, f32[9,1,24,2,24,1,1,32]{4,2,3,0,1,7,6,5:T(8,128)S(1)} %get-tuple-element.64, f32[9,1,24,2,24,1,1,32]{4,2,3,0,1,7,6,5:T(8,128)S(1)} %get-tuple-element.63), kind=kOutput, calls=%fused_computation.1 | convolution fusion | flops 32514048 | bytes 2899968 | tf_op jit(solution)/shard_map/kqipjtza,kprjtza->qritza/dot_general | solution.py:177
  (940 shorter events, 460.8 us)
Async XLA Ops:
  6.5 552.6 %all-gather.2.cloned.1.call-start = ((), (), s32[]{:S(2)}) async-start(), calls=%async_computation | async-start | bytes 8847360 | tf_op jit(solution)/shard_map/all_gather | solution.py:246
  8.3 126.6 %collective-permute-start = (bf16[2,4,4,3,1,4,128]{6,5,4,3,2,1,0:T(4,128)(2,1)}, bf16[2,4,4,3,1,4,128]{6,5,4,3,2,1,0:T(4,128)(2,1)}, u32[]{:S(2)}, u32[]{:S(2)}) collective-permute-start(bf16[2,4,4,3,1,4,128]{6,5,4,3,2,1,0:T(4,128)(2,1)} %get-tuple-element.230), channel_id=1, source_target_pairs={{16,0},{32,16},{48,32},{64,48},{80,64},{96,80},{112,96},{0,112},{1... | collective-permute-start | bytes 294920 | tf_op jit(solution)/shard_map/ppermute | solution.py:29
  13.4 121.5 %collective-permute-start.1 = (bf16[2,4,4,3,1,4,128]{6,5,4,3,2,1,0:T(4,128)(2,1)}, bf16[2,4,4,3,1,4,128]{6,5,4,3,2,1,0:T(4,128)(2,1)}, u32[]{:S(2)}, u32[]{:S(2)}) collective-permute-start(bf16[2,4,4,3,1,4,128]{6,5,4,3,2,1,0:T(4,128)(2,1)} %get-tuple-element.229), channel_id=1, source_target_pairs={{0,16},{16,32},{32,48},{48,64},{64,80},{80,96},{96,112},{112,0},{1... | collective-permute-start | bytes 294920 | tf_op jit(solution)/shard_map/ppermute | solution.py:26
  15.7 204.7 %collective-permute-start.4 = (bf16[2,4,4,3,4,4,32]{6,5,4,3,2,1,0:T(4,128)(2,1)}, bf16[2,4,4,3,4,4,32]{6,5,4,3,2,1,0:T(4,128)(2,1)}, u32[]{:S(2)}, u32[]{:S(2)}) collective-permute-start(bf16[2,4,4,3,4,4,32]{6,5,4,3,2,1,0:T(4,128)(2,1)} %get-tuple-element.237), channel_id=1, source_target_pairs={{1,0},{2,1},{3,2},{0,3},{5,4},{6,5},{7,6},{4,7},{9,8},{10,9},{11,1... | collective-permute-start | bytes 294920 | tf_op jit(solution)/shard_map/ppermute | solution.py:29
  17.8 202.6 %collective-permute-start.5 = (bf16[2,4,4,3,4,4,32]{6,5,4,3,2,1,0:T(4,128)(2,1)}, bf16[2,4,4,3,4,4,32]{6,5,4,3,2,1,0:T(4,128)(2,1)}, u32[]{:S(2)}, u32[]{:S(2)}) collective-permute-start(bf16[2,4,4,3,4,4,32]{6,5,4,3,2,1,0:T(4,128)(2,1)} %get-tuple-element.238), channel_id=1, source_target_pairs={{0,1},{1,2},{2,3},{3,0},{4,5},{5,6},{6,7},{7,4},{8,9},{9,10},{10,1... | collective-permute-start | bytes 294920 | tf_op jit(solution)/shard_map/ppermute | solution.py:26
  137.5 82.9 %collective-permute-start.2 = (bf16[2,4,4,3,6,1,128]{6,5,4,3,2,1,0:T(2,128)(2,1)}, bf16[2,4,4,3,6,1,128]{6,5,4,3,2,1,0:T(2,128)(2,1)}, u32[]{:S(2)}, u32[]{:S(2)}) collective-permute-start(bf16[2,4,4,3,6,1,128]{6,5,4,3,2,1,0:T(2,128)(2,1)} %get-tuple-element.155), channel_id=1, source_target_pairs={{4,0},{8,4},{12,8},{0,12},{5,1},{9,5},{13,9},{1,13},{6,2},{10,6},{... | collective-permute-start | bytes 442376 | tf_op jit(solution)/shard_map/ppermute | solution.py:29
  140.3 80.2 %collective-permute-start.3 = (bf16[2,4,4,3,6,1,128]{6,5,4,3,2,1,0:T(2,128)(2,1)}, bf16[2,4,4,3,6,1,128]{6,5,4,3,2,1,0:T(2,128)(2,1)}, u32[]{:S(2)}, u32[]{:S(2)}) collective-permute-start(bf16[2,4,4,3,6,1,128]{6,5,4,3,2,1,0:T(2,128)(2,1)} %get-tuple-element.156), channel_id=1, source_target_pairs={{0,4},{4,8},{8,12},{12,0},{1,5},{5,9},{9,13},{13,1},{2,6},{6,10},{... | collective-permute-start | bytes 442376 | tf_op jit(solution)/shard_map/ppermute | solution.py:26
  227.4 54.4 %copy-start.86 = (f32[4,4,3,4,4,128]{5,4,3,2,1,0:T(4,128)}, f32[4,4,3,4,4,128]{5,4,3,2,1,0:T(4,128)S(1)}, u32[]{:S(2)}) copy-start(f32[4,4,3,4,4,128]{5,4,3,2,1,0:T(4,128)S(1)} %mul.3357) | copy-start | bytes 1179652
  533.4 6.9 collective-permute-start.6
  537.0 7.6 collective-permute-start.7
  544.7 10.8 %collective-permute-start.8 = (f32[2,4,24,3,1,32]{2,1,0,5,4,3:T(4,128)S(1)}, f32[2,4,24,3,1,32]{2,1,0,5,4,3:T(4,128)S(1)}, u32[]{:S(2)}, u32[]{:S(2)}) collective-permute-start(f32[2,4,24,3,1,32]{2,1,0,5,4,3:T(4,128)S(1)} %pad_maximum_fusion.29), channel_id=1, source_target_pairs={{4,0},{8,4},{12,8},{0,12},{5,1},{9,5},{13,9},{1,13},{6,2},{10,6},{... | collective-permute-start | bytes 221192 | tf_op jit(solution)/shard_map/ppermute | solution.py:29
  547.7 11.2 %collective-permute-start.9 = (f32[2,4,24,3,1,32]{2,1,0,5,4,3:T(4,128)S(1)}, f32[2,4,24,3,1,32]{2,1,0,5,4,3:T(4,128)S(1)}, u32[]{:S(2)}, u32[]{:S(2)}) collective-permute-start(f32[2,4,24,3,1,32]{2,1,0,5,4,3:T(4,128)S(1)} %pad_maximum_fusion.29), channel_id=1, source_target_pairs={{0,4},{4,8},{8,12},{12,0},{1,5},{5,9},{9,13},{13,1},{2,6},{6,10},{... | collective-permute-start | bytes 221192 | tf_op jit(solution)/shard_map/ppermute | solution.py:26
  600.4 5.0 collective-permute-start.10
  601.0 7.1 collective-permute-start.11
  608.2 8.0 %collective-permute-start.12 = (f32[2,4,24,3,1,32]{2,1,0,5,4,3:T(4,128)S(1)}, f32[2,4,24,3,1,32]{2,1,0,5,4,3:T(4,128)S(1)}, u32[]{:S(2)}, u32[]{:S(2)}) collective-permute-start(f32[2,4,24,3,1,32]{2,1,0,5,4,3:T(4,128)S(1)} %pad_maximum_fusion.30), channel_id=1, source_target_pairs={{4,0},{8,4},{12,8},{0,12},{5,1},{9,5},{13,9},{1,13},{6,2},{10,6},{... | collective-permute-start | bytes 221192 | tf_op jit(solution)/shard_map/ppermute | solution.py:29
  608.6 9.1 %collective-permute-start.13 = (f32[2,4,24,3,1,32]{2,1,0,5,4,3:T(4,128)S(1)}, f32[2,4,24,3,1,32]{2,1,0,5,4,3:T(4,128)S(1)}, u32[]{:S(2)}, u32[]{:S(2)}) collective-permute-start(f32[2,4,24,3,1,32]{2,1,0,5,4,3:T(4,128)S(1)} %pad_maximum_fusion.30), channel_id=1, source_target_pairs={{0,4},{4,8},{8,12},{12,0},{1,5},{5,9},{9,13},{13,1},{2,6},{6,10},{... | collective-permute-start | bytes 221192 | tf_op jit(solution)/shard_map/ppermute | solution.py:26
  653.3 5.0 collective-permute-start.14
  653.7 7.1 collective-permute-start.15
  660.8 7.8 %collective-permute-start.16 = (f32[2,4,24,3,1,32]{2,1,0,5,4,3:T(4,128)S(1)}, f32[2,4,24,3,1,32]{2,1,0,5,4,3:T(4,128)S(1)}, u32[]{:S(2)}, u32[]{:S(2)}) collective-permute-start(f32[2,4,24,3,1,32]{2,1,0,5,4,3:T(4,128)S(1)} %pad_maximum_fusion.31), channel_id=1, source_target_pairs={{4,0},{8,4},{12,8},{0,12},{5,1},{9,5},{13,9},{1,13},{6,2},{10,6},{... | collective-permute-start | bytes 221192 | tf_op jit(solution)/shard_map/ppermute | solution.py:29
  661.2 9.0 %collective-permute-start.17 = (f32[2,4,24,3,1,32]{2,1,0,5,4,3:T(4,128)S(1)}, f32[2,4,24,3,1,32]{2,1,0,5,4,3:T(4,128)S(1)}, u32[]{:S(2)}, u32[]{:S(2)}) collective-permute-start(f32[2,4,24,3,1,32]{2,1,0,5,4,3:T(4,128)S(1)} %pad_maximum_fusion.31), channel_id=1, source_target_pairs={{0,4},{4,8},{8,12},{12,0},{1,5},{5,9},{9,13},{13,1},{2,6},{6,10},{... | collective-permute-start | bytes 221192 | tf_op jit(solution)/shard_map/ppermute | solution.py:26
  705.5 5.2 collective-permute-start.18
  705.8 7.1 collective-permute-start.19
  713.1 7.8 %collective-permute-start.20 = (f32[2,4,24,3,1,32]{2,1,0,5,4,3:T(4,128)S(1)}, f32[2,4,24,3,1,32]{2,1,0,5,4,3:T(4,128)S(1)}, u32[]{:S(2)}, u32[]{:S(2)}) collective-permute-start(f32[2,4,24,3,1,32]{2,1,0,5,4,3:T(4,128)S(1)} %pad_maximum_fusion.32), channel_id=1, source_target_pairs={{4,0},{8,4},{12,8},{0,12},{5,1},{9,5},{13,9},{1,13},{6,2},{10,6},{... | collective-permute-start | bytes 221192 | tf_op jit(solution)/shard_map/ppermute | solution.py:29
  713.2 9.0 %collective-permute-start.21 = (f32[2,4,24,3,1,32]{2,1,0,5,4,3:T(4,128)S(1)}, f32[2,4,24,3,1,32]{2,1,0,5,4,3:T(4,128)S(1)}, u32[]{:S(2)}, u32[]{:S(2)}) collective-permute-start(f32[2,4,24,3,1,32]{2,1,0,5,4,3:T(4,128)S(1)} %pad_maximum_fusion.32), channel_id=1, source_target_pairs={{0,4},{4,8},{8,12},{12,0},{1,5},{5,9},{9,13},{13,1},{2,6},{6,10},{... | collective-permute-start | bytes 221192 | tf_op jit(solution)/shard_map/ppermute | solution.py:26
  (224 other events, 4864.0 us)
Sparse Core Ops, SparseCore 0:
  21.0 56.4 all-gather.1
where the time goes:
time: 788 us; the launch traced here: 773 us
  local copies, waits for them, and re-layouts  383 us (49%)
  other arithmetic  140 us (18%)
  matrix products  140 us (18%)
  waiting for transfers between devices  55.8 us (7%)
  starting transfers between devices  29.4 us (4%)
  between operations  17.7 us (2%)
    mul x48, local copies, waits for them, and re-layouts, restrict(): term_re = near_re * res_re + near_im * res_im  155 us
    dot_general x4, matrix products, coarse_apply(): jnp.einsum('kqipjtza,kprjtza->qritza', operator, stacked, precision=lax.P...  140 us
    reduce_sum x4, other arithmetic, block_reduce(): summed = jnp.sum(shaped, axis=(start + 1, start + 3, start + 5, start + 7))  64.8 us
    mul x120, local copies, waits for them, and re-layouts, color_apply(): term_re = link_re * field_re - link_im * field_im  62 us
    convert_element_type x24, local copies, waits for them, and re-layouts, restrict(): near_im = near_vectors[:, 1, position].astype(jnp.float32)[:, None]  38.9 us
    ppermute x11, waiting for transfers between devices, extended(): lax.ppermute(lax.slice_in_dim(block, 0, width, axis=dim), axis, backward)  36.5 us
    convert_element_type x22, local copies, waits for them, and re-layouts, restrict(): near_re = near_vectors[:, 0, position].astype(jnp.float32)[:, None]  34.4 us
    slice x13, local copies, waits for them, and re-layouts, restrict(): near_im = near_vectors[:, 1, position].astype(jnp.float32)[:, None]  19.9 us
  transfers between devices with their start and end apart: 23, of which 16 were waited for; matrix products, arithmetic and copies ran while one was open for 65% of the time, Pallas kernels for 0%

commit v1 on v0

v1 whole, which is shorter than its diff:
```python
import jax
import jax.numpy as jnp
from jax import lax
from jax.experimental import pallas as pl
from jax.experimental.pallas import tpu as pltpu
from jax.sharding import PartitionSpec as P

BLOCK = 4
ITERS = 4
NY = 32
ROWS = 16
LANES = 128
HALF = 8
MASS = 4.1
F32 = jnp.float32
BF16 = jnp.bfloat16

gammas = [
    [[0j, 0j, 1 + 0j, 0j], [0j, 0j, 0j, 1 + 0j], [1 + 0j, 0j, 0j, 0j], [0j, 1 + 0j, 0j, 0j]],
    [[0j, 0j, 1j, 0j], [0j, 0j, 0j, -1j], [-1j, 0j, 0j, 0j], [0j, 1j, 0j, 0j]],
    [[0j, 0j, 0j, 1j], [0j, 0j, 1j, 0j], [0j, -1j, 0j, 0j], [-1j, 0j, 0j, 0j]],
    [[0j, 0j, 0j, -1 + 0j], [0j, 0j, 1 + 0j, 0j], [0j, 1 + 0j, 0j, 0j], [-1 + 0j, 0j, 0j, 0j]],
]


def vmem_params(mib):
    return pltpu.CompilerParams(vmem_limit_bytes=mib * 1024 * 1024)


def lane_index(rows):
    return lax.broadcasted_iota(jnp.int32, (rows, LANES), 1)


def row_index(rows):
    return lax.broadcasted_iota(jnp.int32, (rows, LANES), 0)


def turn_lanes(value, shift):
    return pltpu.roll(value, shift % LANES, 1)


def pack_kernel(psi_ref, t_first, t_last, z_first, z_last, x_first, x_last, stage):
    lanes = lane_index(ROWS)

    def body(component, carry):
        part = component // 12
        c = component % 12
        fields = [psi_ref[part, r, c].astype(F32) for r in range(4)]
        for r in range(4):
            stage[16 * r : 16 * r + 16, :] = fields[r]
        t_first[component] = jnp.concatenate([stage[16 * r : 16 * r + 4, :] for r in range(4)], axis=0).astype(BF16)
        t_last[component] = jnp.concatenate([stage[16 * r + 12 : 16 * r + 16, :] for r in range(4)], axis=0).astype(BF16)
        z_first[component] = stage[pl.ds(0, 16, stride=4), :].astype(BF16)
        z_last[component] = stage[pl.ds(3, 16, stride=4), :].astype(BF16)
        low = fields[0]
        high = turn_lanes(fields[0], 32)
        for r in range(1, 4):
            mask = lanes >= 32 * r
            low = jnp.where(mask, turn_lanes(fields[r], 32 * r), low)
            high = jnp.where(mask, turn_lanes(fields[r], 32 * r + 32), high)
        x_first[component] = low.astype(BF16)
        x_last[component] = high.astype(BF16)
        return carry

    lax.fori_loop(0, 24, body, 0)


def pack(psi):
    slab = jax.ShapeDtypeStruct((24, ROWS, LANES), BF16)
    vm = pl.BlockSpec(memory_space=pltpu.VMEM)
    return pl.pallas_call(
        pack_kernel,
        out_shape=(slab,) * 6,
        in_specs=[vm],
        out_specs=(vm,) * 6,
        scratch_shapes=[pltpu.VMEM((64, LANES), F32)],
        compiler_params=vmem_params(16),
    )(psi)


def times(entry, re, im):
    if entry.real != 0:
        return (entry.real, re), (entry.real, im)
    return (-entry.imag, im), (entry.imag, re)


def add_signed(total, term):
    sign, value = term
    if total is None:
        return value if sign > 0 else -value
    return total + value if sign > 0 else total - value


def fine_kernel(
    when_ref, spin_ref, offset_ref, wall_ref, psi_ref, tp_ref, tm_ref, zp_ref, zm_ref, xp_ref, xm_ref,
    links_ref, clover_ref, near_ref, out_ref, halo, shifted, text, residual, rows_ref,
):
    lanes16 = lane_index(ROWS)
    y16 = lanes16 % NY
    for which, ref in enumerate((tp_ref, tm_ref, zp_ref, zm_ref, xp_ref, xm_ref)):
        def widen(component, carry, which=which, ref=ref):
            halo[which, component] = ref[component].astype(F32)
            return carry
        lax.fori_loop(0, 24, widen, 0)

    def prepare(component, r):
        part = component // 12
        c = component % 12
        center = psi_ref[part, r, c].astype(F32)
        four = pl.multiple_of(4 * r, 4)
        text[component, 0:4, :] = halo[1, component, pl.ds(four, 4), :]
        text[component, 4:20, :] = center
        text[component, 20:24, :] = halo[0, component, pl.ds(four, 4), :]
        shifted[0, component] = center
        shifted[1, component] = pltpu.roll(center, ROWS - 1, 0)
        shifted[1, component, pl.ds(3, 4, stride=4), :] = halo[2, component, pl.ds(four, 4), :]
        shifted[2, component] = pltpu.roll(center, 1, 0)
        shifted[2, component, pl.ds(0, 4, stride=4), :] = halo[3, component, pl.ds(four, 4), :]
        above = pltpu.roll(halo[4, component], lax.rem(96 - 32 * r + LANES, LANES), 1)
        below = pltpu.roll(halo[5, component], lax.rem(LANES - 32 * r, LANES), 1)
        shifted[3, component] = jnp.where(lanes16 < 96, turn_lanes(center, -32), above)
        shifted[4, component] = jnp.where(lanes16 >= 32, turn_lanes(center, 32), below)
        shifted[5, component] = jnp.where(y16 < NY - 1, turn_lanes(center, -1), turn_lanes(center, NY - 1))
        shifted[6, component] = jnp.where(y16 > 0, turn_lanes(center, 1), turn_lanes(center, 1 - NY))

    def rhs(r, carry):
        def prep(component, inner):
            prepare(component, r)
            return inner
        lax.fori_loop(0, 24, prep, 0)
        when = when_ref[r]
        spin = spin_ref[r]
        for half in range(2):
            low = HALF * half

            def field(direction, sign, spin_in, colour, part):
                component = 12 * part + 3 * spin_in + colour
                if direction == 0:
                    start = low + 8 if sign < 0 else low
                    return text[component, start : start + HALF, :]
                which = 2 * direction - (1 if sign < 0 else 0)
                return shifted[which, component, low : low + HALF, :]

            total = [[[None, None] for _ in range(3)] for _ in range(4)]
            for direction in range(4):
                for sign in (-1.0, 1.0):
                    number = 2 * direction + (0 if sign < 0 else 1)
                    half_field = []
                    for s in range(2):
                        partner = 2 if gammas[direction][s][2] != 0 else 3
                        entry = gammas[direction][s][partner] * sign
                        row = []
                        for colour in range(3):
                            re = field(direction, sign, s, colour, 0)
                            im = field(direction, sign, s, colour, 1)
                            pre = field(direction, sign, partner, colour, 0)
                            pim = field(direction, sign, partner, colour, 1)
                            a, b = times(entry, pre, pim)
                            row.append((add_signed(re, a), add_signed(im, b)))
                        half_field.append(row)
                    for out in range(3):
                        link = [
                            (
                                links_ref[number, 0, out, inn].astype(F32)[low : low + HALF],
                                links_ref[number, 1, out, inn].astype(F32)[low : low + HALF],
                            )
                            for inn in range(3)
                        ]
                        moved = []
                        for s in range(2):
                            re = None
                            im = None
                            for inn in range(3):
                                ure, uim = link[inn]
                                hre, him = half_field[s][inn]
                                tre = ure * hre - uim * him
                                tim = ure * him + uim * hre
                                re = tre if re is None else re + tre
                                im = tim if im is None else im + tim
                            moved.append((re, im))
                        for s in range(2):
                            for part in range(2):
                                total[s][out][part] = add_signed(total[s][out][part], (1.0, moved[s][part]))
                        for s in range(2, 4):
                            source = 0 if gammas[direction][s][0] != 0 else 1
                            entry = gammas[direction][s][source] * sign
                            terms = times(entry, *moved[source])
                            for part in range(2):
                                total[s][out][part] = add_signed(total[s][out][part], terms[part])
            times_here = offset_ref[0] + 2 * half + row_index(HALF) // BLOCK
            at_wall = times_here == when
            for chirality in range(2):
                values = [
                    (
                        shifted[0, 6 * chirality + i, low : low + HALF, :],
                        shifted[0, 12 + 6 * chirality + i, low : low + HALF, :],
                    )
                    for i in range(6)
                ]
                for i in range(6):
                    re = MASS * values[i][0]
                    im = MASS * values[i][1]
                    for j in range(6):
                        cre = clover_ref[chirality, 0, i, j].astype(F32)[low : low + HALF]
                        cim = clover_ref[chirality, 1, i, j].astype(F32)[low : low + HALF]
                        re = re + (cre * values[j][0] - cim * values[j][1])
                        im = im + (cre * values[j][1] + cim * values[j][0])
                    s = 2 * chirality + i // 3
                    colour = i % 3
                    re = 0.5 * total[s][colour][0] - re
                    im = 0.5 * total[s][colour][1] - im
                    here = at_wall & (spin == s)
                    zero = jnp.zeros((HALF, LANES), F32)
                    re = re + jnp.where(here, wall_ref[r * 3 + colour], zero)
                    im = im + jnp.where(here, wall_ref[12 + r * 3 + colour], zero)
                    residual[r, 6 * chirality + i, low : low + HALF, :] = re
                    residual[r, 12 + 6 * chirality + i, low : low + HALF, :] = im
        return carry

    lax.fori_loop(0, 4, rhs, 0)

    for part in range(2):
        rows_ref[part] = jnp.zeros((LANES, LANES), F32)

    def vector(v, carry):
        for chirality in range(2):
            acc = [[None, None] for _ in range(4)]
            for c in range(6):
                position = 6 * chirality + c
                nre16 = near_ref[v, 0, position].astype(F32)
                nim16 = near_ref[v, 1, position].astype(F32)
                for half in range(2):
                    low = HALF * half
                    nre = nre16[low : low + HALF]
                    nim = nim16[low : low + HALF]
                    for r in range(4):
                        rre = residual[r, position, low : low + HALF, :]
                        rim = residual[r, 12 + position, low : low + HALF, :]
                        tre = nre * rre + nim * rim
                        tim = nre * rim - nim * rre
                        acc[r][0] = tre if acc[r][0] is None else acc[r][0] + tre
                        acc[r][1] = tim if acc[r][1] is None else acc[r][1] + tim
            for r in range(4):
                for part in range(2):
                    rows_ref[part, pl.ds(r * 32 + chirality * 12 + v, 1), :] = jnp.sum(
                        acc[r][part], axis=0, keepdims=True
                    )
        return carry

    lax.fori_loop(0, 12, vector, 0)
    member = ((lane_index(HALF) % NY) // BLOCK == row_index(HALF)).astype(F32)
    for part in range(2):
        out_ref[part] = lax.dot_general(
            member, rows_ref[part], (((1,), (1,)), ((), ())),
            precision=lax.Precision.HIGHEST, preferred_element_type=F32,
        )


def fine(wall_time, spin_index, offset, wall, psi, halos, links, clover, near):
    vm = pl.BlockSpec(memory_space=pltpu.VMEM)
    sm = pl.BlockSpec(memory_space=pltpu.SMEM)
    return pl.pallas_call(
        fine_kernel,
        out_shape=jax.ShapeDtypeStruct((2, HALF, LANES), F32),
        in_specs=[sm, sm, sm, sm] + [vm] * 10,
        out_specs=vm,
        scratch_shapes=[
            pltpu.VMEM((6, 24, ROWS, LANES), F32),
            pltpu.VMEM((7, 24, ROWS, LANES), F32),
            pltpu.VMEM((24, 24, LANES), F32),
            pltpu.VMEM((4, 24, ROWS, LANES), F32),
            pltpu.VMEM((2, LANES, LANES), F32),
        ],
        compiler_params=vmem_params(32),
    )(wall_time, spin_index, offset, wall, psi, *halos, links, clover, near)


def spread_kernel(stencil_ref, out_ref):
    def body(index, carry):
        block = stencil_ref[index]
        seg = jnp.concatenate([block, jnp.zeros((HALF, 8), F32)], axis=1)
        out_ref[index] = jnp.concatenate([seg] * 4, axis=1)
        return carry

    lax.fori_loop(0, 9 * 2 * 24, body, 0)


def spread(stencil):
    vm = pl.BlockSpec(memory_space=pltpu.VMEM)
    return pl.pallas_call(
        spread_kernel,
        out_shape=jax.ShapeDtypeStruct((9 * 2 * 24, HALF, LANES), F32),
        in_specs=[vm],
        out_specs=vm,
        compiler_params=vmem_params(16),
    )(stencil)


def merge(low, high, width, inside):
    if high is None:
        high = jnp.zeros_like(low)
    keep = jnp.where(inside, low, high)
    other = jnp.where(inside, high, low)
    return keep + jnp.where(inside, turn_lanes(other, -width), turn_lanes(other, width))


def coarse_step(estimate, neighbours, restricted_ref, operator_ref):
    members = [estimate] + neighbours
    lanes = lane_index(HALF)
    out = []
    sums = [[None] * 24, [None] * 24]
    for i in range(24):
        re = None
        im = None
        for k in range(9):
            cre = operator_ref[(k * 2) * 24 + i]
            cim = operator_ref[(k * 2 + 1) * 24 + i]
            ere, eim = members[k]
            tre = cre * ere - cim * eim
            tim = cre * eim + cim * ere
            re = tre if re is None else re + tre
            im = tim if im is None else im + tim
        sums[0][i] = re
        sums[1][i] = im
    for part in range(2):
        values = sums[part] + [None] * 8
        width = 16
        while width >= 1:
            inside = (lanes // width) % 2 == 0
            count = width
            values = [
                None if values[i] is None else merge(values[i], values[i + count], width, inside)
                for i in range(count)
            ]
            width //= 2
        out.append(restricted_ref[part] + values[0])
    return out


def coarse_neighbours(estimate, refs):
    neighbours = [(ref[0], ref[1]) for ref in refs]
    neighbours.append(tuple(pltpu.roll(value, HALF - 1, 0) for value in estimate))
    neighbours.append(tuple(pltpu.roll(value, 1, 0) for value in estimate))
    return neighbours


def coarse_kernel(e_ref, tp, tm, zp, zm, xp, xm, r_ref, operator_ref, out_ref):
    estimate = (e_ref[0], e_ref[1])
    out = coarse_step(estimate, coarse_neighbours(estimate, (tp, tm, zp, zm, xp, xm)), r_ref, operator_ref)
    out_ref[0] = out[0]
    out_ref[1] = out[1]


def coarse(estimate, halos, restricted, operator):
    vm = pl.BlockSpec(memory_space=pltpu.VMEM)
    return pl.pallas_call(
        coarse_kernel,
        out_shape=jax.ShapeDtypeStruct((2, HALF, LANES), F32),
        in_specs=[vm] * 9,
        out_specs=vm,
        compiler_params=vmem_params(16),
    )(estimate, *halos, restricted, operator)


def last_kernel(e_ref, tp, tm, zp, zm, xp, xm, r_ref, operator_ref, psi_ref, near_ref, out_ref, wide):
    estimate = (e_ref[0], e_ref[1])
    final = coarse_step(estimate, coarse_neighbours(estimate, (tp, tm, zp, zm, xp, xm)), r_ref, operator_ref)
    member = ((lane_index(HALF) % NY) // BLOCK == row_index(HALF)).astype(F32)
    for part in range(2):
        wide[part] = lax.dot_general(
            final[part], member, (((0,), (0,)), ((), ())),
            precision=lax.Precision.HIGHEST, preferred_element_type=F32,
        )

    def component(c, carry):
        base = (c // 6) * 12
        near = [(near_ref[v, 0, c].astype(F32), near_ref[v, 1, c].astype(F32)) for v in range(12)]
        for r in range(4):
            re = psi_ref[0, r, c].astype(F32)
            im = psi_ref[1, r, c].astype(F32)
            for v in range(12):
                ere = wide[0, pl.ds(r * 32 + base + v, 1), :]
                eim = wide[1, pl.ds(r * 32 + base + v, 1), :]
                nre, nim = near[v]
                re = re + (nre * ere - nim * eim)
                im = im + (nre * eim + nim * ere)
            out_ref[0, r, c] = re
            out_ref[1, r, c] = im
        return carry

    lax.fori_loop(0, 12, component, 0)


def last(estimate, halos, restricted, operator, psi, near):
    vm = pl.BlockSpec(memory_space=pltpu.VMEM)
    return pl.pallas_call(
        last_kernel,
        out_shape=jax.ShapeDtypeStruct((2, 4, 12, ROWS, LANES), F32),
        in_specs=[vm] * 11,
        out_specs=vm,
        scratch_shapes=[pltpu.VMEM((2, LANES, LANES), F32)],
        compiler_params=vmem_params(24),
    )(estimate, *halos, restricted, operator, psi, near)


def send(value, axis, step):
    count = lax.axis_size(axis)
    return lax.ppermute(value, axis, [(i, (i + step) % count) for i in range(count)])


def exchange(value):
    halos = []
    for axis in ("ta", "gz", "xy"):
        halos.append(send(value, axis, -1))
        halos.append(send(value, axis, 1))
    return halos


def local(
    fine_solution, links, clover, near_null, coarse_links, wall_time, spin_index, wall_colour
):
    psi = fine_solution.reshape((2, 4, 12, ROWS, LANES))
    links = links.reshape((8, 2, 3, 3, ROWS, LANES))
    clover = clover.reshape((2, 2, 6, 6, ROWS, LANES))
    near = near_null.reshape((12, 2, 12, ROWS, LANES))
    stencil = jnp.transpose(coarse_links, (0, 1, 2, 4, 5, 6, 3)).reshape((9 * 2 * 24, HALF, 24))
    wall = wall_colour.reshape((24,))
    offset = (lax.axis_index("ta") * 4).astype(jnp.int32).reshape((1,))
    t_first, t_last, z_first, z_last, x_first, x_last = pack(psi)
    halos = [
        send(t_first, "ta", -1),
        send(t_last, "ta", 1),
        send(z_first, "gz", -1),
        send(z_last, "gz", 1),
        send(x_first, "xy", -1),
        send(x_last, "xy", 1),
    ]
    operator = spread(stencil)
    restricted = fine(wall_time, spin_index, offset, wall, psi, halos, links, clover, near)
    estimate = restricted
    for step in range(ITERS - 1):
        estimate = coarse(estimate, exchange(estimate), restricted, operator)
    result = last(estimate, exchange(estimate), restricted, operator, psi, near)
    return result.reshape(fine_solution.shape)


def solution(mesh):
    placed = (
        P(None, None, None, "ta", "gz", "xy"),
        P(None, None, None, None, "ta", "gz", "xy"),
        P(None, None, None, None, "ta", "gz", "xy"),
        P(None, None, None, "ta", "gz", "xy"),
        P(None, None, None, None, "ta", "gz", "xy"),
        P(),
        P(),
        P(),
    )
    return jax.shard_map(
        local,
        mesh=mesh,
        in_specs=placed,
        out_specs=P(None, None, None, "ta", "gz", "xy"),
        check_vma=False,
    )
```

time: 788 us -> 123 us (0.16); the launches traced: 773 us -> 123 us
  local copies, waits for them, and re-layouts: 383 us -> 7.56 us
  matrix products: 140 us -> 0 us
  other arithmetic: 140 us -> 0 us
  Pallas kernels: 0 us -> 53.1 us
  waiting for transfers between devices: 55.8 us -> 9.56 us
  starting transfers between devices: 29.4 us -> 52.4 us
  between operations: 17.7 us -> 0.16 us
    mul x176 -> x0, local copies, waits for them, and re-layouts: 223 us -> none  [the longest x48 155 us: restrict(): term_re = near_re * res_re + near_im * res_im]
    dot_general x4 -> x0, matrix products: 140 us -> none  [coarse_apply(): jnp.einsum('kqipjtza,kprjtza->qritza', operator, stacked, precision=lax.P...]
    convert_element_type x49 -> x0, local copies, waits for them, and re-layouts: 79.3 us -> none  [the longest x24 38.9 us: restrict(): near_im = near_vectors[:, 1, position].astype(jnp.float32)[:, None]]
    reduce_sum x7 -> x0, other arithmetic: 72.4 us -> none  [the longest x4 64.8 us: block_reduce(): summed = jnp.sum(shaped, axis=(start + 1, start + 3, start + 5, start + 7))]
    slice x68 -> x0, local copies, waits for them, and re-layouts: 59.9 us -> none  [the longest x13 19.9 us: restrict(): near_im = near_vectors[:, 1, position].astype(jnp.float32)[:, None]]
    pallas_call x0 -> x7, Pallas kernels: none -> 53.1 us  [the longest x1 31.3 us: spread(): pl.pallas_call(spread_kernel, out_shape=jax.ShapeDtypeStruct((9 * 2 * 24,...]
    ppermute x22 -> x30, waiting for transfers between devices: 55.8 us -> 9.56 us  [send(): lax.ppermute(value, axis, [(i, (i + step) % count) for i in range(count)])]
    convert_element_type x29 -> x0, other arithmetic: 33 us -> none  [the longest x12 13.1 us: restrict(): near_im = near_vectors[:, 1, position].astype(jnp.float32)[:, None]]
  transfers between devices with their start and end apart: 23 -> 30, of which waited for: 16 -> 6; matrix products, arithmetic and copies ran while one was open for 65% -> 1% of each run, Pallas kernels for 0% -> 25%
where the time goes in v1:
time: 123 us
  Pallas kernels  53.1 us (43%)
  starting transfers between devices  52.4 us (43%)
  waiting for transfers between devices  9.56 us (8%)
  local copies, waits for them, and re-layouts  7.56 us (6%)
    ppermute x30, starting transfers between devices, send(): lax.ppermute(value, axis, [(i, (i + step) % count) for i in range(count)])  52.4 us
    pallas_call x1, Pallas kernels, spread(): pl.pallas_call(spread_kernel, out_shape=jax.ShapeDtypeStruct((9 * 2 * 24,...  31.3 us
    pallas_call x1, Pallas kernels, fine(): pl.pallas_call(fine_kernel, out_shape=jax.ShapeDtypeStruct((2, HALF, LANE...  14.3 us
    ppermute x30, waiting for transfers between devices, send(): lax.ppermute(value, axis, [(i, (i + step) % count) for i in range(count)])  9.56 us
    unnamed x17, local copies, waits for them, and re-layouts  7.48 us
    pallas_call x1, Pallas kernels, last(): pl.pallas_call(last_kernel, out_shape=jax.ShapeDtypeStruct((2, 4, 12, ROW...  3.46 us
  transfers between devices with their start and end apart: 30, of which 6 were waited for; matrix products, arithmetic and copies ran while one was open for 1% of the time, Pallas kernels for 25%

profile of v1, /device:TPU:0, one launch (start us, length us, event | category | flops | bytes accessed | tf_op | source)
XLA Modules:
  0.0 122.8 jit_solution(15316155211967113115)
XLA Ops:
  1.0 1.9 %shard_map.82 = (bf16[24,16,128]{2,1,0:T(8,128)(2,1)S(1)}, bf16[24,16,128]{2,1,0:T(8,128)(2,1)S(1)}, bf16[24,16,128]{2,1,0:T(8,128)(2,1)S(1)}, bf16[24,16,128]{2...) custom-call(bf16[2,4,12,16,128]{4,3,2,1,0:T(8,128)(2,1)S(1)} %bitcast.11), custom_call_target="tpu_custom_call" | custom-call | tf_op jit(solution)/shard_map/pallas_call | solution.py:71
  2.9 5.1 %collective-permute-start = (bf16[24,16,128]{2,1,0:T(8,128)(2,1)S(1)}, bf16[24,16,128]{2,1,0:T(8,128)(2,1)S(1)}, u32[]{:S(2)}, u32[]{:S(2)}) collective-permute-start(bf16[24,16,128]{2,1,0:T(8,128)(2,1)S(1)} %get-tuple-element.11), channel_id=1, source_target_pairs={{0,112},{16,0},{32,16},{48,32},{64,48},{80,64},{96,80},{112,96},{1... | collective-permute-start | bytes 294920 | tf_op jit(solution)/shard_map/ppermute | solution.py:408
  8.1 2.8 %collective-permute-start.2 = (bf16[24,16,128]{2,1,0:T(8,128)(2,1)S(1)}, bf16[24,16,128]{2,1,0:T(8,128)(2,1)S(1)}, u32[]{:S(2)}, u32[]{:S(2)}) collective-permute-start(bf16[24,16,128]{2,1,0:T(8,128)(2,1)S(1)} %get-tuple-element.13), channel_id=1, source_target_pairs={{0,12},{4,0},{8,4},{12,8},{1,13},{5,1},{9,5},{13,9},{2,14},{6,2},{... | collective-permute-start | bytes 294920 | tf_op jit(solution)/shard_map/ppermute | solution.py:408
  10.9 1.8 %collective-permute-start.4 = (bf16[24,16,128]{2,1,0:T(8,128)(2,1)S(1)}, bf16[24,16,128]{2,1,0:T(8,128)(2,1)S(1)}, u32[]{:S(2)}, u32[]{:S(2)}) collective-permute-start(bf16[24,16,128]{2,1,0:T(8,128)(2,1)S(1)} %get-tuple-element.15), channel_id=1, source_target_pairs={{0,3},{1,0},{2,1},{3,2},{4,7},{5,4},{6,5},{7,6},{8,11},{9,8},{10,9... | collective-permute-start | bytes 294920 | tf_op jit(solution)/shard_map/ppermute | solution.py:408
  14.8 1.9 %collective-permute-done.3.zm_ref = bf16[24,16,128]{2,1,0:T(8,128)(2,1)S(1)} collective-permute-done((bf16[24,16,128]{2,1,0:T(8,128)(2,1)S(1)}, bf16[24,16,128]{2,1,0:T(8,128)(2,1)S(1)}, u32[]{:S(2)}, u32[]{:S(2)}) %collective-permute-start.3) | collective-permute-done | bytes 98336 | tf_op jit(solution)/shard_map/ppermute | solution.py:408
  16.7 1.5 %collective-permute-done.5.xm_ref = bf16[24,16,128]{2,1,0:T(8,128)(2,1)S(1)} collective-permute-done((bf16[24,16,128]{2,1,0:T(8,128)(2,1)S(1)}, bf16[24,16,128]{2,1,0:T(8,128)(2,1)S(1)}, u32[]{:S(2)}, u32[]{:S(2)}) %collective-permute-start.5) | collective-permute-done | bytes 98336 | tf_op jit(solution)/shard_map/ppermute | solution.py:408
  23.9 14.3 %shard_map.83.e_ref.r_ref = f32[2,8,128]{2,1,0:T(8,128)S(1)} custom-call(s32[4]{0:T(128)S(1)} %copy-done.6, s32[4]{0:T(128)S(1)} %copy-done.7, s32[1]{0:T(128)} %bitcast.offset_ref, f32[24]{0:T(128)S(1)} %reshape.25.wall_ref, bf16[2,4,12,16,128]{4,3,2,1,0:T(8,128)(2,1)S(1)} %bitcast.12, bf16[24,16,128]{2,1,0:T(8,128)(2,1)S(1)} %collective-permute-done.tp_ref, ...), custom_call_target="tpu_custom_call" | custom-call | tf_op jit(solution)/shard_map/pallas_call | solution.py:262
  38.2 3.3 %collective-permute-start.10 = (f32[2,8,128]{2,1,0:T(8,128)S(1)}, f32[2,8,128]{2,1,0:T(8,128)S(1)}, u32[]{:S(2)}, u32[]{:S(2)}) collective-permute-start(f32[2,8,128]{2,1,0:T(8,128)S(1)} %shard_map.83.e_ref.r_ref), channel_id=1, source_target_pairs={{0,3},{1,0},{2,1},{3,2},{4,7},{5,4},{6,5},{7,6},{8,11},{9,8},{10,9... | collective-permute-start | bytes 24584 | tf_op jit(solution)/shard_map/ppermute | solution.py:408
  42.0 2.8 %collective-permute-start.8 = (f32[2,8,128]{2,1,0:T(8,128)S(1)}, f32[2,8,128]{2,1,0:T(8,128)S(1)}, u32[]{:S(2)}, u32[]{:S(2)}) collective-permute-start(f32[2,8,128]{2,1,0:T(8,128)S(1)} %shard_map.83.e_ref.r_ref), channel_id=1, source_target_pairs={{0,12},{4,0},{8,4},{12,8},{1,13},{5,1},{9,5},{13,9},{2,14},{6,2},{... | collective-permute-start | bytes 24584 | tf_op jit(solution)/shard_map/ppermute | solution.py:408
  44.7 4.1 %collective-permute-start.6 = (f32[2,8,128]{2,1,0:T(8,128)S(1)}, f32[2,8,128]{2,1,0:T(8,128)S(1)}, u32[]{:S(2)}, u32[]{:S(2)}) collective-permute-start(f32[2,8,128]{2,1,0:T(8,128)S(1)} %shard_map.83.e_ref.r_ref), channel_id=1, source_target_pairs={{0,112},{16,0},{32,16},{48,32},{64,48},{80,64},{96,80},{112,96},{1... | collective-permute-start | bytes 24584 | tf_op jit(solution)/shard_map/ppermute | solution.py:408
  48.9 31.3 %shard_map.84.operator_ref = f32[432,8,128]{2,1,0:T(8,128)S(1)} custom-call(f32[432,8,24]{2,1,0:T(8,128)S(1)} %bitcast.14), custom_call_target="tpu_custom_call" | custom-call | tf_op jit(solution)/shard_map/pallas_call | solution.py:290
  81.0 3.2 %collective-permute-start.16 = (f32[2,8,128]{2,1,0:T(8,128)S(1)}, f32[2,8,128]{2,1,0:T(8,128)S(1)}, u32[]{:S(2)}, u32[]{:S(2)}) collective-permute-start(f32[2,8,128]{2,1,0:T(8,128)S(1)} %shard_map.85.e_ref), channel_id=1, source_target_pairs={{0,3},{1,0},{2,1},{3,2},{4,7},{5,4},{6,5},{7,6},{8,11},{9,8},{10,9... | collective-permute-start | bytes 24584 | tf_op jit(solution)/shard_map/ppermute | solution.py:408
  84.2 3.2 %collective-permute-start.14 = (f32[2,8,128]{2,1,0:T(8,128)S(1)}, f32[2,8,128]{2,1,0:T(8,128)S(1)}, u32[]{:S(2)}, u32[]{:S(2)}) collective-permute-start(f32[2,8,128]{2,1,0:T(8,128)S(1)} %shard_map.85.e_ref), channel_id=1, source_target_pairs={{0,12},{4,0},{8,4},{12,8},{1,13},{5,1},{9,5},{13,9},{2,14},{6,2},{... | collective-permute-start | bytes 24584 | tf_op jit(solution)/shard_map/ppermute | solution.py:408
  87.5 4.1 %collective-permute-start.12 = (f32[2,8,128]{2,1,0:T(8,128)S(1)}, f32[2,8,128]{2,1,0:T(8,128)S(1)}, u32[]{:S(2)}, u32[]{:S(2)}) collective-permute-start(f32[2,8,128]{2,1,0:T(8,128)S(1)} %shard_map.85.e_ref), channel_id=1, source_target_pairs={{0,112},{16,0},{32,16},{48,32},{64,48},{80,64},{96,80},{112,96},{1... | collective-permute-start | bytes 24584 | tf_op jit(solution)/shard_map/ppermute | solution.py:408
  91.6 1.6 %collective-permute-done.13.tm = f32[2,8,128]{2,1,0:T(8,128)S(1)} collective-permute-done((f32[2,8,128]{2,1,0:T(8,128)S(1)}, f32[2,8,128]{2,1,0:T(8,128)S(1)}, u32[]{:S(2)}, u32[]{:S(2)}) %collective-permute-start.13) | collective-permute-done | bytes 8224 | tf_op jit(solution)/shard_map/ppermute | solution.py:408
  93.9 3.2 %collective-permute-start.22 = (f32[2,8,128]{2,1,0:T(8,128)S(1)}, f32[2,8,128]{2,1,0:T(8,128)S(1)}, u32[]{:S(2)}, u32[]{:S(2)}) collective-permute-start(f32[2,8,128]{2,1,0:T(8,128)S(1)} %shard_map.86.e_ref), channel_id=1, source_target_pairs={{0,3},{1,0},{2,1},{3,2},{4,7},{5,4},{6,5},{7,6},{8,11},{9,8},{10,9... | collective-permute-start | bytes 24584 | tf_op jit(solution)/shard_map/ppermute | solution.py:408
  97.2 3.2 %collective-permute-start.20 = (f32[2,8,128]{2,1,0:T(8,128)S(1)}, f32[2,8,128]{2,1,0:T(8,128)S(1)}, u32[]{:S(2)}, u32[]{:S(2)}) collective-permute-start(f32[2,8,128]{2,1,0:T(8,128)S(1)} %shard_map.86.e_ref), channel_id=1, source_target_pairs={{0,12},{4,0},{8,4},{12,8},{1,13},{5,1},{9,5},{13,9},{2,14},{6,2},{... | collective-permute-start | bytes 24584 | tf_op jit(solution)/shard_map/ppermute | solution.py:408
  100.4 4.1 %collective-permute-start.18 = (f32[2,8,128]{2,1,0:T(8,128)S(1)}, f32[2,8,128]{2,1,0:T(8,128)S(1)}, u32[]{:S(2)}, u32[]{:S(2)}) collective-permute-start(f32[2,8,128]{2,1,0:T(8,128)S(1)} %shard_map.86.e_ref), channel_id=1, source_target_pairs={{0,112},{16,0},{32,16},{48,32},{64,48},{80,64},{96,80},{112,96},{1... | collective-permute-start | bytes 24584 | tf_op jit(solution)/shard_map/ppermute | solution.py:408
  104.6 1.6 %collective-permute-done.19.tm = f32[2,8,128]{2,1,0:T(8,128)S(1)} collective-permute-done((f32[2,8,128]{2,1,0:T(8,128)S(1)}, f32[2,8,128]{2,1,0:T(8,128)S(1)}, u32[]{:S(2)}, u32[]{:S(2)}) %collective-permute-start.19) | collective-permute-done | bytes 8224 | tf_op jit(solution)/shard_map/ppermute | solution.py:408
  107.1 3.2 %collective-permute-start.28 = (f32[2,8,128]{2,1,0:T(8,128)S(1)}, f32[2,8,128]{2,1,0:T(8,128)S(1)}, u32[]{:S(2)}, u32[]{:S(2)}) collective-permute-start(f32[2,8,128]{2,1,0:T(8,128)S(1)} %shard_map.87.e_ref), channel_id=1, source_target_pairs={{0,3},{1,0},{2,1},{3,2},{4,7},{5,4},{6,5},{7,6},{8,11},{9,8},{10,9... | collective-permute-start | bytes 24584 | tf_op jit(solution)/shard_map/ppermute | solution.py:408
  110.3 3.2 %collective-permute-start.26 = (f32[2,8,128]{2,1,0:T(8,128)S(1)}, f32[2,8,128]{2,1,0:T(8,128)S(1)}, u32[]{:S(2)}, u32[]{:S(2)}) collective-permute-start(f32[2,8,128]{2,1,0:T(8,128)S(1)} %shard_map.87.e_ref), channel_id=1, source_target_pairs={{0,12},{4,0},{8,4},{12,8},{1,13},{5,1},{9,5},{13,9},{2,14},{6,2},{... | collective-permute-start | bytes 24584 | tf_op jit(solution)/shard_map/ppermute | solution.py:408
  114.0 3.7 %collective-permute-start.24 = (f32[2,8,128]{2,1,0:T(8,128)S(1)}, f32[2,8,128]{2,1,0:T(8,128)S(1)}, u32[]{:S(2)}, u32[]{:S(2)}) collective-permute-start(f32[2,8,128]{2,1,0:T(8,128)S(1)} %shard_map.87.e_ref), channel_id=1, source_target_pairs={{0,112},{16,0},{32,16},{48,32},{64,48},{80,64},{96,80},{112,96},{1... | collective-permute-start | bytes 24584 | tf_op jit(solution)/shard_map/ppermute | solution.py:408
  117.7 1.6 %collective-permute-done.25.tm = f32[2,8,128]{2,1,0:T(8,128)S(1)} collective-permute-done((f32[2,8,128]{2,1,0:T(8,128)S(1)}, f32[2,8,128]{2,1,0:T(8,128)S(1)}, u32[]{:S(2)}, u32[]{:S(2)}) %collective-permute-start.25) | collective-permute-done | bytes 8224 | tf_op jit(solution)/shard_map/ppermute | solution.py:408
  119.3 3.5 %shard_map.88 = f32[2,4,12,16,128]{4,3,2,1,0:T(8,128)} custom-call(f32[2,8,128]{2,1,0:T(8,128)S(1)} %shard_map.87.e_ref, f32[2,8,128]{2,1,0:T(8,128)S(1)} %collective-permute-done.24.tp, f32[2,8,128]{2,1,0:T(8,128)S(1)} %collective-permute-done.25.tm, f32[2,8,128]{2,1,0:T(8,128)S(1)} %collective-permute-done.26.zp, ...), custom_call_target="tpu_custom_call" | custom-call | tf_op jit(solution)/shard_map/pallas_call | solution.py:396
  (61 shorter events, 12.1 us)
Async XLA Ops:
  2.9 9.7 %collective-permute-start = (bf16[24,16,128]{2,1,0:T(8,128)(2,1)S(1)}, bf16[24,16,128]{2,1,0:T(8,128)(2,1)S(1)}, u32[]{:S(2)}, u32[]{:S(2)}) collective-permute-start(bf16[24,16,128]{2,1,0:T(8,128)(2,1)S(1)} %get-tuple-element.11), channel_id=1, source_target_pairs={{0,112},{16,0},{32,16},{48,32},{64,48},{80,64},{96,80},{112,96},{1... | collective-permute-start | bytes 294920 | tf_op jit(solution)/shard_map/ppermute | solution.py:408
  8.1 6.7 %collective-permute-start.1 = (bf16[24,16,128]{2,1,0:T(8,128)(2,1)S(1)}, bf16[24,16,128]{2,1,0:T(8,128)(2,1)S(1)}, u32[]{:S(2)}, u32[]{:S(2)}) collective-permute-start(bf16[24,16,128]{2,1,0:T(8,128)(2,1)S(1)} %get-tuple-element.12), channel_id=1, source_target_pairs={{0,16},{16,32},{32,48},{48,64},{64,80},{80,96},{96,112},{112,0},{1... | collective-permute-start | bytes 294920 | tf_op jit(solution)/shard_map/ppermute | solution.py:408
  8.1 6.7 %collective-permute-start.2 = (bf16[24,16,128]{2,1,0:T(8,128)(2,1)S(1)}, bf16[24,16,128]{2,1,0:T(8,128)(2,1)S(1)}, u32[]{:S(2)}, u32[]{:S(2)}) collective-permute-start(bf16[24,16,128]{2,1,0:T(8,128)(2,1)S(1)} %get-tuple-element.13), channel_id=1, source_target_pairs={{0,12},{4,0},{8,4},{12,8},{1,13},{5,1},{9,5},{13,9},{2,14},{6,2},{... | collective-permute-start | bytes 294920 | tf_op jit(solution)/shard_map/ppermute | solution.py:408
  10.9 5.8 %collective-permute-start.3 = (bf16[24,16,128]{2,1,0:T(8,128)(2,1)S(1)}, bf16[24,16,128]{2,1,0:T(8,128)(2,1)S(1)}, u32[]{:S(2)}, u32[]{:S(2)}) collective-permute-start(bf16[24,16,128]{2,1,0:T(8,128)(2,1)S(1)} %get-tuple-element.14), channel_id=1, source_target_pairs={{0,4},{4,8},{8,12},{12,0},{1,5},{5,9},{9,13},{13,1},{2,6},{6,10},{... | collective-permute-start | bytes 294920 | tf_op jit(solution)/shard_map/ppermute | solution.py:408
  10.9 5.8 %collective-permute-start.4 = (bf16[24,16,128]{2,1,0:T(8,128)(2,1)S(1)}, bf16[24,16,128]{2,1,0:T(8,128)(2,1)S(1)}, u32[]{:S(2)}, u32[]{:S(2)}) collective-permute-start(bf16[24,16,128]{2,1,0:T(8,128)(2,1)S(1)} %get-tuple-element.15), channel_id=1, source_target_pairs={{0,3},{1,0},{2,1},{3,2},{4,7},{5,4},{6,5},{7,6},{8,11},{9,8},{10,9... | collective-permute-start | bytes 294920 | tf_op jit(solution)/shard_map/ppermute | solution.py:408
  38.2 6.5 %collective-permute-start.11 = (f32[2,8,128]{2,1,0:T(8,128)S(1)}, f32[2,8,128]{2,1,0:T(8,128)S(1)}, u32[]{:S(2)}, u32[]{:S(2)}) collective-permute-start(f32[2,8,128]{2,1,0:T(8,128)S(1)} %shard_map.83.e_ref.r_ref), channel_id=1, source_target_pairs={{0,1},{1,2},{2,3},{3,0},{4,5},{5,6},{6,7},{7,4},{8,9},{9,10},{10,1... | collective-permute-start | bytes 24584 | tf_op jit(solution)/shard_map/ppermute | solution.py:408
  38.2 42.0 %collective-permute-start.10 = (f32[2,8,128]{2,1,0:T(8,128)S(1)}, f32[2,8,128]{2,1,0:T(8,128)S(1)}, u32[]{:S(2)}, u32[]{:S(2)}) collective-permute-start(f32[2,8,128]{2,1,0:T(8,128)S(1)} %shard_map.83.e_ref.r_ref), channel_id=1, source_target_pairs={{0,3},{1,0},{2,1},{3,2},{4,7},{5,4},{6,5},{7,6},{8,11},{9,8},{10,9... | collective-permute-start | bytes 24584 | tf_op jit(solution)/shard_map/ppermute | solution.py:408
  41.5 38.7 %collective-permute-start.9 = (f32[2,8,128]{2,1,0:T(8,128)S(1)}, f32[2,8,128]{2,1,0:T(8,128)S(1)}, u32[]{:S(2)}, u32[]{:S(2)}) collective-permute-start(f32[2,8,128]{2,1,0:T(8,128)S(1)} %shard_map.83.e_ref.r_ref), channel_id=1, source_target_pairs={{0,4},{4,8},{8,12},{12,0},{1,5},{5,9},{9,13},{13,1},{2,6},{6,10},{... | collective-permute-start | bytes 24584 | tf_op jit(solution)/shard_map/ppermute | solution.py:408
  42.0 38.3 %collective-permute-start.8 = (f32[2,8,128]{2,1,0:T(8,128)S(1)}, f32[2,8,128]{2,1,0:T(8,128)S(1)}, u32[]{:S(2)}, u32[]{:S(2)}) collective-permute-start(f32[2,8,128]{2,1,0:T(8,128)S(1)} %shard_map.83.e_ref.r_ref), channel_id=1, source_target_pairs={{0,12},{4,0},{8,4},{12,8},{1,13},{5,1},{9,5},{13,9},{2,14},{6,2},{... | collective-permute-start | bytes 24584 | tf_op jit(solution)/shard_map/ppermute | solution.py:408
  44.7 35.5 %collective-permute-start.7 = (f32[2,8,128]{2,1,0:T(8,128)S(1)}, f32[2,8,128]{2,1,0:T(8,128)S(1)}, u32[]{:S(2)}, u32[]{:S(2)}) collective-permute-start(f32[2,8,128]{2,1,0:T(8,128)S(1)} %shard_map.83.e_ref.r_ref), channel_id=1, source_target_pairs={{0,16},{16,32},{32,48},{48,64},{64,80},{80,96},{96,112},{112,0},{1... | collective-permute-start | bytes 24584 | tf_op jit(solution)/shard_map/ppermute | solution.py:408
  44.7 35.5 %collective-permute-start.6 = (f32[2,8,128]{2,1,0:T(8,128)S(1)}, f32[2,8,128]{2,1,0:T(8,128)S(1)}, u32[]{:S(2)}, u32[]{:S(2)}) collective-permute-start(f32[2,8,128]{2,1,0:T(8,128)S(1)} %shard_map.83.e_ref.r_ref), channel_id=1, source_target_pairs={{0,112},{16,0},{32,16},{48,32},{64,48},{80,64},{96,80},{112,96},{1... | collective-permute-start | bytes 24584 | tf_op jit(solution)/shard_map/ppermute | solution.py:408
  81.0 6.5 %collective-permute-start.17 = (f32[2,8,128]{2,1,0:T(8,128)S(1)}, f32[2,8,128]{2,1,0:T(8,128)S(1)}, u32[]{:S(2)}, u32[]{:S(2)}) collective-permute-start(f32[2,8,128]{2,1,0:T(8,128)S(1)} %shard_map.85.e_ref), channel_id=1, source_target_pairs={{0,1},{1,2},{2,3},{3,0},{4,5},{5,6},{6,7},{7,4},{8,9},{9,10},{10,1... | collective-permute-start | bytes 24584 | tf_op jit(solution)/shard_map/ppermute | solution.py:408
  81.0 10.6 %collective-permute-start.16 = (f32[2,8,128]{2,1,0:T(8,128)S(1)}, f32[2,8,128]{2,1,0:T(8,128)S(1)}, u32[]{:S(2)}, u32[]{:S(2)}) collective-permute-start(f32[2,8,128]{2,1,0:T(8,128)S(1)} %shard_map.85.e_ref), channel_id=1, source_target_pairs={{0,3},{1,0},{2,1},{3,2},{4,7},{5,4},{6,5},{7,6},{8,11},{9,8},{10,9... | collective-permute-start | bytes 24584 | tf_op jit(solution)/shard_map/ppermute | solution.py:408
  84.2 7.4 %collective-permute-start.15 = (f32[2,8,128]{2,1,0:T(8,128)S(1)}, f32[2,8,128]{2,1,0:T(8,128)S(1)}, u32[]{:S(2)}, u32[]{:S(2)}) collective-permute-start(f32[2,8,128]{2,1,0:T(8,128)S(1)} %shard_map.85.e_ref), channel_id=1, source_target_pairs={{0,4},{4,8},{8,12},{12,0},{1,5},{5,9},{9,13},{13,1},{2,6},{6,10},{... | collective-permute-start | bytes 24584 | tf_op jit(solution)/shard_map/ppermute | solution.py:408
  84.2 7.4 %collective-permute-start.14 = (f32[2,8,128]{2,1,0:T(8,128)S(1)}, f32[2,8,128]{2,1,0:T(8,128)S(1)}, u32[]{:S(2)}, u32[]{:S(2)}) collective-permute-start(f32[2,8,128]{2,1,0:T(8,128)S(1)} %shard_map.85.e_ref), channel_id=1, source_target_pairs={{0,12},{4,0},{8,4},{12,8},{1,13},{5,1},{9,5},{13,9},{2,14},{6,2},{... | collective-permute-start | bytes 24584 | tf_op jit(solution)/shard_map/ppermute | solution.py:408
  93.9 6.5 %collective-permute-start.23 = (f32[2,8,128]{2,1,0:T(8,128)S(1)}, f32[2,8,128]{2,1,0:T(8,128)S(1)}, u32[]{:S(2)}, u32[]{:S(2)}) collective-permute-start(f32[2,8,128]{2,1,0:T(8,128)S(1)} %shard_map.86.e_ref), channel_id=1, source_target_pairs={{0,1},{1,2},{2,3},{3,0},{4,5},{5,6},{6,7},{7,4},{8,9},{9,10},{10,1... | collective-permute-start | bytes 24584 | tf_op jit(solution)/shard_map/ppermute | solution.py:408
  93.9 10.6 %collective-permute-start.22 = (f32[2,8,128]{2,1,0:T(8,128)S(1)}, f32[2,8,128]{2,1,0:T(8,128)S(1)}, u32[]{:S(2)}, u32[]{:S(2)}) collective-permute-start(f32[2,8,128]{2,1,0:T(8,128)S(1)} %shard_map.86.e_ref), channel_id=1, source_target_pairs={{0,3},{1,0},{2,1},{3,2},{4,7},{5,4},{6,5},{7,6},{8,11},{9,8},{10,9... | collective-permute-start | bytes 24584 | tf_op jit(solution)/shard_map/ppermute | solution.py:408
  97.2 7.4 %collective-permute-start.21 = (f32[2,8,128]{2,1,0:T(8,128)S(1)}, f32[2,8,128]{2,1,0:T(8,128)S(1)}, u32[]{:S(2)}, u32[]{:S(2)}) collective-permute-start(f32[2,8,128]{2,1,0:T(8,128)S(1)} %shard_map.86.e_ref), channel_id=1, source_target_pairs={{0,4},{4,8},{8,12},{12,0},{1,5},{5,9},{9,13},{13,1},{2,6},{6,10},{... | collective-permute-start | bytes 24584 | tf_op jit(solution)/shard_map/ppermute | solution.py:408
  97.2 7.4 %collective-permute-start.20 = (f32[2,8,128]{2,1,0:T(8,128)S(1)}, f32[2,8,128]{2,1,0:T(8,128)S(1)}, u32[]{:S(2)}, u32[]{:S(2)}) collective-permute-start(f32[2,8,128]{2,1,0:T(8,128)S(1)} %shard_map.86.e_ref), channel_id=1, source_target_pairs={{0,12},{4,0},{8,4},{12,8},{1,13},{5,1},{9,5},{13,9},{2,14},{6,2},{... | collective-permute-start | bytes 24584 | tf_op jit(solution)/shard_map/ppermute | solution.py:408
  106.9 7.1 %collective-permute-start.29 = (f32[2,8,128]{2,1,0:T(8,128)S(1)}, f32[2,8,128]{2,1,0:T(8,128)S(1)}, u32[]{:S(2)}, u32[]{:S(2)}) collective-permute-start(f32[2,8,128]{2,1,0:T(8,128)S(1)} %shard_map.87.e_ref), channel_id=1, source_target_pairs={{0,1},{1,2},{2,3},{3,0},{4,5},{5,6},{6,7},{7,4},{8,9},{9,10},{10,1... | collective-permute-start | bytes 24584 | tf_op jit(solution)/shard_map/ppermute | solution.py:408
  107.1 10.6 %collective-permute-start.28 = (f32[2,8,128]{2,1,0:T(8,128)S(1)}, f32[2,8,128]{2,1,0:T(8,128)S(1)}, u32[]{:S(2)}, u32[]{:S(2)}) collective-permute-start(f32[2,8,128]{2,1,0:T(8,128)S(1)} %shard_map.87.e_ref), channel_id=1, source_target_pairs={{0,3},{1,0},{2,1},{3,2},{4,7},{5,4},{6,5},{7,6},{8,11},{9,8},{10,9... | collective-permute-start | bytes 24584 | tf_op jit(solution)/shard_map/ppermute | solution.py:408
  110.3 7.4 %collective-permute-start.27 = (f32[2,8,128]{2,1,0:T(8,128)S(1)}, f32[2,8,128]{2,1,0:T(8,128)S(1)}, u32[]{:S(2)}, u32[]{:S(2)}) collective-permute-start(f32[2,8,128]{2,1,0:T(8,128)S(1)} %shard_map.87.e_ref), channel_id=1, source_target_pairs={{0,4},{4,8},{8,12},{12,0},{1,5},{5,9},{9,13},{13,1},{2,6},{6,10},{... | collective-permute-start | bytes 24584 | tf_op jit(solution)/shard_map/ppermute | solution.py:408
  110.3 7.4 %collective-permute-start.26 = (f32[2,8,128]{2,1,0:T(8,128)S(1)}, f32[2,8,128]{2,1,0:T(8,128)S(1)}, u32[]{:S(2)}, u32[]{:S(2)}) collective-permute-start(f32[2,8,128]{2,1,0:T(8,128)S(1)} %shard_map.87.e_ref), channel_id=1, source_target_pairs={{0,12},{4,0},{8,4},{12,8},{1,13},{5,1},{9,5},{13,9},{2,14},{6,2},{... | collective-permute-start | bytes 24584 | tf_op jit(solution)/shard_map/ppermute | solution.py:408
  113.6 5.8 %collective-permute-start.25 = (f32[2,8,128]{2,1,0:T(8,128)S(1)}, f32[2,8,128]{2,1,0:T(8,128)S(1)}, u32[]{:S(2)}, u32[]{:S(2)}) collective-permute-start(f32[2,8,128]{2,1,0:T(8,128)S(1)} %shard_map.87.e_ref), channel_id=1, source_target_pairs={{0,16},{16,32},{32,48},{48,64},{64,80},{80,96},{96,112},{112,0},{1... | collective-permute-start | bytes 24584 | tf_op jit(solution)/shard_map/ppermute | solution.py:408
  (14 other events, 65.6 us)

commit v2 on v1

v2 whole, which is shorter than its diff:
```python
import jax
import jax.numpy as jnp
from jax import lax
from jax.experimental import pallas as pl
from jax.experimental.pallas import tpu as pltpu
from jax.sharding import PartitionSpec as P

BLOCK = 4
ITERS = 4
NY = 32
ROWS = 16
LANES = 128
HALF = 8
MASS = 4.1
F32 = jnp.float32
BF16 = jnp.bfloat16

gammas = [
    [[0j, 0j, 1 + 0j, 0j], [0j, 0j, 0j, 1 + 0j], [1 + 0j, 0j, 0j, 0j], [0j, 1 + 0j, 0j, 0j]],
    [[0j, 0j, 1j, 0j], [0j, 0j, 0j, -1j], [-1j, 0j, 0j, 0j], [0j, 1j, 0j, 0j]],
    [[0j, 0j, 0j, 1j], [0j, 0j, 1j, 0j], [0j, -1j, 0j, 0j], [-1j, 0j, 0j, 0j]],
    [[0j, 0j, 0j, -1 + 0j], [0j, 0j, 1 + 0j, 0j], [0j, 1 + 0j, 0j, 0j], [-1 + 0j, 0j, 0j, 0j]],
]


def vmem_params(mib):
    return pltpu.CompilerParams(vmem_limit_bytes=mib * 1024 * 1024)


def lane_index(rows):
    return lax.broadcasted_iota(jnp.int32, (rows, LANES), 1)


def row_index(rows):
    return lax.broadcasted_iota(jnp.int32, (rows, LANES), 0)


def turn_lanes(value, shift):
    return pltpu.roll(value, shift % LANES, 1)


def swap(value, axis, matching):
    count = lax.axis_size(axis)
    if matching == 0:
        pairs = [(i, i ^ 1) for i in range(count)]
    else:
        pairs = [(i, (i + 1 if i % 2 else i - 1) % count) for i in range(count)]
    return lax.ppermute(value, axis, pairs)


def is_even(axis):
    return lax.rem(lax.axis_index(axis), 2) == 0


def pack_kernel(psi_ref, ta_ref, tb_ref, za_ref, zb_ref, xa_ref, xb_ref, wide_ref):
    lanes = lane_index(ROWS)
    even = [is_even(axis) for axis in ("ta", "gz", "xy")]

    def store(component, which, first, last):
        toward_a, toward_b = ((ta_ref, tb_ref), (za_ref, zb_ref), (xa_ref, xb_ref))[which]
        toward_a[component] = jnp.where(even[which], last, first).astype(BF16)
        toward_b[component] = jnp.where(even[which], first, last).astype(BF16)

    def body(component, carry):
        part = component // 12
        c = component % 12
        fields = [psi_ref[part, r, c].astype(F32) for r in range(4)]
        for r in range(4):
            wide_ref[part, r, c] = fields[r]
        store(
            component, 0,
            jnp.concatenate([wide_ref[part, r, c, 0:4, :] for r in range(4)], axis=0),
            jnp.concatenate([wide_ref[part, r, c, 12:16, :] for r in range(4)], axis=0),
        )
        store(
            component, 1,
            jnp.concatenate([wide_ref[part, r, c, pl.ds(0, 4, stride=4), :] for r in range(4)], axis=0),
            jnp.concatenate([wide_ref[part, r, c, pl.ds(3, 4, stride=4), :] for r in range(4)], axis=0),
        )
        low = fields[0]
        high = turn_lanes(fields[0], 32)
        for r in range(1, 4):
            mask = lanes >= 32 * r
            low = jnp.where(mask, turn_lanes(fields[r], 32 * r), low)
            high = jnp.where(mask, turn_lanes(fields[r], 32 * r + 32), high)
        store(component, 2, low, high)
        return carry

    lax.fori_loop(0, 24, body, 0, unroll=4)


def pack(psi):
    slab = jax.ShapeDtypeStruct((24, ROWS, LANES), BF16)
    wide = jax.ShapeDtypeStruct((2, 4, 12, ROWS, LANES), F32)
    vm = pl.BlockSpec(memory_space=pltpu.VMEM)
    return pl.pallas_call(
        pack_kernel,
        out_shape=(slab,) * 6 + (wide,),
        in_specs=[vm],
        out_specs=(vm,) * 7,
        compiler_params=vmem_params(16),
    )(psi)


def times(entry, re, im):
    if entry.real != 0:
        return (entry.real, re), (entry.real, im)
    return (-entry.imag, im), (entry.imag, re)


def add_signed(total, term):
    sign, value = term
    if total is None:
        return value if sign > 0 else -value
    return total + value if sign > 0 else total - value


def projected(direction, sign, load):
    rows = []
    for s in range(2):
        partner = 2 if gammas[direction][s][2] != 0 else 3
        entry = gammas[direction][s][partner] * sign
        row = []
        for colour in range(3):
            a, b = times(entry, load(0, 3 * partner + colour), load(1, 3 * partner + colour))
            row.append((
                add_signed(load(0, 3 * s + colour), a),
                add_signed(load(1, 3 * s + colour), b),
            ))
        rows.append(row)
    return rows


def mapped(function, *tables):
    return [
        [
            tuple(function(*[table[s][colour][part] for table in tables]) for part in range(2))
            for colour in range(3)
        ]
        for s in range(2)
    ]


def hop(direction, sign, half_field, link, total):
    for out in range(3):
        row = [link(0, out, inn) for inn in range(3)], [link(1, out, inn) for inn in range(3)]
        moved = []
        for s in range(2):
            re = None
            im = None
            for inn in range(3):
                ure, uim = row[0][inn], row[1][inn]
                hre, him = half_field[s][inn]
                tre = ure * hre - uim * him
                tim = ure * him + uim * hre
                re = tre if re is None else re + tre
                im = tim if im is None else im + tim
            moved.append((re, im))
        for s in range(2):
            for part in range(2):
                total[s][out][part] = add_signed(total[s][out][part], (1.0, moved[s][part]))
        for s in range(2, 4):
            source = 0 if gammas[direction][s][0] != 0 else 1
            entry = gammas[direction][s][source] * sign
            terms = times(entry, *moved[source])
            for part in range(2):
                total[s][out][part] = add_signed(total[s][out][part], terms[part])


def link_loader(links_ref, number, low):
    def link(part, out, inn):
        return links_ref[number, part, out, inn].astype(F32)[low : low + HALF]
    return link


def centre_kernel(
    wide_ref, when_hbm, spin_hbm, wall_hbm, links_hbm, clover_hbm, stencil_hbm, out_ref, operator_ref,
    when_ref, spin_ref, wall_ref, links_ref, clover_ref, stencil_ref, sems,
):
    copies = [
        pltpu.make_async_copy(source, target, sems.at[i])
        for i, (source, target) in enumerate((
            (when_hbm, when_ref), (spin_hbm, spin_ref), (wall_hbm, wall_ref),
            (links_hbm.at[pl.ds(6, 2)], links_ref), (clover_hbm, clover_ref), (stencil_hbm, stencil_ref),
        ))
    ]
    for copy in copies:
        copy.start()
    for copy in copies[:5]:
        copy.wait()
    lanes = lane_index(HALF)
    y = lanes % NY
    first_time = lax.axis_index("ta") * BLOCK

    def rhs(r, carry):
        when = when_ref[r]
        spin = spin_ref[r]
        for half in range(2):
            low = HALF * half

            def load(part, component):
                return wide_ref[part, r, component, low : low + HALF, :]

            total = [[[None, None] for _ in range(3)] for _ in range(4)]
            ahead = mapped(
                lambda p: jnp.where(y < NY - 1, turn_lanes(p, -1), turn_lanes(p, NY - 1)),
                projected(3, -1.0, load),
            )
            hop(3, -1.0, ahead, link_loader(links_ref, 0, low), total)
            behind = mapped(
                lambda p: jnp.where(y > 0, turn_lanes(p, 1), turn_lanes(p, 1 - NY)),
                projected(3, 1.0, load),
            )
            hop(3, 1.0, behind, link_loader(links_ref, 1, low), total)
            at_wall = first_time + 2 * half + row_index(HALF) // BLOCK == when
            for chirality in range(2):
                values = [(load(0, 6 * chirality + i), load(1, 6 * chirality + i)) for i in range(6)]
                for i in range(6):
                    re = MASS * values[i][0]
                    im = MASS * values[i][1]
                    for j in range(6):
                        cre = clover_ref[chirality, 0, i, j].astype(F32)[low : low + HALF]
                        cim = clover_ref[chirality, 1, i, j].astype(F32)[low : low + HALF]
                        re = re + (cre * values[j][0] - cim * values[j][1])
                        im = im + (cre * values[j][1] + cim * values[j][0])
                    s = 2 * chirality + i // 3
                    colour = i % 3
                    here = spin == s
                    sre = jnp.where(here, wall_ref[colour, 0, r], 0.0)
                    sim = jnp.where(here, wall_ref[colour, 1, r], 0.0)
                    re = jnp.where(at_wall, sre, 0.0) + (0.5 * total[s][colour][0] - re)
                    im = jnp.where(at_wall, sim, 0.0) + (0.5 * total[s][colour][1] - im)
                    out_ref[r, 6 * chirality + i, low : low + HALF, :] = re
                    out_ref[r, 12 + 6 * chirality + i, low : low + HALF, :] = im
        return carry

    lax.fori_loop(0, 4, rhs, 0)
    copies[5].wait()

    def spread(index, carry):
        start = pl.multiple_of(24 * index, 24)
        block = stencil_ref[pl.ds(start, 24)].reshape((24 * HALF, 24))
        block = jnp.concatenate([block, jnp.zeros((24 * HALF, LANES - 24), F32)], axis=1)
        block = block + turn_lanes(block, 32)
        block = block + turn_lanes(block, 64)
        operator_ref[pl.ds(start, 24)] = block.reshape((24, HALF, LANES))
        return carry

    lax.fori_loop(0, 18, spread, 0)


def centre(wide, wall_time, spin_index, wall, links, clover, stencil):
    vm = pl.BlockSpec(memory_space=pltpu.VMEM)
    hbm = pl.BlockSpec(memory_space=pltpu.HBM)
    return pl.pallas_call(
        centre_kernel,
        out_shape=(
            jax.ShapeDtypeStruct((4, 24, ROWS, LANES), F32),
            jax.ShapeDtypeStruct((9 * 2 * 24, HALF, LANES), F32),
        ),
        in_specs=[vm] + [hbm] * 6,
        out_specs=(vm, vm),
        scratch_shapes=[
            pltpu.SMEM((4,), jnp.int32),
            pltpu.SMEM((4,), jnp.int32),
            pltpu.SMEM((3, 2, 4), F32),
            pltpu.VMEM((2, 2, 3, 3, ROWS, LANES), BF16),
            pltpu.VMEM((2, 2, 6, 6, ROWS, LANES), BF16),
            pltpu.VMEM((9 * 2 * 24, HALF, 24), F32),
            pltpu.SemaphoreType.DMA((6,)),
        ],
        compiler_params=vmem_params(24),
        cost_estimate=pl.CostEstimate(flops=40_000_000, bytes_accessed=6_000_000, transcendentals=0),
    )(wide, wall_time, spin_index, wall, links, clover, stencil)


def fine_kernel(
    wide_ref, partial_ref, ta_ref, tb_ref, za_ref, zb_ref, xa_ref, xb_ref, links_hbm, near_hbm,
    out_ref, links_ref, near_ref, tedge, zedge, xedge, residual, rows_ref, sems,
):
    links_copy = pltpu.make_async_copy(links_hbm.at[pl.ds(0, 6)], links_ref, sems.at[0])
    near_copy = pltpu.make_async_copy(near_hbm, near_ref, sems.at[1])
    links_copy.start()
    near_copy.start()
    even = [is_even(axis) for axis in ("ta", "gz", "xy")]
    slabs = ((ta_ref, tb_ref), (za_ref, zb_ref), (xa_ref, xb_ref))
    for direction in range(3):
        for side, sign in enumerate((-1.0, 1.0)):
            toward_a, toward_b = slabs[direction]

            def load(part, component):
                a = toward_a[12 * part + component].astype(F32)
                b = toward_b[12 * part + component].astype(F32)
                return jnp.where(even[direction], a, b) if side == 0 else jnp.where(even[direction], b, a)

            edge = projected(direction, sign, load)
            for s in range(2):
                for colour in range(3):
                    for part in range(2):
                        slot = 6 * s + 2 * colour + part
                        value = edge[s][colour][part]
                        if direction == 0:
                            for r in range(4):
                                tedge[side, slot, r, 0:4, :] = value[4 * r : 4 * r + 4]
                                tedge[side, slot, r, 4:8, :] = value[4 * r : 4 * r + 4]
                        elif direction == 1:
                            zedge[side, slot] = value
                        else:
                            xedge[side, slot] = value
    links_copy.wait()
    lanes = lane_index(HALF)
    sub = row_index(HALF)
    upper = sub >= 4
    z = sub % BLOCK

    def rhs(r, carry):
        def table(read):
            return [[tuple(read(6 * s + 2 * colour + part) for part in range(2)) for colour in range(3)] for s in range(2)]

        for half in range(2):
            low = HALF * half

            def loader(start):
                def load(part, component):
                    return wide_ref[part, r, component, start : start + HALF, :]
                return load

            total = [[[None, None] for _ in range(3)] for _ in range(4)]
            for side, sign in enumerate((-1.0, 1.0)):
                def turned(start):
                    return mapped(lambda p: pltpu.roll(p, 4, 0), projected(0, sign, loader(start)))

                edge = table(lambda slot: tedge[side, slot, r])
                if side == 0:
                    lower_part, upper_part = (turned(0), turned(8)) if half == 0 else (turned(8), edge)
                else:
                    lower_part, upper_part = (edge, turned(0)) if half == 0 else (turned(0), turned(8))
                field = mapped(lambda a, b: jnp.where(upper, b, a), lower_part, upper_part)
                hop(0, sign, field, link_loader(links_ref, side, low), total)
            for side, sign in enumerate((-1.0, 1.0)):
                row = 4 * r + 2 * half
                first = table(lambda slot: zedge[side, slot, pl.ds(row, 1), :])
                second = table(lambda slot: zedge[side, slot, pl.ds(row + 1, 1), :])
                shift, place = (HALF - 1, 3) if side == 0 else (1, 0)
                field = mapped(
                    lambda p, a, b: jnp.where(z == place, jnp.where(upper, b, a), pltpu.roll(p, shift, 0)),
                    projected(1, sign, loader(low)), first, second,
                )
                hop(1, sign, field, link_loader(links_ref, 2 + side, low), total)
            for side, sign in enumerate((-1.0, 1.0)):
                edge = table(lambda slot: xedge[side, slot, low : low + HALF, :])
                if side == 0:
                    inside = lanes < 96
                    amount = lax.rem(96 - 32 * r + LANES, LANES)
                    shift = LANES - 32
                else:
                    inside = lanes >= 32
                    amount = lax.rem(LANES - 32 * r, LANES)
                    shift = 32
                field = mapped(
                    lambda p, e: jnp.where(inside, pltpu.roll(p, shift, 1), pltpu.roll(e, amount, 1)),
                    projected(2, sign, loader(low)), edge,
                )
                hop(2, sign, field, link_loader(links_ref, 4 + side, low), total)
            for s in range(4):
                for colour in range(3):
                    for part in range(2):
                        position = 12 * part + 3 * s + colour
                        residual[r, position, low : low + HALF, :] = (
                            partial_ref[r, position, low : low + HALF, :] + 0.5 * total[s][colour][part]
                        )
        return carry

    lax.fori_loop(0, 4, rhs, 0)

    for part in range(2):
        rows_ref[part] = jnp.zeros((LANES, LANES), F32)
    near_copy.wait()

    def vector(v, carry):
        for chirality in range(2):
            acc = [[None, None] for _ in range(4)]
            for c in range(6):
                position = 6 * chirality + c
                nre16 = near_ref[v, 0, position].astype(F32)
                nim16 = near_ref[v, 1, position].astype(F32)
                for half in range(2):
                    low = HALF * half
                    nre = nre16[low : low + HALF]
                    nim = nim16[low : low + HALF]
                    for r in range(4):
                        rre = residual[r, position, low : low + HALF, :]
                        rim = residual[r, 12 + position, low : low + HALF, :]
                        tre = nre * rre + nim * rim
                        tim = nre * rim - nim * rre
                        acc[r][0] = tre if acc[r][0] is None else acc[r][0] + tre
                        acc[r][1] = tim if acc[r][1] is None else acc[r][1] + tim
            for r in range(4):
                for part in range(2):
                    rows_ref[part, pl.ds(r * 32 + chirality * 12 + v, 1), :] = jnp.sum(
                        acc[r][part], axis=0, keepdims=True
                    )
        return carry

    lax.fori_loop(0, 12, vector, 0)
    member = ((lane_index(HALF) % NY) // BLOCK == row_index(HALF)).astype(F32)
    for part in range(2):
        out_ref[part] = lax.dot_general(
            member, rows_ref[part], (((1,), (1,)), ((), ())),
            precision=lax.Precision.HIGHEST, preferred_element_type=F32,
        )


def fine(wide, partial, halos, links, near):
    vm = pl.BlockSpec(memory_space=pltpu.VMEM)
    hbm = pl.BlockSpec(memory_space=pltpu.HBM)
    return pl.pallas_call(
        fine_kernel,
        out_shape=jax.ShapeDtypeStruct((2, HALF, LANES), F32),
        in_specs=[vm] * 8 + [hbm] * 2,
        out_specs=vm,
        scratch_shapes=[
            pltpu.VMEM((6, 2, 3, 3, ROWS, LANES), BF16),
            pltpu.VMEM((12, 2, 12, ROWS, LANES), BF16),
            pltpu.VMEM((2, 12, 4, HALF, LANES), F32),
            pltpu.VMEM((2, 12, ROWS, LANES), F32),
            pltpu.VMEM((2, 12, ROWS, LANES), F32),
            pltpu.VMEM((4, 24, ROWS, LANES), F32),
            pltpu.VMEM((2, LANES, LANES), F32),
            pltpu.SemaphoreType.DMA((2,)),
        ],
        compiler_params=vmem_params(24),
    )(wide, partial, *halos, links, near)


def merge(low, high, width, inside):
    if high is None:
        high = jnp.zeros_like(low)
    keep = jnp.where(inside, low, high)
    other = jnp.where(inside, high, low)
    return keep + jnp.where(inside, turn_lanes(other, -width), turn_lanes(other, width))


def coarse_step(estimate, neighbours, restricted_ref, operator_ref):
    members = [estimate] + neighbours
    lanes = lane_index(HALF)
    out = []
    sums = [[None] * 24, [None] * 24]
    for i in range(24):
        re = None
        im = None
        for k in range(9):
            cre = operator_ref[(k * 2) * 24 + i]
            cim = operator_ref[(k * 2 + 1) * 24 + i]
            ere, eim = members[k]
            tre = cre * ere - cim * eim
            tim = cre * eim + cim * ere
            re = tre if re is None else re + tre
            im = tim if im is None else im + tim
        sums[0][i] = re
        sums[1][i] = im
    for part in range(2):
        values = sums[part] + [None] * 8
        width = 16
        while width >= 1:
            inside = (lanes // width) % 2 == 0
            count = width
            values = [
                None if values[i] is None else merge(values[i], values[i + count], width, inside)
                for i in range(count)
            ]
            width //= 2
        out.append(restricted_ref[part] + values[0])
    return out


def coarse_neighbours(estimate, refs):
    neighbours = []
    for direction, axis in enumerate(("ta", "gz", "xy")):
        even = is_even(axis)
        a = refs[2 * direction]
        b = refs[2 * direction + 1]
        neighbours.append(tuple(jnp.where(even, a[part], b[part]) for part in range(2)))
        neighbours.append(tuple(jnp.where(even, b[part], a[part]) for part in range(2)))
    neighbours.append(tuple(pltpu.roll(value, HALF - 1, 0) for value in estimate))
    neighbours.append(tuple(pltpu.roll(value, 1, 0) for value in estimate))
    return neighbours


def coarse_kernel(e_ref, tp, tm, zp, zm, xp, xm, r_ref, operator_ref, out_ref):
    estimate = (e_ref[0], e_ref[1])
    out = coarse_step(estimate, coarse_neighbours(estimate, (tp, tm, zp, zm, xp, xm)), r_ref, operator_ref)
    out_ref[0] = out[0]
    out_ref[1] = out[1]


def coarse(estimate, halos, restricted, operator):
    vm = pl.BlockSpec(memory_space=pltpu.VMEM)
    return pl.pallas_call(
        coarse_kernel,
        out_shape=jax.ShapeDtypeStruct((2, HALF, LANES), F32),
        in_specs=[vm] * 9,
        out_specs=vm,
        compiler_params=vmem_params(16),
    )(estimate, *halos, restricted, operator)


def last_kernel(e_ref, tp, tm, zp, zm, xp, xm, r_ref, operator_ref, psi_ref, near_ref, out_ref, wide):
    estimate = (e_ref[0], e_ref[1])
    final = coarse_step(estimate, coarse_neighbours(estimate, (tp, tm, zp, zm, xp, xm)), r_ref, operator_ref)
    member = ((lane_index(HALF) % NY) // BLOCK == row_index(HALF)).astype(F32)
    for part in range(2):
        wide[part] = lax.dot_general(
            final[part], member, (((0,), (0,)), ((), ())),
            precision=lax.Precision.HIGHEST, preferred_element_type=F32,
        )

    def component(c, carry):
        base = (c // 6) * 12
        near = [(near_ref[v, 0, c].astype(F32), near_ref[v, 1, c].astype(F32)) for v in range(12)]
        for r in range(4):
            re = psi_ref[0, r, c]
            im = psi_ref[1, r, c]
            for v in range(12):
                ere = wide[0, pl.ds(r * 32 + base + v, 1), :]
                eim = wide[1, pl.ds(r * 32 + base + v, 1), :]
                nre, nim = near[v]
                re = re + (nre * ere - nim * eim)
                im = im + (nre * eim + nim * ere)
            out_ref[0, r, c] = re
            out_ref[1, r, c] = im
        return carry

    lax.fori_loop(0, 12, component, 0)


def last(estimate, halos, restricted, operator, psi, near):
    vm = pl.BlockSpec(memory_space=pltpu.VMEM)
    return pl.pallas_call(
        last_kernel,
        out_shape=jax.ShapeDtypeStruct((2, 4, 12, ROWS, LANES), F32),
        in_specs=[vm] * 11,
        out_specs=vm,
        scratch_shapes=[pltpu.VMEM((2, LANES, LANES), F32)],
        compiler_params=vmem_params(24),
    )(estimate, *halos, restricted, operator, psi, near)


def exchange(values):
    return [
        swap(value, axis, which % 2)
        for which, (value, axis) in enumerate(zip(values, ("ta", "ta", "gz", "gz", "xy", "xy")))
    ]


def local(
    fine_solution, links, clover, near_null, coarse_links, wall_time, spin_index, wall_colour
):
    psi = fine_solution.reshape((2, 4, 12, ROWS, LANES))
    links = links.reshape((8, 2, 3, 3, ROWS, LANES))
    clover = clover.reshape((2, 2, 6, 6, ROWS, LANES))
    near = near_null.reshape((12, 2, 12, ROWS, LANES))
    stencil = jnp.transpose(coarse_links, (0, 1, 2, 4, 5, 6, 3)).reshape((9 * 2 * 24, HALF, 24))
    wall = jnp.transpose(wall_colour, (2, 0, 1))
    *slabs, wide = pack(psi)
    halos = exchange(slabs)
    partial, operator = centre(wide, wall_time, spin_index, wall, links, clover, stencil)
    restricted = fine(wide, partial, halos, links, near)
    estimate = restricted
    for step in range(ITERS - 1):
        estimate = coarse(estimate, exchange([estimate] * 6), restricted, operator)
    result = last(estimate, exchange([estimate] * 6), restricted, operator, wide, near)
    return result.reshape(fine_solution.shape)


def solution(mesh):
    placed = (
        P(None, None, None, "ta", "gz", "xy"),
        P(None, None, None, None, "ta", "gz", "xy"),
        P(None, None, None, None, "ta", "gz", "xy"),
        P(None, None, None, "ta", "gz", "xy"),
        P(None, None, None, None, "ta", "gz", "xy"),
        P(),
        P(),
        P(),
    )
    return jax.shard_map(
        local,
        mesh=mesh,
        in_specs=placed,
        out_specs=P(None, None, None, "ta", "gz", "xy"),
        check_vma=False,
    )
```

time: 123 us -> 75.3 us (0.61)
  Pallas kernels: 53.1 us -> 15.5 us
  starting transfers between devices: 52.4 us -> 35.7 us
  waiting for transfers between devices: 9.56 us -> 17 us
    pallas_call x2, Pallas kernels: 33.3 us -> 5.94 us  [the longest x1 5.16 us: centre(): pl.pallas_call(centre_kernel, out_shape=(jax.ShapeDtypeStruct((4, 24, ROW...]
    ppermute x30, starting transfers between devices: 52.4 us -> 35.7 us  [swap(): return lax.ppermute(value, axis, pairs)]
    pallas_call x1, Pallas kernels: 14.3 us -> 4.12 us  [fine(): pl.pallas_call(fine_kernel, out_shape=jax.ShapeDtypeStruct((2, HALF, LANE...]
    ppermute x30, waiting for transfers between devices: 9.56 us -> 17 us  [swap(): return lax.ppermute(value, axis, pairs)]
    unnamed x17 -> x18, local copies, waits for them, and re-layouts: 7.48 us -> 6.6 us
  transfers between devices with their start and end apart: 30 -> 30, of which waited for: 6 -> 11; matrix products, arithmetic and copies ran while one was open for 1% -> 0% of each run, Pallas kernels for 25% -> 7%
where the time goes in v2:
time: 75.3 us; the launch traced here: 75 us
  starting transfers between devices  35.7 us (47%)
  waiting for transfers between devices  17 us (23%)
  Pallas kernels  15.5 us (21%)
  local copies, waits for them, and re-layouts  6.6 us (9%)
    ppermute x30, starting transfers between devices, swap(): return lax.ppermute(value, axis, pairs)  35.7 us
    ppermute x30, waiting for transfers between devices, swap(): return lax.ppermute(value, axis, pairs)  17 us
    unnamed x18, local copies, waits for them, and re-layouts  6.6 us
    pallas_call x1, Pallas kernels, centre(): pl.pallas_call(centre_kernel, out_shape=(jax.ShapeDtypeStruct((4, 24, ROW...  5.16 us
    pallas_call x1, Pallas kernels, fine(): pl.pallas_call(fine_kernel, out_shape=jax.ShapeDtypeStruct((2, HALF, LANE...  4.12 us
    pallas_call x1, Pallas kernels, last(): pl.pallas_call(last_kernel, out_shape=jax.ShapeDtypeStruct((2, 4, 12, ROW...  3.39 us
    pallas_call x3, Pallas kernels, coarse(): pl.pallas_call(coarse_kernel, out_shape=jax.ShapeDtypeStruct((2, HALF, LA...  2.04 us
  transfers between devices with their start and end apart: 30, of which 11 were waited for; matrix products, arithmetic and copies ran while one was open for 0% of the time, Pallas kernels for 7%

profile of v2, /device:TPU:0, one launch (start us, length us, event | category | flops | bytes accessed | tf_op | source)
XLA Modules:
  0.0 75.0 jit_solution(557351453483261765)
XLA Ops:
  1.8 2.1 %collective-permute-start = (bf16[24,16,128]{2,1,0:T(8,128)(2,1)S(1)}, bf16[24,16,128]{2,1,0:T(8,128)(2,1)S(1)}, u32[]{:S(2)}, u32[]{:S(2)}) collective-permute-start(bf16[24,16,128]{2,1,0:T(8,128)(2,1)S(1)} %get-tuple-element.16), channel_id=1, source_target_pairs={{0,16},{16,0},{32,48},{48,32},{64,80},{80,64},{96,112},{112,96},{1... | collective-permute-start | bytes 294920 | tf_op jit(solution)/shard_map/ppermute | solution.py:48
  3.9 3.5 %collective-permute-start.1 = (bf16[24,16,128]{2,1,0:T(8,128)(2,1)S(1)}, bf16[24,16,128]{2,1,0:T(8,128)(2,1)S(1)}, u32[]{:S(2)}, u32[]{:S(2)}) collective-permute-start(bf16[24,16,128]{2,1,0:T(8,128)(2,1)S(1)} %get-tuple-element.17), channel_id=1, source_target_pairs={{0,112},{16,32},{32,16},{48,64},{64,48},{80,96},{96,80},{112,0},{1... | collective-permute-start | bytes 294920 | tf_op jit(solution)/shard_map/ppermute | solution.py:48
  7.4 1.5 %collective-permute-start.2 = (bf16[24,16,128]{2,1,0:T(8,128)(2,1)S(1)}, bf16[24,16,128]{2,1,0:T(8,128)(2,1)S(1)}, u32[]{:S(2)}, u32[]{:S(2)}) collective-permute-start(bf16[24,16,128]{2,1,0:T(8,128)(2,1)S(1)} %get-tuple-element.18), channel_id=1, source_target_pairs={{0,4},{4,0},{8,12},{12,8},{1,5},{5,1},{9,13},{13,9},{2,6},{6,2},{1... | collective-permute-start | bytes 294920 | tf_op jit(solution)/shard_map/ppermute | solution.py:48
  8.9 2.1 %collective-permute-start.3 = (bf16[24,16,128]{2,1,0:T(8,128)(2,1)S(1)}, bf16[24,16,128]{2,1,0:T(8,128)(2,1)S(1)}, u32[]{:S(2)}, u32[]{:S(2)}) collective-permute-start(bf16[24,16,128]{2,1,0:T(8,128)(2,1)S(1)} %get-tuple-element.19), channel_id=1, source_target_pairs={{0,12},{4,8},{8,4},{12,0},{1,13},{5,9},{9,5},{13,1},{2,14},{6,10},... | collective-permute-start | bytes 294920 | tf_op jit(solution)/shard_map/ppermute | solution.py:48
  11.0 3.0 %collective-permute-start.5 = (bf16[24,16,128]{2,1,0:T(8,128)(2,1)S(1)}, bf16[24,16,128]{2,1,0:T(8,128)(2,1)S(1)}, u32[]{:S(2)}, u32[]{:S(2)}) collective-permute-start(bf16[24,16,128]{2,1,0:T(8,128)(2,1)S(1)} %get-tuple-element.21), channel_id=1, source_target_pairs={{0,3},{1,2},{2,1},{3,0},{4,7},{5,6},{6,5},{7,4},{8,11},{9,10},{10,... | collective-permute-start | bytes 294920 | tf_op jit(solution)/shard_map/ppermute | solution.py:48
  15.1 1.5 %copy-done.3 = f32[9,2,24,24,1,1,8]{3,6,5,4,2,1,0:T(8,128)S(1)} copy-done((f32[9,2,24,24,1,1,8]{3,6,5,4,2,1,0:T(8,128)S(1)}, f32[9,2,24,24,1,1,8]{3,6,5,4,2,1,0:T(8,128)}, u32[]{:S(2)}) %copy-start.3) | copy-done | bytes 331800
  19.6 5.2 %shard_map.83 = (f32[4,24,16,128]{3,2,1,0:T(8,128)S(1)}, f32[432,8,128]{2,1,0:T(8,128)S(1)}) custom-call(f32[2,4,12,16,128]{4,3,2,1,0:T(8,128)S(1)} %get-tuple-element.14.wide_ref.psi_ref, s32[4]{0:T(128)S(1)} %copy-done.7, s32[4]{0:T(128)S(1)} %copy-done.8, f32[3,2,4]{2,1,0:T(2,128)S(1)} %bitcast.16, bf16[8,2,3,3,16,128]{5,4,3,2,1,0:T(8,128)(2,1)S(1)} %bitcast.11, ...), custom_call_target="tpu_custom_call" | custom-call | flops 40000000 | bytes 6000000 | tf_op jit(solution)/shard_map/pallas_call | solution.py:255
  24.9 4.1 %shard_map.84.e_ref.r_ref = f32[2,8,128]{2,1,0:T(8,128)S(1)} custom-call(f32[2,4,12,16,128]{4,3,2,1,0:T(8,128)S(1)} %get-tuple-element.14.wide_ref.psi_ref, f32[4,24,16,128]{3,2,1,0:T(8,128)S(1)} %get-tuple-element.15.partial_ref, bf16[24,16,128]{2,1,0:T(8,128)(2,1)S(1)} %collective-permute-done.ta_ref, ...), custom_call_target="tpu_custom_call" | custom-call | tf_op jit(solution)/shard_map/pallas_call | solution.py:417
  31.0 2.0 %collective-permute-start.7 = (f32[2,8,128]{2,1,0:T(8,128)S(1)}, f32[2,8,128]{2,1,0:T(8,128)S(1)}, u32[]{:S(2)}, u32[]{:S(2)}) collective-permute-start(f32[2,8,128]{2,1,0:T(8,128)S(1)} %shard_map.84.e_ref.r_ref), channel_id=1, source_target_pairs={{0,112},{16,32},{32,16},{48,64},{64,48},{80,96},{96,80},{112,0},{1... | collective-permute-start | bytes 24584 | tf_op jit(solution)/shard_map/ppermute | solution.py:48
  34.7 2.0 %collective-permute-done.7.tm = f32[2,8,128]{2,1,0:T(8,128)S(1)} collective-permute-done((f32[2,8,128]{2,1,0:T(8,128)S(1)}, f32[2,8,128]{2,1,0:T(8,128)S(1)}, u32[]{:S(2)}, u32[]{:S(2)}) %collective-permute-start.7) | collective-permute-done | bytes 8224 | tf_op jit(solution)/shard_map/ppermute | solution.py:48
  38.5 1.9 %collective-permute-start.16 = (f32[2,8,128]{2,1,0:T(8,128)S(1)}, f32[2,8,128]{2,1,0:T(8,128)S(1)}, u32[]{:S(2)}, u32[]{:S(2)}) collective-permute-start(f32[2,8,128]{2,1,0:T(8,128)S(1)} %shard_map.85.e_ref), channel_id=1, source_target_pairs={{0,1},{1,0},{2,3},{3,2},{4,5},{5,4},{6,7},{7,6},{8,9},{9,8},{10,11... | collective-permute-start | bytes 24584 | tf_op jit(solution)/shard_map/ppermute | solution.py:48
  40.4 2.1 %collective-permute-start.15 = (f32[2,8,128]{2,1,0:T(8,128)S(1)}, f32[2,8,128]{2,1,0:T(8,128)S(1)}, u32[]{:S(2)}, u32[]{:S(2)}) collective-permute-start(f32[2,8,128]{2,1,0:T(8,128)S(1)} %shard_map.85.e_ref), channel_id=1, source_target_pairs={{0,12},{4,8},{8,4},{12,0},{1,13},{5,9},{9,5},{13,1},{2,14},{6,10},... | collective-permute-start | bytes 24584 | tf_op jit(solution)/shard_map/ppermute | solution.py:48
  42.5 1.4 %collective-permute-start.14 = (f32[2,8,128]{2,1,0:T(8,128)S(1)}, f32[2,8,128]{2,1,0:T(8,128)S(1)}, u32[]{:S(2)}, u32[]{:S(2)}) collective-permute-start(f32[2,8,128]{2,1,0:T(8,128)S(1)} %shard_map.85.e_ref), channel_id=1, source_target_pairs={{0,4},{4,0},{8,12},{12,8},{1,5},{5,1},{9,13},{13,9},{2,6},{6,2},{1... | collective-permute-start | bytes 24584 | tf_op jit(solution)/shard_map/ppermute | solution.py:48
  44.0 1.4 %collective-permute-start.13 = (f32[2,8,128]{2,1,0:T(8,128)S(1)}, f32[2,8,128]{2,1,0:T(8,128)S(1)}, u32[]{:S(2)}, u32[]{:S(2)}) collective-permute-start(f32[2,8,128]{2,1,0:T(8,128)S(1)} %shard_map.85.e_ref), channel_id=1, source_target_pairs={{0,112},{16,32},{32,16},{48,64},{64,48},{80,96},{96,80},{112,0},{1... | collective-permute-start | bytes 24584 | tf_op jit(solution)/shard_map/ppermute | solution.py:48
  46.2 3.5 %collective-permute-done.13.tm = f32[2,8,128]{2,1,0:T(8,128)S(1)} collective-permute-done((f32[2,8,128]{2,1,0:T(8,128)S(1)}, f32[2,8,128]{2,1,0:T(8,128)S(1)}, u32[]{:S(2)}, u32[]{:S(2)}) %collective-permute-start.13) | collective-permute-done | bytes 8224 | tf_op jit(solution)/shard_map/ppermute | solution.py:48
  52.9 1.4 %collective-permute-start.19 = (f32[2,8,128]{2,1,0:T(8,128)S(1)}, f32[2,8,128]{2,1,0:T(8,128)S(1)}, u32[]{:S(2)}, u32[]{:S(2)}) collective-permute-start(f32[2,8,128]{2,1,0:T(8,128)S(1)} %shard_map.86.e_ref), channel_id=1, source_target_pairs={{0,112},{16,32},{32,16},{48,64},{64,48},{80,96},{96,80},{112,0},{1... | collective-permute-start | bytes 24584 | tf_op jit(solution)/shard_map/ppermute | solution.py:48
  55.0 1.5 %collective-permute-done.21.zm = f32[2,8,128]{2,1,0:T(8,128)S(1)} collective-permute-done((f32[2,8,128]{2,1,0:T(8,128)S(1)}, f32[2,8,128]{2,1,0:T(8,128)S(1)}, u32[]{:S(2)}, u32[]{:S(2)}) %collective-permute-start.21) | collective-permute-done | bytes 8224 | tf_op jit(solution)/shard_map/ppermute | solution.py:48
  56.5 2.1 %collective-permute-done.19.tm = f32[2,8,128]{2,1,0:T(8,128)S(1)} collective-permute-done((f32[2,8,128]{2,1,0:T(8,128)S(1)}, f32[2,8,128]{2,1,0:T(8,128)S(1)}, u32[]{:S(2)}, u32[]{:S(2)}) %collective-permute-start.19) | collective-permute-done | bytes 8224 | tf_op jit(solution)/shard_map/ppermute | solution.py:48
  60.4 1.9 %collective-permute-start.28 = (f32[2,8,128]{2,1,0:T(8,128)S(1)}, f32[2,8,128]{2,1,0:T(8,128)S(1)}, u32[]{:S(2)}, u32[]{:S(2)}) collective-permute-start(f32[2,8,128]{2,1,0:T(8,128)S(1)} %shard_map.87.e_ref), channel_id=1, source_target_pairs={{0,1},{1,0},{2,3},{3,2},{4,5},{5,4},{6,7},{7,6},{8,9},{9,8},{10,11... | collective-permute-start | bytes 24584 | tf_op jit(solution)/shard_map/ppermute | solution.py:48
  62.3 2.1 %collective-permute-start.27 = (f32[2,8,128]{2,1,0:T(8,128)S(1)}, f32[2,8,128]{2,1,0:T(8,128)S(1)}, u32[]{:S(2)}, u32[]{:S(2)}) collective-permute-start(f32[2,8,128]{2,1,0:T(8,128)S(1)} %shard_map.87.e_ref), channel_id=1, source_target_pairs={{0,12},{4,8},{8,4},{12,0},{1,13},{5,9},{9,5},{13,1},{2,14},{6,10},... | collective-permute-start | bytes 24584 | tf_op jit(solution)/shard_map/ppermute | solution.py:48
  64.4 1.4 %collective-permute-start.26 = (f32[2,8,128]{2,1,0:T(8,128)S(1)}, f32[2,8,128]{2,1,0:T(8,128)S(1)}, u32[]{:S(2)}, u32[]{:S(2)}) collective-permute-start(f32[2,8,128]{2,1,0:T(8,128)S(1)} %shard_map.87.e_ref), channel_id=1, source_target_pairs={{0,4},{4,0},{8,12},{12,8},{1,5},{5,1},{9,13},{13,9},{2,6},{6,2},{1... | collective-permute-start | bytes 24584 | tf_op jit(solution)/shard_map/ppermute | solution.py:48
  65.8 1.5 %collective-permute-start.25 = (f32[2,8,128]{2,1,0:T(8,128)S(1)}, f32[2,8,128]{2,1,0:T(8,128)S(1)}, u32[]{:S(2)}, u32[]{:S(2)}) collective-permute-start(f32[2,8,128]{2,1,0:T(8,128)S(1)} %shard_map.87.e_ref), channel_id=1, source_target_pairs={{0,112},{16,32},{32,16},{48,64},{64,48},{80,96},{96,80},{112,0},{1... | collective-permute-start | bytes 24584 | tf_op jit(solution)/shard_map/ppermute | solution.py:48
  68.0 3.5 %collective-permute-done.25.tm = f32[2,8,128]{2,1,0:T(8,128)S(1)} collective-permute-done((f32[2,8,128]{2,1,0:T(8,128)S(1)}, f32[2,8,128]{2,1,0:T(8,128)S(1)}, u32[]{:S(2)}, u32[]{:S(2)}) %collective-permute-start.25) | collective-permute-done | bytes 8224 | tf_op jit(solution)/shard_map/ppermute | solution.py:48
  71.6 3.4 %shard_map.88 = f32[2,4,12,16,128]{4,3,2,1,0:T(8,128)} custom-call(f32[2,8,128]{2,1,0:T(8,128)S(1)} %shard_map.87.e_ref, f32[2,8,128]{2,1,0:T(8,128)S(1)} %collective-permute-done.24.tp, f32[2,8,128]{2,1,0:T(8,128)S(1)} %collective-permute-done.25.tm, f32[2,8,128]{2,1,0:T(8,128)S(1)} %collective-permute-done.26.zp, ...), custom_call_target="tpu_custom_call" | custom-call | tf_op jit(solution)/shard_map/pallas_call | solution.py:539
  (61 shorter events, 18.5 us)
Async XLA Ops:
  1.8 9.2 %collective-permute-start = (bf16[24,16,128]{2,1,0:T(8,128)(2,1)S(1)}, bf16[24,16,128]{2,1,0:T(8,128)(2,1)S(1)}, u32[]{:S(2)}, u32[]{:S(2)}) collective-permute-start(bf16[24,16,128]{2,1,0:T(8,128)(2,1)S(1)} %get-tuple-element.16), channel_id=1, source_target_pairs={{0,16},{16,0},{32,48},{48,32},{64,80},{80,64},{96,112},{112,96},{1... | collective-permute-start | bytes 294920 | tf_op jit(solution)/shard_map/ppermute | solution.py:48
  3.9 20.9 %collective-permute-start.1 = (bf16[24,16,128]{2,1,0:T(8,128)(2,1)S(1)}, bf16[24,16,128]{2,1,0:T(8,128)(2,1)S(1)}, u32[]{:S(2)}, u32[]{:S(2)}) collective-permute-start(bf16[24,16,128]{2,1,0:T(8,128)(2,1)S(1)} %get-tuple-element.17), channel_id=1, source_target_pairs={{0,112},{16,32},{32,16},{48,64},{64,48},{80,96},{96,80},{112,0},{1... | collective-permute-start | bytes 294920 | tf_op jit(solution)/shard_map/ppermute | solution.py:48
  7.4 17.4 %collective-permute-start.2 = (bf16[24,16,128]{2,1,0:T(8,128)(2,1)S(1)}, bf16[24,16,128]{2,1,0:T(8,128)(2,1)S(1)}, u32[]{:S(2)}, u32[]{:S(2)}) collective-permute-start(bf16[24,16,128]{2,1,0:T(8,128)(2,1)S(1)} %get-tuple-element.18), channel_id=1, source_target_pairs={{0,4},{4,0},{8,12},{12,8},{1,5},{5,1},{9,13},{13,9},{2,6},{6,2},{1... | collective-permute-start | bytes 294920 | tf_op jit(solution)/shard_map/ppermute | solution.py:48
  8.9 15.9 %collective-permute-start.3 = (bf16[24,16,128]{2,1,0:T(8,128)(2,1)S(1)}, bf16[24,16,128]{2,1,0:T(8,128)(2,1)S(1)}, u32[]{:S(2)}, u32[]{:S(2)}) collective-permute-start(bf16[24,16,128]{2,1,0:T(8,128)(2,1)S(1)} %get-tuple-element.19), channel_id=1, source_target_pairs={{0,12},{4,8},{8,4},{12,0},{1,13},{5,9},{9,5},{13,1},{2,14},{6,10},... | collective-permute-start | bytes 294920 | tf_op jit(solution)/shard_map/ppermute | solution.py:48
  11.0 13.8 %collective-permute-start.4 = (bf16[24,16,128]{2,1,0:T(8,128)(2,1)S(1)}, bf16[24,16,128]{2,1,0:T(8,128)(2,1)S(1)}, u32[]{:S(2)}, u32[]{:S(2)}) collective-permute-start(bf16[24,16,128]{2,1,0:T(8,128)(2,1)S(1)} %get-tuple-element.20), channel_id=1, source_target_pairs={{0,1},{1,0},{2,3},{3,2},{4,5},{5,4},{6,7},{7,6},{8,9},{9,8},{10,11... | collective-permute-start | bytes 294920 | tf_op jit(solution)/shard_map/ppermute | solution.py:48
  11.0 13.8 %collective-permute-start.5 = (bf16[24,16,128]{2,1,0:T(8,128)(2,1)S(1)}, bf16[24,16,128]{2,1,0:T(8,128)(2,1)S(1)}, u32[]{:S(2)}, u32[]{:S(2)}) collective-permute-start(bf16[24,16,128]{2,1,0:T(8,128)(2,1)S(1)} %get-tuple-element.21), channel_id=1, source_target_pairs={{0,3},{1,2},{2,1},{3,0},{4,7},{5,6},{6,5},{7,4},{8,11},{9,10},{10,... | collective-permute-start | bytes 294920 | tf_op jit(solution)/shard_map/ppermute | solution.py:48
  29.0 4.7 %collective-permute-start.11 = (f32[2,8,128]{2,1,0:T(8,128)S(1)}, f32[2,8,128]{2,1,0:T(8,128)S(1)}, u32[]{:S(2)}, u32[]{:S(2)}) collective-permute-start(f32[2,8,128]{2,1,0:T(8,128)S(1)} %shard_map.84.e_ref.r_ref), channel_id=1, source_target_pairs={{0,3},{1,2},{2,1},{3,0},{4,7},{5,6},{6,5},{7,4},{8,11},{9,10},{10,... | collective-permute-start | bytes 24584 | tf_op jit(solution)/shard_map/ppermute | solution.py:48
  29.3 4.6 %collective-permute-start.10 = (f32[2,8,128]{2,1,0:T(8,128)S(1)}, f32[2,8,128]{2,1,0:T(8,128)S(1)}, u32[]{:S(2)}, u32[]{:S(2)}) collective-permute-start(f32[2,8,128]{2,1,0:T(8,128)S(1)} %shard_map.84.e_ref.r_ref), channel_id=1, source_target_pairs={{0,1},{1,0},{2,3},{3,2},{4,5},{5,4},{6,7},{7,6},{8,9},{9,8},{10,11... | collective-permute-start | bytes 24584 | tf_op jit(solution)/shard_map/ppermute | solution.py:48
  29.8 4.9 %collective-permute-start.9 = (f32[2,8,128]{2,1,0:T(8,128)S(1)}, f32[2,8,128]{2,1,0:T(8,128)S(1)}, u32[]{:S(2)}, u32[]{:S(2)}) collective-permute-start(f32[2,8,128]{2,1,0:T(8,128)S(1)} %shard_map.84.e_ref.r_ref), channel_id=1, source_target_pairs={{0,12},{4,8},{8,4},{12,0},{1,13},{5,9},{9,5},{13,1},{2,14},{6,10},... | collective-permute-start | bytes 24584 | tf_op jit(solution)/shard_map/ppermute | solution.py:48
  31.0 5.8 %collective-permute-start.7 = (f32[2,8,128]{2,1,0:T(8,128)S(1)}, f32[2,8,128]{2,1,0:T(8,128)S(1)}, u32[]{:S(2)}, u32[]{:S(2)}) collective-permute-start(f32[2,8,128]{2,1,0:T(8,128)S(1)} %shard_map.84.e_ref.r_ref), channel_id=1, source_target_pairs={{0,112},{16,32},{32,16},{48,64},{64,48},{80,96},{96,80},{112,0},{1... | collective-permute-start | bytes 24584 | tf_op jit(solution)/shard_map/ppermute | solution.py:48
  38.0 7.4 %collective-permute-start.17 = (f32[2,8,128]{2,1,0:T(8,128)S(1)}, f32[2,8,128]{2,1,0:T(8,128)S(1)}, u32[]{:S(2)}, u32[]{:S(2)}) collective-permute-start(f32[2,8,128]{2,1,0:T(8,128)S(1)} %shard_map.85.e_ref), channel_id=1, source_target_pairs={{0,3},{1,2},{2,1},{3,0},{4,7},{5,6},{6,5},{7,4},{8,11},{9,10},{10,... | collective-permute-start | bytes 24584 | tf_op jit(solution)/shard_map/ppermute | solution.py:48
  38.5 6.9 %collective-permute-start.16 = (f32[2,8,128]{2,1,0:T(8,128)S(1)}, f32[2,8,128]{2,1,0:T(8,128)S(1)}, u32[]{:S(2)}, u32[]{:S(2)}) collective-permute-start(f32[2,8,128]{2,1,0:T(8,128)S(1)} %shard_map.85.e_ref), channel_id=1, source_target_pairs={{0,1},{1,0},{2,3},{3,2},{4,5},{5,4},{6,7},{7,6},{8,9},{9,8},{10,11... | collective-permute-start | bytes 24584 | tf_op jit(solution)/shard_map/ppermute | solution.py:48
  40.4 5.0 %collective-permute-start.15 = (f32[2,8,128]{2,1,0:T(8,128)S(1)}, f32[2,8,128]{2,1,0:T(8,128)S(1)}, u32[]{:S(2)}, u32[]{:S(2)}) collective-permute-start(f32[2,8,128]{2,1,0:T(8,128)S(1)} %shard_map.85.e_ref), channel_id=1, source_target_pairs={{0,12},{4,8},{8,4},{12,0},{1,13},{5,9},{9,5},{13,1},{2,14},{6,10},... | collective-permute-start | bytes 24584 | tf_op jit(solution)/shard_map/ppermute | solution.py:48
  44.0 5.8 %collective-permute-start.13 = (f32[2,8,128]{2,1,0:T(8,128)S(1)}, f32[2,8,128]{2,1,0:T(8,128)S(1)}, u32[]{:S(2)}, u32[]{:S(2)}) collective-permute-start(f32[2,8,128]{2,1,0:T(8,128)S(1)} %shard_map.85.e_ref), channel_id=1, source_target_pairs={{0,112},{16,32},{32,16},{48,64},{64,48},{80,96},{96,80},{112,0},{1... | collective-permute-start | bytes 24584 | tf_op jit(solution)/shard_map/ppermute | solution.py:48
  45.4 4.3 %collective-permute-start.12 = (f32[2,8,128]{2,1,0:T(8,128)S(1)}, f32[2,8,128]{2,1,0:T(8,128)S(1)}, u32[]{:S(2)}, u32[]{:S(2)}) collective-permute-start(f32[2,8,128]{2,1,0:T(8,128)S(1)} %shard_map.85.e_ref), channel_id=1, source_target_pairs={{0,16},{16,0},{32,48},{48,32},{64,80},{80,64},{96,112},{112,96},{1... | collective-permute-start | bytes 24584 | tf_op jit(solution)/shard_map/ppermute | solution.py:48
  50.4 4.6 %collective-permute-start.23 = (f32[2,8,128]{2,1,0:T(8,128)S(1)}, f32[2,8,128]{2,1,0:T(8,128)S(1)}, u32[]{:S(2)}, u32[]{:S(2)}) collective-permute-start(f32[2,8,128]{2,1,0:T(8,128)S(1)} %shard_map.86.e_ref), channel_id=1, source_target_pairs={{0,3},{1,2},{2,1},{3,0},{4,7},{5,6},{6,5},{7,4},{8,11},{9,10},{10,... | collective-permute-start | bytes 24584 | tf_op jit(solution)/shard_map/ppermute | solution.py:48
  50.4 4.6 %collective-permute-start.22 = (f32[2,8,128]{2,1,0:T(8,128)S(1)}, f32[2,8,128]{2,1,0:T(8,128)S(1)}, u32[]{:S(2)}, u32[]{:S(2)}) collective-permute-start(f32[2,8,128]{2,1,0:T(8,128)S(1)} %shard_map.86.e_ref), channel_id=1, source_target_pairs={{0,1},{1,0},{2,3},{3,2},{4,5},{5,4},{6,7},{7,6},{8,9},{9,8},{10,11... | collective-permute-start | bytes 24584 | tf_op jit(solution)/shard_map/ppermute | solution.py:48
  51.7 4.9 %collective-permute-start.21 = (f32[2,8,128]{2,1,0:T(8,128)S(1)}, f32[2,8,128]{2,1,0:T(8,128)S(1)}, u32[]{:S(2)}, u32[]{:S(2)}) collective-permute-start(f32[2,8,128]{2,1,0:T(8,128)S(1)} %shard_map.86.e_ref), channel_id=1, source_target_pairs={{0,12},{4,8},{8,4},{12,0},{1,13},{5,9},{9,5},{13,1},{2,14},{6,10},... | collective-permute-start | bytes 24584 | tf_op jit(solution)/shard_map/ppermute | solution.py:48
  52.9 5.8 %collective-permute-start.19 = (f32[2,8,128]{2,1,0:T(8,128)S(1)}, f32[2,8,128]{2,1,0:T(8,128)S(1)}, u32[]{:S(2)}, u32[]{:S(2)}) collective-permute-start(f32[2,8,128]{2,1,0:T(8,128)S(1)} %shard_map.86.e_ref), channel_id=1, source_target_pairs={{0,112},{16,32},{32,16},{48,64},{64,48},{80,96},{96,80},{112,0},{1... | collective-permute-start | bytes 24584 | tf_op jit(solution)/shard_map/ppermute | solution.py:48
  59.3 8.0 %collective-permute-start.29 = (f32[2,8,128]{2,1,0:T(8,128)S(1)}, f32[2,8,128]{2,1,0:T(8,128)S(1)}, u32[]{:S(2)}, u32[]{:S(2)}) collective-permute-start(f32[2,8,128]{2,1,0:T(8,128)S(1)} %shard_map.87.e_ref), channel_id=1, source_target_pairs={{0,3},{1,2},{2,1},{3,0},{4,7},{5,6},{6,5},{7,4},{8,11},{9,10},{10,... | collective-permute-start | bytes 24584 | tf_op jit(solution)/shard_map/ppermute | solution.py:48
  60.4 7.0 %collective-permute-start.28 = (f32[2,8,128]{2,1,0:T(8,128)S(1)}, f32[2,8,128]{2,1,0:T(8,128)S(1)}, u32[]{:S(2)}, u32[]{:S(2)}) collective-permute-start(f32[2,8,128]{2,1,0:T(8,128)S(1)} %shard_map.87.e_ref), channel_id=1, source_target_pairs={{0,1},{1,0},{2,3},{3,2},{4,5},{5,4},{6,7},{7,6},{8,9},{9,8},{10,11... | collective-permute-start | bytes 24584 | tf_op jit(solution)/shard_map/ppermute | solution.py:48
  62.3 5.0 %collective-permute-start.27 = (f32[2,8,128]{2,1,0:T(8,128)S(1)}, f32[2,8,128]{2,1,0:T(8,128)S(1)}, u32[]{:S(2)}, u32[]{:S(2)}) collective-permute-start(f32[2,8,128]{2,1,0:T(8,128)S(1)} %shard_map.87.e_ref), channel_id=1, source_target_pairs={{0,12},{4,8},{8,4},{12,0},{1,13},{5,9},{9,5},{13,1},{2,14},{6,10},... | collective-permute-start | bytes 24584 | tf_op jit(solution)/shard_map/ppermute | solution.py:48
  65.8 5.8 %collective-permute-start.25 = (f32[2,8,128]{2,1,0:T(8,128)S(1)}, f32[2,8,128]{2,1,0:T(8,128)S(1)}, u32[]{:S(2)}, u32[]{:S(2)}) collective-permute-start(f32[2,8,128]{2,1,0:T(8,128)S(1)} %shard_map.87.e_ref), channel_id=1, source_target_pairs={{0,112},{16,32},{32,16},{48,64},{64,48},{80,96},{96,80},{112,0},{1... | collective-permute-start | bytes 24584 | tf_op jit(solution)/shard_map/ppermute | solution.py:48
  67.3 4.3 %collective-permute-start.24 = (f32[2,8,128]{2,1,0:T(8,128)S(1)}, f32[2,8,128]{2,1,0:T(8,128)S(1)}, u32[]{:S(2)}, u32[]{:S(2)}) collective-permute-start(f32[2,8,128]{2,1,0:T(8,128)S(1)} %shard_map.87.e_ref), channel_id=1, source_target_pairs={{0,16},{16,0},{32,48},{48,32},{64,80},{80,64},{96,112},{112,96},{1... | collective-permute-start | bytes 24584 | tf_op jit(solution)/shard_map/ppermute | solution.py:48
  (15 other events, 39.1 us)

commit v3 on v2

--- a/solution.py
+++ b/solution.py
@@ -99,6 +99,7 @@
         in_specs=[vm],
         out_specs=(vm,) * 7,
         compiler_params=vmem_params(16),
+        cost_estimate=pl.CostEstimate(flops=40_000_000, bytes_accessed=40_000_000, transcendentals=0),
     )(psi)
 
 
@@ -175,18 +176,18 @@
 
 def centre_kernel(
     wide_ref, when_hbm, spin_hbm, wall_hbm, links_hbm, clover_hbm, stencil_hbm, out_ref, operator_ref,
-    when_ref, spin_ref, wall_ref, links_ref, clover_ref, stencil_ref, sems,
+    links_ref, clover_ref, stencil_ref, when_ref, spin_ref, wall_ref, sems,
 ):
     copies = [
         pltpu.make_async_copy(source, target, sems.at[i])
         for i, (source, target) in enumerate((
+            (links_hbm.at[pl.ds(6, 2)], links_ref), (clover_hbm, clover_ref), (stencil_hbm, stencil_ref),
             (when_hbm, when_ref), (spin_hbm, spin_ref), (wall_hbm, wall_ref),
-            (links_hbm.at[pl.ds(6, 2)], links_ref), (clover_hbm, clover_ref), (stencil_hbm, stencil_ref),
         ))
     ]
     for copy in copies:
         copy.start()
-    for copy in copies[:5]:
+    for copy in copies:
         copy.wait()
     lanes = lane_index(HALF)
     y = lanes % NY
@@ -235,7 +236,6 @@
         return carry
 
     lax.fori_loop(0, 4, rhs, 0)
-    copies[5].wait()
 
     def spread(index, carry):
         start = pl.multiple_of(24 * index, 24)
@@ -246,7 +246,7 @@
         operator_ref[pl.ds(start, 24)] = block.reshape((24, HALF, LANES))
         return carry
 
-    lax.fori_loop(0, 18, spread, 0)
+    lax.fori_loop(0, 18, spread, 0, unroll=3)
 
 
 def centre(wide, wall_time, spin_index, wall, links, clover, stencil):
@@ -261,27 +261,23 @@
         in_specs=[vm] + [hbm] * 6,
         out_specs=(vm, vm),
         scratch_shapes=[
+            pltpu.VMEM((2, 2, 3, 3, ROWS, LANES), BF16),
+            pltpu.VMEM((2, 2, 6, 6, ROWS, LANES), BF16),
+            pltpu.VMEM((9 * 2 * 24, HALF, 24), F32),
             pltpu.SMEM((4,), jnp.int32),
             pltpu.SMEM((4,), jnp.int32),
             pltpu.SMEM((3, 2, 4), F32),
-            pltpu.VMEM((2, 2, 3, 3, ROWS, LANES), BF16),
-            pltpu.VMEM((2, 2, 6, 6, ROWS, LANES), BF16),
-            pltpu.VMEM((9 * 2 * 24, HALF, 24), F32),
             pltpu.SemaphoreType.DMA((6,)),
         ],
-        compiler_params=vmem_params(24),
-        cost_estimate=pl.CostEstimate(flops=40_000_000, bytes_accessed=6_000_000, transcendentals=0),
+        compiler_params=vmem_params(54),
+        cost_estimate=pl.CostEstimate(flops=40_000_000, bytes_accessed=20_000_000, transcendentals=0),
     )(wide, wall_time, spin_index, wall, links, clover, stencil)
 
 
 def fine_kernel(
-    wide_ref, partial_ref, ta_ref, tb_ref, za_ref, zb_ref, xa_ref, xb_ref, links_hbm, near_hbm,
-    out_ref, links_ref, near_ref, tedge, zedge, xedge, residual, rows_ref, sems,
+    wide_ref, partial_ref, tb_ref, zb_ref, xb_ref, ta_ref, za_ref, xa_ref, links_ref, near_ref,
+    out_ref, tedge, zedge, xedge, residual, rows_ref,
 ):
-    links_copy = pltpu.make_async_copy(links_hbm.at[pl.ds(0, 6)], links_ref, sems.at[0])
-    near_copy = pltpu.make_async_copy(near_hbm, near_ref, sems.at[1])
-    links_copy.start()
-    near_copy.start()
     even = [is_even(axis) for axis in ("ta", "gz", "xy")]
     slabs = ((ta_ref, tb_ref), (za_ref, zb_ref), (xa_ref, xb_ref))
     for direction in range(3):
@@ -307,7 +303,6 @@
                             zedge[side, slot] = value
                         else:
                             xedge[side, slot] = value
-    links_copy.wait()
     lanes = lane_index(HALF)
     sub = row_index(HALF)
     upper = sub >= 4
@@ -375,7 +370,6 @@
 
     for part in range(2):
         rows_ref[part] = jnp.zeros((LANES, LANES), F32)
-    near_copy.wait()
 
     def vector(v, carry):
         for chirality in range(2):
@@ -413,24 +407,21 @@
 
 def fine(wide, partial, halos, links, near):
     vm = pl.BlockSpec(memory_space=pltpu.VMEM)
-    hbm = pl.BlockSpec(memory_space=pltpu.HBM)
     return pl.pallas_call(
         fine_kernel,
         out_shape=jax.ShapeDtypeStruct((2, HALF, LANES), F32),
-        in_specs=[vm] * 8 + [hbm] * 2,
+        in_specs=[vm] * 10,
         out_specs=vm,
         scratch_shapes=[
-            pltpu.VMEM((6, 2, 3, 3, ROWS, LANES), BF16),
-            pltpu.VMEM((12, 2, 12, ROWS, LANES), BF16),
             pltpu.VMEM((2, 12, 4, HALF, LANES), F32),
             pltpu.VMEM((2, 12, ROWS, LANES), F32),
             pltpu.VMEM((2, 12, ROWS, LANES), F32),
             pltpu.VMEM((4, 24, ROWS, LANES), F32),
             pltpu.VMEM((2, LANES, LANES), F32),
-            pltpu.SemaphoreType.DMA((2,)),
         ],
         compiler_params=vmem_params(24),
-    )(wide, partial, *halos, links, near)
+        cost_estimate=pl.CostEstimate(flops=40_000_000, bytes_accessed=20_000_000, transcendentals=0),
+    )(wide, partial, *[halos[i] for i in (1, 3, 5, 0, 2, 4)], links, near)
 
 
 def merge(low, high, width, inside):
@@ -487,9 +478,9 @@
     return neighbours
 
 
-def coarse_kernel(e_ref, tp, tm, zp, zm, xp, xm, r_ref, operator_ref, out_ref):
+def coarse_kernel(e_ref, xa, za, ta, xb, zb, tb, r_ref, operator_ref, out_ref):
     estimate = (e_ref[0], e_ref[1])
-    out = coarse_step(estimate, coarse_neighbours(estimate, (tp, tm, zp, zm, xp, xm)), r_ref, operator_ref)
+    out = coarse_step(estimate, coarse_neighbours(estimate, (ta, tb, za, zb, xa, xb)), r_ref, operator_ref)
     out_ref[0] = out[0]
     out_ref[1] = out[1]
 
@@ -502,12 +493,12 @@
         in_specs=[vm] * 9,
         out_specs=vm,
         compiler_params=vmem_params(16),
-    )(estimate, *halos, restricted, operator)
-
-
-def last_kernel(e_ref, tp, tm, zp, zm, xp, xm, r_ref, operator_ref, psi_ref, near_ref, out_ref, wide):
+    )(estimate, *[halos[i] for i in (4, 2, 0, 5, 3, 1)], restricted, operator)
+
+
+def last_kernel(e_ref, xa, za, ta, xb, zb, tb, r_ref, operator_ref, psi_ref, near_ref, out_hbm, out_ref, wide, sems):
     estimate = (e_ref[0], e_ref[1])
-    final = coarse_step(estimate, coarse_neighbours(estimate, (tp, tm, zp, zm, xp, xm)), r_ref, operator_ref)
+    final = coarse_step(estimate, coarse_neighbours(estimate, (ta, tb, za, zb, xa, xb)), r_ref, operator_ref)
     member = ((lane_index(HALF) % NY) // BLOCK == row_index(HALF)).astype(F32)
     for part in range(2):
         wide[part] = lax.dot_general(
@@ -527,11 +518,16 @@
                 nre, nim = near[v]
                 re = re + (nre * ere - nim * eim)
                 im = im + (nre * eim + nim * ere)
-            out_ref[0, r, c] = re
-            out_ref[1, r, c] = im
+            out_ref[c, 0, r] = re
+            out_ref[c, 1, r] = im
+        for part in range(2):
+            pltpu.make_async_copy(out_ref.at[c, part], out_hbm.at[part, :, c], sems.at[c, part]).start()
         return carry
 
     lax.fori_loop(0, 12, component, 0)
+    for c in range(12):
+        for part in range(2):
+            pltpu.make_async_copy(out_ref.at[c, part], out_hbm.at[part, :, c], sems.at[c, part]).wait()
 
 
 def last(estimate, halos, restricted, operator, psi, near):
@@ -540,17 +536,21 @@
         last_kernel,
         out_shape=jax.ShapeDtypeStruct((2, 4, 12, ROWS, LANES), F32),
         in_specs=[vm] * 11,
-        out_specs=vm,
-        scratch_shapes=[pltpu.VMEM((2, LANES, LANES), F32)],
+        out_specs=pl.BlockSpec(memory_space=pltpu.HBM),
+        scratch_shapes=[
+            pltpu.VMEM((12, 2, 4, ROWS, LANES), F32),
+            pltpu.VMEM((2, LANES, LANES), F32),
+            pltpu.SemaphoreType.DMA((12, 2)),
+        ],
         compiler_params=vmem_params(24),
-    )(estimate, *halos, restricted, operator, psi, near)
+    )(estimate, *[halos[i] for i in (4, 2, 0, 5, 3, 1)], restricted, operator, psi, near)
 
 
 def exchange(values):
-    return [
-        swap(value, axis, which % 2)
-        for which, (value, axis) in enumerate(zip(values, ("ta", "ta", "gz", "gz", "xy", "xy")))
-    ]
+    halos = [None] * 6
+    for which in (4, 2, 0, 5, 3, 1):
+        halos[which] = swap(values[which], ("ta", "gz", "xy")[which // 2], which % 2)
+    return halos
 
 
 def local(

time: 75.3 us -> 67 us (0.89); the launches traced: 75 us -> 65.7 us
  waiting for transfers between devices: 17 us -> 13.1 us
  local copies, waits for them, and re-layouts: 6.6 us -> 3.01 us
  starting transfers between devices: 35.7 us -> 32.4 us
  Pallas kernels: 15.5 us -> 17.1 us
    ppermute x30, waiting for transfers between devices: 17 us -> 13.1 us  [swap(): return lax.ppermute(value, axis, pairs)]
    unnamed x18 -> x14, local copies, waits for them, and re-layouts: 6.6 us -> 3.01 us
    ppermute x30, starting transfers between devices: 35.7 us -> 32.4 us  [swap(): return lax.ppermute(value, axis, pairs)]
    pallas_call x1, Pallas kernels: 5.16 us -> 7.37 us  [centre(): pl.pallas_call(centre_kernel, out_shape=(jax.ShapeDtypeStruct((4, 24, ROW...]
  transfers between devices with their start and end apart: 30 -> 30, of which waited for: 11 -> 12; matrix products, arithmetic and copies ran while one was open for 0% -> 0% of each run, Pallas kernels for 7% -> 11%
where the time goes in v3:
time: 67 us; the launch traced here: 65.7 us
  starting transfers between devices  32.4 us (48%)
  Pallas kernels  17.1 us (26%)
  waiting for transfers between devices  13.1 us (20%)
  local copies, waits for them, and re-layouts  3.01 us (4%)
    ppermute x30, starting transfers between devices, swap(): return lax.ppermute(value, axis, pairs)  32.4 us
    ppermute x30, waiting for transfers between devices, swap(): return lax.ppermute(value, axis, pairs)  13.1 us
    pallas_call x1, Pallas kernels, centre(): pl.pallas_call(centre_kernel, out_shape=(jax.ShapeDtypeStruct((4, 24, ROW...  7.37 us
    pallas_call x1, Pallas kernels, fine(): pl.pallas_call(fine_kernel, out_shape=jax.ShapeDtypeStruct((2, HALF, LANE...  3.53 us
    pallas_call x1, Pallas kernels, last(): pl.pallas_call(last_kernel, out_shape=jax.ShapeDtypeStruct((2, 4, 12, ROW...  3.37 us
    unnamed x14, local copies, waits for them, and re-layouts  3.01 us
    pallas_call x3, Pallas kernels, coarse(): pl.pallas_call(coarse_kernel, out_shape=jax.ShapeDtypeStruct((2, HALF, LA...  2.03 us
  transfers between devices with their start and end apart: 30, of which 12 were waited for; matrix products, arithmetic and copies ran while one was open for 0% of the time, Pallas kernels for 11%

profile of v3, /device:TPU:0, one launch (start us, length us, event | category | flops | bytes accessed | tf_op | source)
XLA Modules:
  0.0 65.7 jit_solution(15030606030496287919)
XLA Ops:
  0.0 1.0 %copy-done.6 = bf16[2,4,12,4,4,128]{5,4,3,2,1,0:T(4,128)(2,1)S(1)} copy-done((bf16[2,4,12,4,4,128]{5,4,3,2,1,0:T(4,128)(2,1)S(1)}, bf16[2,4,12,4,4,128]{5,4,3,2,1,0:T(4,128)(2,1)}, u32[]{:S(2)}) %copy-start.6) | copy-done | bytes 393240
  2.7 5.1 %collective-permute-start = (bf16[24,16,128]{2,1,0:T(8,128)(2,1)S(1)}, bf16[24,16,128]{2,1,0:T(8,128)(2,1)S(1)}, u32[]{:S(2)}, u32[]{:S(2)}) collective-permute-start(bf16[24,16,128]{2,1,0:T(8,128)(2,1)S(1)} %get-tuple-element.16), channel_id=1, source_target_pairs={{0,112},{16,32},{32,16},{48,64},{64,48},{80,96},{96,80},{112,0},{1... | collective-permute-start | bytes 294920 | tf_op jit(solution)/shard_map/ppermute | solution.py:48
  7.8 2.8 %collective-permute-start.1 = (bf16[24,16,128]{2,1,0:T(8,128)(2,1)S(1)}, bf16[24,16,128]{2,1,0:T(8,128)(2,1)S(1)}, u32[]{:S(2)}, u32[]{:S(2)}) collective-permute-start(bf16[24,16,128]{2,1,0:T(8,128)(2,1)S(1)} %get-tuple-element.17), channel_id=1, source_target_pairs={{0,12},{4,8},{8,4},{12,0},{1,13},{5,9},{9,5},{13,1},{2,14},{6,10},... | collective-permute-start | bytes 294920 | tf_op jit(solution)/shard_map/ppermute | solution.py:48
  10.6 1.8 %collective-permute-start.2 = (bf16[24,16,128]{2,1,0:T(8,128)(2,1)S(1)}, bf16[24,16,128]{2,1,0:T(8,128)(2,1)S(1)}, u32[]{:S(2)}, u32[]{:S(2)}) collective-permute-start(bf16[24,16,128]{2,1,0:T(8,128)(2,1)S(1)} %get-tuple-element.18), channel_id=1, source_target_pairs={{0,3},{1,2},{2,1},{3,0},{4,7},{5,6},{6,5},{7,4},{8,11},{9,10},{10,... | collective-permute-start | bytes 294920 | tf_op jit(solution)/shard_map/ppermute | solution.py:48
  12.6 1.1 %collective-permute-start.5 = (bf16[24,16,128]{2,1,0:T(8,128)(2,1)S(1)}, bf16[24,16,128]{2,1,0:T(8,128)(2,1)S(1)}, u32[]{:S(2)}, u32[]{:S(2)}) collective-permute-start(bf16[24,16,128]{2,1,0:T(8,128)(2,1)S(1)} %get-tuple-element.21), channel_id=1, source_target_pairs={{0,1},{1,0},{2,3},{3,2},{4,5},{5,4},{6,7},{7,6},{8,9},{9,8},{10,11... | collective-permute-start | bytes 294920 | tf_op jit(solution)/shard_map/ppermute | solution.py:48
  13.7 7.4 %shard_map.83 = (f32[4,24,16,128]{3,2,1,0:T(8,128)}, f32[432,8,128]{2,1,0:T(8,128)}) custom-call(f32[2,4,12,16,128]{4,3,2,1,0:T(8,128)} %copy-done.1, s32[4]{0:T(128)} %when_hbm.1, s32[4]{0:T(128)} %spin_hbm.1, f32[3,2,4]{2,1,0:T(2,128)} %bitcast.16, bf16[8,2,3,3,16,128]{5,4,3,2,1,0:T(8,128)(2,1)} %bitcast.11, bf16[2,2,6,6,16,128]{5,4,3,2,1,0:T(8,128)(2,1)} %bitcast.15, ...), custom_call_target="tpu_custom_call" | custom-call | flops 40000000 | bytes 20000000 | tf_op jit(solution)/shard_map/pallas_call | solution.py:255
  21.2 1.1 %copy-done.5 = f32[4,24,16,128]{3,2,1,0:T(8,128)S(1)} copy-done((f32[4,24,16,128]{3,2,1,0:T(8,128)S(1)}, f32[4,24,16,128]{3,2,1,0:T(8,128)}, u32[]{:S(2)}) %copy-start.5) | copy-done | bytes 786456
  22.3 3.5 %shard_map.84.e_ref.r_ref = f32[2,8,128]{2,1,0:T(8,128)S(1)} custom-call(f32[2,4,12,16,128]{4,3,2,1,0:T(8,128)S(1)} %copy-done.2, f32[4,24,16,128]{3,2,1,0:T(8,128)S(1)} %copy-done.5, bf16[24,16,128]{2,1,0:T(8,128)(2,1)S(1)} %collective-permute-done.tb_ref, bf16[24,16,128]{2,1,0:T(8,128)(2,1)S(1)} %collective-permute-done.1.zb_ref, ...), custom_call_target="tpu_custom_call" | custom-call | flops 40000000 | bytes 20000000 | tf_op jit(solution)/shard_map/pallas_call | solution.py:410
  25.8 0.9 %collective-permute-start.11 = (f32[2,8,128]{2,1,0:T(8,128)S(1)}, f32[2,8,128]{2,1,0:T(8,128)S(1)}, u32[]{:S(2)}, u32[]{:S(2)}) collective-permute-start(f32[2,8,128]{2,1,0:T(8,128)S(1)} %shard_map.84.e_ref.r_ref), channel_id=1, source_target_pairs={{0,112},{16,32},{32,16},{48,64},{64,48},{80,96},{96,80},{112,0},{1... | collective-permute-start | bytes 24584 | tf_op jit(solution)/shard_map/ppermute | solution.py:48
  26.7 2.8 %collective-permute-start.10 = (f32[2,8,128]{2,1,0:T(8,128)S(1)}, f32[2,8,128]{2,1,0:T(8,128)S(1)}, u32[]{:S(2)}, u32[]{:S(2)}) collective-permute-start(f32[2,8,128]{2,1,0:T(8,128)S(1)} %shard_map.84.e_ref.r_ref), channel_id=1, source_target_pairs={{0,12},{4,8},{8,4},{12,0},{1,13},{5,9},{9,5},{13,1},{2,14},{6,10},... | collective-permute-start | bytes 24584 | tf_op jit(solution)/shard_map/ppermute | solution.py:48
  29.5 3.0 %collective-permute-start.9 = (f32[2,8,128]{2,1,0:T(8,128)S(1)}, f32[2,8,128]{2,1,0:T(8,128)S(1)}, u32[]{:S(2)}, u32[]{:S(2)}) collective-permute-start(f32[2,8,128]{2,1,0:T(8,128)S(1)} %shard_map.84.e_ref.r_ref), channel_id=1, source_target_pairs={{0,3},{1,2},{2,1},{3,0},{4,7},{5,6},{6,5},{7,4},{8,11},{9,10},{10,... | collective-permute-start | bytes 24584 | tf_op jit(solution)/shard_map/ppermute | solution.py:48
  33.2 0.9 %collective-permute-done.9.xb = f32[2,8,128]{2,1,0:T(8,128)S(1)} collective-permute-done((f32[2,8,128]{2,1,0:T(8,128)S(1)}, f32[2,8,128]{2,1,0:T(8,128)S(1)}, u32[]{:S(2)}, u32[]{:S(2)}) %collective-permute-start.9) | collective-permute-done | bytes 8224 | tf_op jit(solution)/shard_map/ppermute | solution.py:48
  34.0 2.1 %collective-permute-done.8.ta = f32[2,8,128]{2,1,0:T(8,128)S(1)} collective-permute-done((f32[2,8,128]{2,1,0:T(8,128)S(1)}, f32[2,8,128]{2,1,0:T(8,128)S(1)}, u32[]{:S(2)}, u32[]{:S(2)}) %collective-permute-start.8) | collective-permute-done | bytes 8224 | tf_op jit(solution)/shard_map/ppermute | solution.py:48
  36.9 1.6 %collective-permute-start.16 = (f32[2,8,128]{2,1,0:T(8,128)S(1)}, f32[2,8,128]{2,1,0:T(8,128)S(1)}, u32[]{:S(2)}, u32[]{:S(2)}) collective-permute-start(f32[2,8,128]{2,1,0:T(8,128)S(1)} %shard_map.85.e_ref), channel_id=1, source_target_pairs={{0,12},{4,8},{8,4},{12,0},{1,13},{5,9},{9,5},{13,1},{2,14},{6,10},... | collective-permute-start | bytes 24584 | tf_op jit(solution)/shard_map/ppermute | solution.py:48
  38.5 1.5 %collective-permute-start.15 = (f32[2,8,128]{2,1,0:T(8,128)S(1)}, f32[2,8,128]{2,1,0:T(8,128)S(1)}, u32[]{:S(2)}, u32[]{:S(2)}) collective-permute-start(f32[2,8,128]{2,1,0:T(8,128)S(1)} %shard_map.85.e_ref), channel_id=1, source_target_pairs={{0,3},{1,2},{2,1},{3,0},{4,7},{5,6},{6,5},{7,4},{8,11},{9,10},{10,... | collective-permute-start | bytes 24584 | tf_op jit(solution)/shard_map/ppermute | solution.py:48
  40.4 2.2 %collective-permute-done.17.tb = f32[2,8,128]{2,1,0:T(8,128)S(1)} collective-permute-done((f32[2,8,128]{2,1,0:T(8,128)S(1)}, f32[2,8,128]{2,1,0:T(8,128)S(1)}, u32[]{:S(2)}, u32[]{:S(2)}) %collective-permute-start.17) | collective-permute-done | bytes 8224 | tf_op jit(solution)/shard_map/ppermute | solution.py:48
  44.5 2.1 %collective-permute-start.23 = (f32[2,8,128]{2,1,0:T(8,128)S(1)}, f32[2,8,128]{2,1,0:T(8,128)S(1)}, u32[]{:S(2)}, u32[]{:S(2)}) collective-permute-start(f32[2,8,128]{2,1,0:T(8,128)S(1)} %shard_map.86.e_ref), channel_id=1, source_target_pairs={{0,112},{16,32},{32,16},{48,64},{64,48},{80,96},{96,80},{112,0},{1... | collective-permute-start | bytes 24584 | tf_op jit(solution)/shard_map/ppermute | solution.py:48
  46.6 2.9 %collective-permute-start.22 = (f32[2,8,128]{2,1,0:T(8,128)S(1)}, f32[2,8,128]{2,1,0:T(8,128)S(1)}, u32[]{:S(2)}, u32[]{:S(2)}) collective-permute-start(f32[2,8,128]{2,1,0:T(8,128)S(1)} %shard_map.86.e_ref), channel_id=1, source_target_pairs={{0,12},{4,8},{8,4},{12,0},{1,13},{5,9},{9,5},{13,1},{2,14},{6,10},... | collective-permute-start | bytes 24584 | tf_op jit(solution)/shard_map/ppermute | solution.py:48
  49.5 1.2 %collective-permute-start.21 = (f32[2,8,128]{2,1,0:T(8,128)S(1)}, f32[2,8,128]{2,1,0:T(8,128)S(1)}, u32[]{:S(2)}, u32[]{:S(2)}) collective-permute-start(f32[2,8,128]{2,1,0:T(8,128)S(1)} %shard_map.86.e_ref), channel_id=1, source_target_pairs={{0,3},{1,2},{2,1},{3,0},{4,7},{5,6},{6,5},{7,4},{8,11},{9,10},{10,... | collective-permute-start | bytes 24584 | tf_op jit(solution)/shard_map/ppermute | solution.py:48
  51.4 2.7 %collective-permute-done.21.xb = f32[2,8,128]{2,1,0:T(8,128)S(1)} collective-permute-done((f32[2,8,128]{2,1,0:T(8,128)S(1)}, f32[2,8,128]{2,1,0:T(8,128)S(1)}, u32[]{:S(2)}, u32[]{:S(2)}) %collective-permute-start.21) | collective-permute-done | bytes 8224 | tf_op jit(solution)/shard_map/ppermute | solution.py:48
  55.1 1.5 %collective-permute-start.29 = (f32[2,8,128]{2,1,0:T(8,128)S(1)}, f32[2,8,128]{2,1,0:T(8,128)S(1)}, u32[]{:S(2)}, u32[]{:S(2)}) collective-permute-start(f32[2,8,128]{2,1,0:T(8,128)S(1)} %shard_map.87.e_ref), channel_id=1, source_target_pairs={{0,112},{16,32},{32,16},{48,64},{64,48},{80,96},{96,80},{112,0},{1... | collective-permute-start | bytes 24584 | tf_op jit(solution)/shard_map/ppermute | solution.py:48
  57.1 1.5 %collective-permute-start.27 = (f32[2,8,128]{2,1,0:T(8,128)S(1)}, f32[2,8,128]{2,1,0:T(8,128)S(1)}, u32[]{:S(2)}, u32[]{:S(2)}) collective-permute-start(f32[2,8,128]{2,1,0:T(8,128)S(1)} %shard_map.87.e_ref), channel_id=1, source_target_pairs={{0,3},{1,2},{2,1},{3,0},{4,7},{5,6},{6,5},{7,4},{8,11},{9,10},{10,... | collective-permute-start | bytes 24584 | tf_op jit(solution)/shard_map/ppermute | solution.py:48
  58.7 2.2 %collective-permute-done.29.tb = f32[2,8,128]{2,1,0:T(8,128)S(1)} collective-permute-done((f32[2,8,128]{2,1,0:T(8,128)S(1)}, f32[2,8,128]{2,1,0:T(8,128)S(1)}, u32[]{:S(2)}, u32[]{:S(2)}) %collective-permute-start.29) | collective-permute-done | bytes 8224 | tf_op jit(solution)/shard_map/ppermute | solution.py:48
  62.4 3.4 %shard_map.88 = f32[2,4,12,16,128]{4,3,2,1,0:T(8,128)} custom-call(f32[2,8,128]{2,1,0:T(8,128)S(1)} %shard_map.87.e_ref, f32[2,8,128]{2,1,0:T(8,128)S(1)} %collective-permute-done.24.xa, f32[2,8,128]{2,1,0:T(8,128)S(1)} %collective-permute-done.25.za, f32[2,8,128]{2,1,0:T(8,128)S(1)} %collective-permute-done.26.ta, ...), custom_call_target="tpu_custom_call" | custom-call | tf_op jit(solution)/shard_map/pallas_call | solution.py:535
  (57 shorter events, 9.3 us)
Async XLA Ops:
  2.7 9.9 %collective-permute-start = (bf16[24,16,128]{2,1,0:T(8,128)(2,1)S(1)}, bf16[24,16,128]{2,1,0:T(8,128)(2,1)S(1)}, u32[]{:S(2)}, u32[]{:S(2)}) collective-permute-start(bf16[24,16,128]{2,1,0:T(8,128)(2,1)S(1)} %get-tuple-element.16), channel_id=1, source_target_pairs={{0,112},{16,32},{32,16},{48,64},{64,48},{80,96},{96,80},{112,0},{1... | collective-permute-start | bytes 294920 | tf_op jit(solution)/shard_map/ppermute | solution.py:48
  7.8 13.3 %collective-permute-start.1 = (bf16[24,16,128]{2,1,0:T(8,128)(2,1)S(1)}, bf16[24,16,128]{2,1,0:T(8,128)(2,1)S(1)}, u32[]{:S(2)}, u32[]{:S(2)}) collective-permute-start(bf16[24,16,128]{2,1,0:T(8,128)(2,1)S(1)} %get-tuple-element.17), channel_id=1, source_target_pairs={{0,12},{4,8},{8,4},{12,0},{1,13},{5,9},{9,5},{13,1},{2,14},{6,10},... | collective-permute-start | bytes 294920 | tf_op jit(solution)/shard_map/ppermute | solution.py:48
  10.6 10.5 %collective-permute-start.2 = (bf16[24,16,128]{2,1,0:T(8,128)(2,1)S(1)}, bf16[24,16,128]{2,1,0:T(8,128)(2,1)S(1)}, u32[]{:S(2)}, u32[]{:S(2)}) collective-permute-start(bf16[24,16,128]{2,1,0:T(8,128)(2,1)S(1)} %get-tuple-element.18), channel_id=1, source_target_pairs={{0,3},{1,2},{2,1},{3,0},{4,7},{5,6},{6,5},{7,4},{8,11},{9,10},{10,... | collective-permute-start | bytes 294920 | tf_op jit(solution)/shard_map/ppermute | solution.py:48
  12.3 8.7 %collective-permute-start.3 = (bf16[24,16,128]{2,1,0:T(8,128)(2,1)S(1)}, bf16[24,16,128]{2,1,0:T(8,128)(2,1)S(1)}, u32[]{:S(2)}, u32[]{:S(2)}) collective-permute-start(bf16[24,16,128]{2,1,0:T(8,128)(2,1)S(1)} %get-tuple-element.19), channel_id=1, source_target_pairs={{0,16},{16,0},{32,48},{48,32},{64,80},{80,64},{96,112},{112,96},{1... | collective-permute-start | bytes 294920 | tf_op jit(solution)/shard_map/ppermute | solution.py:48
  12.3 8.7 %collective-permute-start.4 = (bf16[24,16,128]{2,1,0:T(8,128)(2,1)S(1)}, bf16[24,16,128]{2,1,0:T(8,128)(2,1)S(1)}, u32[]{:S(2)}, u32[]{:S(2)}) collective-permute-start(bf16[24,16,128]{2,1,0:T(8,128)(2,1)S(1)} %get-tuple-element.20), channel_id=1, source_target_pairs={{0,4},{4,0},{8,12},{12,8},{1,5},{5,1},{9,13},{13,9},{2,6},{6,2},{1... | collective-permute-start | bytes 294920 | tf_op jit(solution)/shard_map/ppermute | solution.py:48
  12.6 8.5 %collective-permute-start.5 = (bf16[24,16,128]{2,1,0:T(8,128)(2,1)S(1)}, bf16[24,16,128]{2,1,0:T(8,128)(2,1)S(1)}, u32[]{:S(2)}, u32[]{:S(2)}) collective-permute-start(bf16[24,16,128]{2,1,0:T(8,128)(2,1)S(1)} %get-tuple-element.21), channel_id=1, source_target_pairs={{0,1},{1,0},{2,3},{3,2},{4,5},{5,4},{6,7},{7,6},{8,9},{9,8},{10,11... | collective-permute-start | bytes 294920 | tf_op jit(solution)/shard_map/ppermute | solution.py:48
  25.8 6.8 %collective-permute-start.11 = (f32[2,8,128]{2,1,0:T(8,128)S(1)}, f32[2,8,128]{2,1,0:T(8,128)S(1)}, u32[]{:S(2)}, u32[]{:S(2)}) collective-permute-start(f32[2,8,128]{2,1,0:T(8,128)S(1)} %shard_map.84.e_ref.r_ref), channel_id=1, source_target_pairs={{0,112},{16,32},{32,16},{48,64},{64,48},{80,96},{96,80},{112,0},{1... | collective-permute-start | bytes 24584 | tf_op jit(solution)/shard_map/ppermute | solution.py:48
  26.7 6.5 %collective-permute-start.10 = (f32[2,8,128]{2,1,0:T(8,128)S(1)}, f32[2,8,128]{2,1,0:T(8,128)S(1)}, u32[]{:S(2)}, u32[]{:S(2)}) collective-permute-start(f32[2,8,128]{2,1,0:T(8,128)S(1)} %shard_map.84.e_ref.r_ref), channel_id=1, source_target_pairs={{0,12},{4,8},{8,4},{12,0},{1,13},{5,9},{9,5},{13,1},{2,14},{6,10},... | collective-permute-start | bytes 24584 | tf_op jit(solution)/shard_map/ppermute | solution.py:48
  29.5 4.6 %collective-permute-start.9 = (f32[2,8,128]{2,1,0:T(8,128)S(1)}, f32[2,8,128]{2,1,0:T(8,128)S(1)}, u32[]{:S(2)}, u32[]{:S(2)}) collective-permute-start(f32[2,8,128]{2,1,0:T(8,128)S(1)} %shard_map.84.e_ref.r_ref), channel_id=1, source_target_pairs={{0,3},{1,2},{2,1},{3,0},{4,7},{5,6},{6,5},{7,4},{8,11},{9,10},{10,... | collective-permute-start | bytes 24584 | tf_op jit(solution)/shard_map/ppermute | solution.py:48
  32.5 3.7 %collective-permute-start.8 = (f32[2,8,128]{2,1,0:T(8,128)S(1)}, f32[2,8,128]{2,1,0:T(8,128)S(1)}, u32[]{:S(2)}, u32[]{:S(2)}) collective-permute-start(f32[2,8,128]{2,1,0:T(8,128)S(1)} %shard_map.84.e_ref.r_ref), channel_id=1, source_target_pairs={{0,16},{16,0},{32,48},{48,32},{64,80},{80,64},{96,112},{112,96},{1... | collective-permute-start | bytes 24584 | tf_op jit(solution)/shard_map/ppermute | solution.py:48
  32.5 3.7 %collective-permute-start.7 = (f32[2,8,128]{2,1,0:T(8,128)S(1)}, f32[2,8,128]{2,1,0:T(8,128)S(1)}, u32[]{:S(2)}, u32[]{:S(2)}) collective-permute-start(f32[2,8,128]{2,1,0:T(8,128)S(1)} %shard_map.84.e_ref.r_ref), channel_id=1, source_target_pairs={{0,4},{4,0},{8,12},{12,8},{1,5},{5,1},{9,13},{13,9},{2,6},{6,2},{1... | collective-permute-start | bytes 24584 | tf_op jit(solution)/shard_map/ppermute | solution.py:48
  36.8 5.8 %collective-permute-start.17 = (f32[2,8,128]{2,1,0:T(8,128)S(1)}, f32[2,8,128]{2,1,0:T(8,128)S(1)}, u32[]{:S(2)}, u32[]{:S(2)}) collective-permute-start(f32[2,8,128]{2,1,0:T(8,128)S(1)} %shard_map.85.e_ref), channel_id=1, source_target_pairs={{0,112},{16,32},{32,16},{48,64},{64,48},{80,96},{96,80},{112,0},{1... | collective-permute-start | bytes 24584 | tf_op jit(solution)/shard_map/ppermute | solution.py:48
  36.9 5.8 %collective-permute-start.16 = (f32[2,8,128]{2,1,0:T(8,128)S(1)}, f32[2,8,128]{2,1,0:T(8,128)S(1)}, u32[]{:S(2)}, u32[]{:S(2)}) collective-permute-start(f32[2,8,128]{2,1,0:T(8,128)S(1)} %shard_map.85.e_ref), channel_id=1, source_target_pairs={{0,12},{4,8},{8,4},{12,0},{1,13},{5,9},{9,5},{13,1},{2,14},{6,10},... | collective-permute-start | bytes 24584 | tf_op jit(solution)/shard_map/ppermute | solution.py:48
  38.5 4.6 %collective-permute-start.15 = (f32[2,8,128]{2,1,0:T(8,128)S(1)}, f32[2,8,128]{2,1,0:T(8,128)S(1)}, u32[]{:S(2)}, u32[]{:S(2)}) collective-permute-start(f32[2,8,128]{2,1,0:T(8,128)S(1)} %shard_map.85.e_ref), channel_id=1, source_target_pairs={{0,3},{1,2},{2,1},{3,0},{4,7},{5,6},{6,5},{7,4},{8,11},{9,10},{10,... | collective-permute-start | bytes 24584 | tf_op jit(solution)/shard_map/ppermute | solution.py:48
  40.0 3.7 %collective-permute-start.14 = (f32[2,8,128]{2,1,0:T(8,128)S(1)}, f32[2,8,128]{2,1,0:T(8,128)S(1)}, u32[]{:S(2)}, u32[]{:S(2)}) collective-permute-start(f32[2,8,128]{2,1,0:T(8,128)S(1)} %shard_map.85.e_ref), channel_id=1, source_target_pairs={{0,16},{16,0},{32,48},{48,32},{64,80},{80,64},{96,112},{112,96},{1... | collective-permute-start | bytes 24584 | tf_op jit(solution)/shard_map/ppermute | solution.py:48
  40.0 3.7 %collective-permute-start.13 = (f32[2,8,128]{2,1,0:T(8,128)S(1)}, f32[2,8,128]{2,1,0:T(8,128)S(1)}, u32[]{:S(2)}, u32[]{:S(2)}) collective-permute-start(f32[2,8,128]{2,1,0:T(8,128)S(1)} %shard_map.85.e_ref), channel_id=1, source_target_pairs={{0,4},{4,0},{8,12},{12,8},{1,5},{5,1},{9,13},{13,9},{2,6},{6,2},{1... | collective-permute-start | bytes 24584 | tf_op jit(solution)/shard_map/ppermute | solution.py:48
  44.5 6.3 %collective-permute-start.23 = (f32[2,8,128]{2,1,0:T(8,128)S(1)}, f32[2,8,128]{2,1,0:T(8,128)S(1)}, u32[]{:S(2)}, u32[]{:S(2)}) collective-permute-start(f32[2,8,128]{2,1,0:T(8,128)S(1)} %shard_map.86.e_ref), channel_id=1, source_target_pairs={{0,112},{16,32},{32,16},{48,64},{64,48},{80,96},{96,80},{112,0},{1... | collective-permute-start | bytes 24584 | tf_op jit(solution)/shard_map/ppermute | solution.py:48
  46.6 4.9 %collective-permute-start.22 = (f32[2,8,128]{2,1,0:T(8,128)S(1)}, f32[2,8,128]{2,1,0:T(8,128)S(1)}, u32[]{:S(2)}, u32[]{:S(2)}) collective-permute-start(f32[2,8,128]{2,1,0:T(8,128)S(1)} %shard_map.86.e_ref), channel_id=1, source_target_pairs={{0,12},{4,8},{8,4},{12,0},{1,13},{5,9},{9,5},{13,1},{2,14},{6,10},... | collective-permute-start | bytes 24584 | tf_op jit(solution)/shard_map/ppermute | solution.py:48
  49.5 4.6 %collective-permute-start.21 = (f32[2,8,128]{2,1,0:T(8,128)S(1)}, f32[2,8,128]{2,1,0:T(8,128)S(1)}, u32[]{:S(2)}, u32[]{:S(2)}) collective-permute-start(f32[2,8,128]{2,1,0:T(8,128)S(1)} %shard_map.86.e_ref), channel_id=1, source_target_pairs={{0,3},{1,2},{2,1},{3,0},{4,7},{5,6},{6,5},{7,4},{8,11},{9,10},{10,... | collective-permute-start | bytes 24584 | tf_op jit(solution)/shard_map/ppermute | solution.py:48
  55.1 5.8 %collective-permute-start.29 = (f32[2,8,128]{2,1,0:T(8,128)S(1)}, f32[2,8,128]{2,1,0:T(8,128)S(1)}, u32[]{:S(2)}, u32[]{:S(2)}) collective-permute-start(f32[2,8,128]{2,1,0:T(8,128)S(1)} %shard_map.87.e_ref), channel_id=1, source_target_pairs={{0,112},{16,32},{32,16},{48,64},{64,48},{80,96},{96,80},{112,0},{1... | collective-permute-start | bytes 24584 | tf_op jit(solution)/shard_map/ppermute | solution.py:48
  56.6 4.9 %collective-permute-start.28 = (f32[2,8,128]{2,1,0:T(8,128)S(1)}, f32[2,8,128]{2,1,0:T(8,128)S(1)}, u32[]{:S(2)}, u32[]{:S(2)}) collective-permute-start(f32[2,8,128]{2,1,0:T(8,128)S(1)} %shard_map.87.e_ref), channel_id=1, source_target_pairs={{0,12},{4,8},{8,4},{12,0},{1,13},{5,9},{9,5},{13,1},{2,14},{6,10},... | collective-permute-start | bytes 24584 | tf_op jit(solution)/shard_map/ppermute | solution.py:48
  57.1 4.6 %collective-permute-start.27 = (f32[2,8,128]{2,1,0:T(8,128)S(1)}, f32[2,8,128]{2,1,0:T(8,128)S(1)}, u32[]{:S(2)}, u32[]{:S(2)}) collective-permute-start(f32[2,8,128]{2,1,0:T(8,128)S(1)} %shard_map.87.e_ref), channel_id=1, source_target_pairs={{0,3},{1,2},{2,1},{3,0},{4,7},{5,6},{6,5},{7,4},{8,11},{9,10},{10,... | collective-permute-start | bytes 24584 | tf_op jit(solution)/shard_map/ppermute | solution.py:48
  58.7 3.7 %collective-permute-start.26 = (f32[2,8,128]{2,1,0:T(8,128)S(1)}, f32[2,8,128]{2,1,0:T(8,128)S(1)}, u32[]{:S(2)}, u32[]{:S(2)}) collective-permute-start(f32[2,8,128]{2,1,0:T(8,128)S(1)} %shard_map.87.e_ref), channel_id=1, source_target_pairs={{0,16},{16,0},{32,48},{48,32},{64,80},{80,64},{96,112},{112,96},{1... | collective-permute-start | bytes 24584 | tf_op jit(solution)/shard_map/ppermute | solution.py:48
  58.7 3.7 %collective-permute-start.25 = (f32[2,8,128]{2,1,0:T(8,128)S(1)}, f32[2,8,128]{2,1,0:T(8,128)S(1)}, u32[]{:S(2)}, u32[]{:S(2)}) collective-permute-start(f32[2,8,128]{2,1,0:T(8,128)S(1)} %shard_map.87.e_ref), channel_id=1, source_target_pairs={{0,4},{4,0},{8,12},{12,8},{1,5},{5,1},{9,13},{13,9},{2,6},{6,2},{1... | collective-permute-start | bytes 24584 | tf_op jit(solution)/shard_map/ppermute | solution.py:48
  (13 other events, 56.4 us)

commit v4 on v3

--- a/solution.py
+++ b/solution.py
@@ -174,23 +174,49 @@
     return link
 
 
+def sideways_kernel(wide_ref, out_ref):
+    y = lane_index(HALF) % NY
+
+    def rhs(r, carry):
+        for half in range(2):
+            low = HALF * half
+
+            def load(part, component):
+                return wide_ref[part, r, component, low : low + HALF, :]
+
+            ahead = mapped(
+                lambda p: jnp.where(y < NY - 1, turn_lanes(p, -1), turn_lanes(p, NY - 1)),
+                projected(3, -1.0, load),
+            )
+            behind = mapped(
+                lambda p: jnp.where(y > 0, turn_lanes(p, 1), turn_lanes(p, 1 - NY)),
+                projected(3, 1.0, load),
+            )
+            for side, field in enumerate((ahead, behind)):
+                for s in range(2):
+                    for colour in range(3):
+                        for part in range(2):
+                            out_ref[side, r, 6 * s + 2 * colour + part, low : low + HALF, :] = field[s][colour][part]
+        return carry
+
+    lax.fori_loop(0, 4, rhs, 0)
+
+
+def sideways(wide):
+    vm = pl.BlockSpec(memory_space=pltpu.VMEM)
+    return pl.pallas_call(
+        sideways_kernel,
+        out_shape=jax.ShapeDtypeStruct((2, 4, 12, ROWS, LANES), F32),
+        in_specs=[vm],
+        out_specs=vm,
+        compiler_params=vmem_params(8),
+        cost_estimate=pl.CostEstimate(flops=40_000_000, bytes_accessed=20_000_000, transcendentals=0),
+    )(wide)
+
+
 def centre_kernel(
-    wide_ref, when_hbm, spin_hbm, wall_hbm, links_hbm, clover_hbm, stencil_hbm, out_ref, operator_ref,
-    links_ref, clover_ref, stencil_ref, when_ref, spin_ref, wall_ref, sems,
+    wide_ref, side_ref, when_ref, spin_ref, wall_ref, links_ref, clover_ref, out_ref,
 ):
-    copies = [
-        pltpu.make_async_copy(source, target, sems.at[i])
-        for i, (source, target) in enumerate((
-            (links_hbm.at[pl.ds(6, 2)], links_ref), (clover_hbm, clover_ref), (stencil_hbm, stencil_ref),
-            (when_hbm, when_ref), (spin_hbm, spin_ref), (wall_hbm, wall_ref),
-        ))
-    ]
-    for copy in copies:
-        copy.start()
-    for copy in copies:
-        copy.wait()
-    lanes = lane_index(HALF)
-    y = lanes % NY
     first_time = lax.axis_index("ta") * BLOCK
 
     def rhs(r, carry):
@@ -203,16 +229,15 @@
                 return wide_ref[part, r, component, low : low + HALF, :]
 
             total = [[[None, None] for _ in range(3)] for _ in range(4)]
-            ahead = mapped(
-                lambda p: jnp.where(y < NY - 1, turn_lanes(p, -1), turn_lanes(p, NY - 1)),
-                projected(3, -1.0, load),
-            )
-            hop(3, -1.0, ahead, link_loader(links_ref, 0, low), total)
-            behind = mapped(
-                lambda p: jnp.where(y > 0, turn_lanes(p, 1), turn_lanes(p, 1 - NY)),
-                projected(3, 1.0, load),
-            )
-            hop(3, 1.0, behind, link_loader(links_ref, 1, low), total)
+            for side, sign in enumerate((-1.0, 1.0)):
+                field = [
+                    [
+                        tuple(side_ref[side, r, 6 * s + 2 * colour + part, low : low + HALF, :] for part in range(2))
+                        for colour in range(3)
+                    ]
+                    for s in range(2)
+                ]
+                hop(3, sign, field, link_loader(links_ref, 6 + side, low), total)
             at_wall = first_time + 2 * half + row_index(HALF) // BLOCK == when
             for chirality in range(2):
                 values = [(load(0, 6 * chirality + i), load(1, 6 * chirality + i)) for i in range(6)]
@@ -237,41 +262,46 @@
 
     lax.fori_loop(0, 4, rhs, 0)
 
-    def spread(index, carry):
-        start = pl.multiple_of(24 * index, 24)
-        block = stencil_ref[pl.ds(start, 24)].reshape((24 * HALF, 24))
-        block = jnp.concatenate([block, jnp.zeros((24 * HALF, LANES - 24), F32)], axis=1)
-        block = block + turn_lanes(block, 32)
-        block = block + turn_lanes(block, 64)
-        operator_ref[pl.ds(start, 24)] = block.reshape((24, HALF, LANES))
-        return carry
-
-    lax.fori_loop(0, 18, spread, 0, unroll=3)
-
-
-def centre(wide, wall_time, spin_index, wall, links, clover, stencil):
+
+def centre(wide, side, wall_time, spin_index, wall, links, clover):
     vm = pl.BlockSpec(memory_space=pltpu.VMEM)
-    hbm = pl.BlockSpec(memory_space=pltpu.HBM)
+    sm = pl.BlockSpec(memory_space=pltpu.SMEM)
     return pl.pallas_call(
         centre_kernel,
-        out_shape=(
-            jax.ShapeDtypeStruct((4, 24, ROWS, LANES), F32),
-            jax.ShapeDtypeStruct((9 * 2 * 24, HALF, LANES), F32),
-        ),
-        in_specs=[vm] + [hbm] * 6,
-        out_specs=(vm, vm),
-        scratch_shapes=[
-            pltpu.VMEM((2, 2, 3, 3, ROWS, LANES), BF16),
-            pltpu.VMEM((2, 2, 6, 6, ROWS, LANES), BF16),
-            pltpu.VMEM((9 * 2 * 24, HALF, 24), F32),
-            pltpu.SMEM((4,), jnp.int32),
-            pltpu.SMEM((4,), jnp.int32),
-            pltpu.SMEM((3, 2, 4), F32),
-            pltpu.SemaphoreType.DMA((6,)),
-        ],
-        compiler_params=vmem_params(54),
+        out_shape=jax.ShapeDtypeStruct((4, 24, ROWS, LANES), F32),
+        in_specs=[vm] * 2 + [sm] * 3 + [vm] * 2,
+        out_specs=vm,
+        compiler_params=vmem_params(16),
         cost_estimate=pl.CostEstimate(flops=40_000_000, bytes_accessed=20_000_000, transcendentals=0),
-    )(wide, wall_time, spin_index, wall, links, clover, stencil)
+    )(wide, side, wall_time, spin_index, wall, links, clover)
+
+
+def spread_kernel(stencil_ref, operator_ref):
+    def body(k, carry):
+        parts = []
+        for part in range(2):
+            start = pl.multiple_of(48 * k + 24 * part, 24)
+            block = stencil_ref[pl.ds(start, 24)].reshape((24 * HALF, 24))
+            block = jnp.concatenate([block, jnp.zeros((24 * HALF, LANES - 24), F32)], axis=1)
+            block = block + turn_lanes(block, 32)
+            parts.append(block + turn_lanes(block, 64))
+        operator_ref[k, 0] = parts[0].reshape((24, HALF, LANES))
+        operator_ref[k, 1] = parts[1].reshape((24, HALF, LANES))
+        operator_ref[k, 2] = (parts[0] + parts[1]).reshape((24, HALF, LANES))
+        return carry
+
+    lax.fori_loop(0, 9, body, 0)
+
+
+def spread(stencil):
+    vm = pl.BlockSpec(memory_space=pltpu.VMEM)
+    return pl.pallas_call(
+        spread_kernel,
+        out_shape=jax.ShapeDtypeStruct((9, 3, 24, HALF, LANES), F32),
+        in_specs=[vm],
+        out_specs=vm,
+        compiler_params=vmem_params(8),
+    )(stencil)
 
 
 def fine_kernel(
@@ -359,11 +389,12 @@
                 hop(2, sign, field, link_loader(links_ref, 4 + side, low), total)
             for s in range(4):
                 for colour in range(3):
-                    for part in range(2):
-                        position = 12 * part + 3 * s + colour
-                        residual[r, position, low : low + HALF, :] = (
-                            partial_ref[r, position, low : low + HALF, :] + 0.5 * total[s][colour][part]
-                        )
+                    position = 3 * s + colour
+                    re = partial_ref[r, position, low : low + HALF, :] + 0.5 * total[s][colour][0]
+                    im = partial_ref[r, 12 + position, low : low + HALF, :] + 0.5 * total[s][colour][1]
+                    residual[r, position, low : low + HALF, :] = re
+                    residual[r, 12 + position, low : low + HALF, :] = im - re
+                    residual[r, 24 + position, low : low + HALF, :] = re + im
         return carry
 
     lax.fori_loop(0, 4, rhs, 0)
@@ -373,7 +404,7 @@
 
     def vector(v, carry):
         for chirality in range(2):
-            acc = [[None, None] for _ in range(4)]
+            acc = [[None] * 3 for _ in range(4)]
             for c in range(6):
                 position = 6 * chirality + c
                 nre16 = near_ref[v, 0, position].astype(F32)
@@ -382,17 +413,15 @@
                     low = HALF * half
                     nre = nre16[low : low + HALF]
                     nim = nim16[low : low + HALF]
+                    factors = (nre - nim, nre, nim)
                     for r in range(4):
-                        rre = residual[r, position, low : low + HALF, :]
-                        rim = residual[r, 12 + position, low : low + HALF, :]
-                        tre = nre * rre + nim * rim
-                        tim = nre * rim - nim * rre
-                        acc[r][0] = tre if acc[r][0] is None else acc[r][0] + tre
-                        acc[r][1] = tim if acc[r][1] is None else acc[r][1] + tim
+                        for form in range(3):
+                            term = factors[form] * residual[r, 12 * form + position, low : low + HALF, :]
+                            acc[r][form] = term if acc[r][form] is None else acc[r][form] + term
             for r in range(4):
-                for part in range(2):
+                for part, value in enumerate((acc[r][0] + acc[r][2], acc[r][0] + acc[r][1])):
                     rows_ref[part, pl.ds(r * 32 + chirality * 12 + v, 1), :] = jnp.sum(
-                        acc[r][part], axis=0, keepdims=True
+                        value, axis=0, keepdims=True
                     )
         return carry
 
@@ -416,7 +445,7 @@
             pltpu.VMEM((2, 12, 4, HALF, LANES), F32),
             pltpu.VMEM((2, 12, ROWS, LANES), F32),
             pltpu.VMEM((2, 12, ROWS, LANES), F32),
-            pltpu.VMEM((4, 24, ROWS, LANES), F32),
+            pltpu.VMEM((4, 36, ROWS, LANES), F32),
             pltpu.VMEM((2, LANES, LANES), F32),
         ],
         compiler_params=vmem_params(24),
@@ -433,23 +462,21 @@
 
 
 def coarse_step(estimate, neighbours, restricted_ref, operator_ref):
-    members = [estimate] + neighbours
+    members = [(re, im - re, re + im) for re, im in [estimate] + neighbours]
     lanes = lane_index(HALF)
     out = []
     sums = [[None] * 24, [None] * 24]
     for i in range(24):
-        re = None
-        im = None
+        acc = [None] * 3
         for k in range(9):
-            cre = operator_ref[(k * 2) * 24 + i]
-            cim = operator_ref[(k * 2 + 1) * 24 + i]
-            ere, eim = members[k]
-            tre = cre * ere - cim * eim
-            tim = cre * eim + cim * ere
-            re = tre if re is None else re + tre
-            im = tim if im is None else im + tim
-        sums[0][i] = re
-        sums[1][i] = im
+            ere, difference, total = members[k]
+            terms = (
+                operator_ref[k, 2, i] * ere, operator_ref[k, 0, i] * difference, operator_ref[k, 1, i] * total
+            )
+            for form in range(3):
+                acc[form] = terms[form] if acc[form] is None else acc[form] + terms[form]
+        sums[0][i] = acc[0] - acc[2]
+        sums[1][i] = acc[0] + acc[1]
     for part in range(2):
         values = sums[part] + [None] * 8
         width = 16
@@ -500,26 +527,32 @@
     estimate = (e_ref[0], e_ref[1])
     final = coarse_step(estimate, coarse_neighbours(estimate, (ta, tb, za, zb, xa, xb)), r_ref, operator_ref)
     member = ((lane_index(HALF) % NY) // BLOCK == row_index(HALF)).astype(F32)
-    for part in range(2):
-        wide[part] = lax.dot_general(
+    spreads = [
+        lax.dot_general(
             final[part], member, (((0,), (0,)), ((), ())),
             precision=lax.Precision.HIGHEST, preferred_element_type=F32,
         )
+        for part in range(2)
+    ]
+    wide[0] = spreads[0]
+    wide[1] = spreads[1] - spreads[0]
+    wide[2] = spreads[0] + spreads[1]
 
     def component(c, carry):
         base = (c // 6) * 12
-        near = [(near_ref[v, 0, c].astype(F32), near_ref[v, 1, c].astype(F32)) for v in range(12)]
+        near = []
+        for v in range(12):
+            nre = near_ref[v, 0, c].astype(F32)
+            nim = near_ref[v, 1, c].astype(F32)
+            near.append((nre + nim, nre, nim))
         for r in range(4):
-            re = psi_ref[0, r, c]
-            im = psi_ref[1, r, c]
+            acc = [None] * 3
             for v in range(12):
-                ere = wide[0, pl.ds(r * 32 + base + v, 1), :]
-                eim = wide[1, pl.ds(r * 32 + base + v, 1), :]
-                nre, nim = near[v]
-                re = re + (nre * ere - nim * eim)
-                im = im + (nre * eim + nim * ere)
-            out_ref[c, 0, r] = re
-            out_ref[c, 1, r] = im
+                for form in range(3):
+                    term = near[v][form] * wide[form, pl.ds(r * 32 + base + v, 1), :]
+                    acc[form] = term if acc[form] is None else acc[form] + term
+            out_ref[c, 0, r] = psi_ref[0, r, c] + (acc[0] - acc[2])
+            out_ref[c, 1, r] = psi_ref[1, r, c] + (acc[0] + acc[1])
         for part in range(2):
             pltpu.make_async_copy(out_ref.at[c, part], out_hbm.at[part, :, c], sems.at[c, part]).start()
         return carry
@@ -539,7 +572,7 @@
         out_specs=pl.BlockSpec(memory_space=pltpu.HBM),
         scratch_shapes=[
             pltpu.VMEM((12, 2, 4, ROWS, LANES), F32),
-            pltpu.VMEM((2, LANES, LANES), F32),
+            pltpu.VMEM((3, LANES, LANES), F32),
             pltpu.SemaphoreType.DMA((12, 2)),
         ],
         compiler_params=vmem_params(24),
@@ -564,7 +597,8 @@
     wall = jnp.transpose(wall_colour, (2, 0, 1))
     *slabs, wide = pack(psi)
     halos = exchange(slabs)
-    partial, operator = centre(wide, wall_time, spin_index, wall, links, clover, stencil)
+    partial = centre(wide, sideways(wide), wall_time, spin_index, wall, links, clover)
+    operator = spread(stencil)
     restricted = fine(wide, partial, halos, links, near)
     estimate = restricted
     for step in range(ITERS - 1):

time: 67 us -> 60.8 us (0.907)
  Pallas kernels: 17.1 us -> 13.3 us
  local copies, waits for them, and re-layouts: 3.01 us -> 1.12 us
    pallas_call x1 -> x3, Pallas kernels: 7.37 us -> 4.34 us  [the longest x1 1.95 us: centre(): pl.pallas_call(centre_kernel, out_shape=jax.ShapeDtypeStruct((4, 24, ROWS...]
    unnamed x14 -> x16, local copies, waits for them, and re-layouts: 3.01 us -> 1.12 us
  transfers between devices with their start and end apart: 30 -> 30, of which waited for: 12 -> 15; matrix products, arithmetic and copies ran while one was open for 0% -> 0% of each run, Pallas kernels for 11% -> 7%
where the time goes in v4:
time: 60.8 us; the launch traced here: 59.7 us
  starting transfers between devices  32.1 us (53%)
  Pallas kernels  13.3 us (22%)
  waiting for transfers between devices  13.1 us (22%)
  local copies, waits for them, and re-layouts  1.12 us (2%)
    ppermute x30, starting transfers between devices, swap(): return lax.ppermute(value, axis, pairs)  32.1 us
    ppermute x30, waiting for transfers between devices, swap(): return lax.ppermute(value, axis, pairs)  13.1 us
    pallas_call x1, Pallas kernels, fine(): pl.pallas_call(fine_kernel, out_shape=jax.ShapeDtypeStruct((2, HALF, LANE...  3.33 us
    pallas_call x1, Pallas kernels, last(): pl.pallas_call(last_kernel, out_shape=jax.ShapeDtypeStruct((2, 4, 12, ROW...  3.11 us
    pallas_call x1, Pallas kernels, centre(): pl.pallas_call(centre_kernel, out_shape=jax.ShapeDtypeStruct((4, 24, ROWS...  1.95 us
    pallas_call x1, Pallas kernels, spread(): pl.pallas_call(spread_kernel, out_shape=jax.ShapeDtypeStruct((9, 3, 24, H...  1.71 us
    pallas_call x3, Pallas kernels, coarse(): pl.pallas_call(coarse_kernel, out_shape=jax.ShapeDtypeStruct((2, HALF, LA...  1.7 us
  transfers between devices with their start and end apart: 30, of which 15 were waited for; matrix products, arithmetic and copies ran while one was open for 0% of the time, Pallas kernels for 7%

profile of v4, /device:TPU:0, one launch (start us, length us, event | category | flops | bytes accessed | tf_op | source)
XLA Modules:
  0.0 59.7 jit_solution(5647124454723957683)
XLA Ops:
  0.0 1.1 %copy-done.4 = bf16[2,4,12,4,4,128]{5,4,3,2,1,0:T(4,128)(2,1)S(1)} copy-done((bf16[2,4,12,4,4,128]{5,4,3,2,1,0:T(4,128)(2,1)S(1)}, bf16[2,4,12,4,4,128]{5,4,3,2,1,0:T(4,128)(2,1)}, u32[]{:S(2)}) %copy-start.4) | copy-done | bytes 393240
  1.9 5.2 %collective-permute-start = (bf16[24,16,128]{2,1,0:T(8,128)(2,1)S(1)}, bf16[24,16,128]{2,1,0:T(8,128)(2,1)S(1)}, u32[]{:S(2)}, u32[]{:S(2)}) collective-permute-start(bf16[24,16,128]{2,1,0:T(8,128)(2,1)S(1)} %get-tuple-element.13), channel_id=1, source_target_pairs={{0,112},{16,32},{32,16},{48,64},{64,48},{80,96},{96,80},{112,0},{1... | collective-permute-start | bytes 294920 | tf_op jit(solution)/shard_map/ppermute | solution.py:48
  7.1 2.8 %collective-permute-start.1 = (bf16[24,16,128]{2,1,0:T(8,128)(2,1)S(1)}, bf16[24,16,128]{2,1,0:T(8,128)(2,1)S(1)}, u32[]{:S(2)}, u32[]{:S(2)}) collective-permute-start(bf16[24,16,128]{2,1,0:T(8,128)(2,1)S(1)} %get-tuple-element.14), channel_id=1, source_target_pairs={{0,12},{4,8},{8,4},{12,0},{1,13},{5,9},{9,5},{13,1},{2,14},{6,10},... | collective-permute-start | bytes 294920 | tf_op jit(solution)/shard_map/ppermute | solution.py:48
  9.9 1.8 %collective-permute-start.2 = (bf16[24,16,128]{2,1,0:T(8,128)(2,1)S(1)}, bf16[24,16,128]{2,1,0:T(8,128)(2,1)S(1)}, u32[]{:S(2)}, u32[]{:S(2)}) collective-permute-start(bf16[24,16,128]{2,1,0:T(8,128)(2,1)S(1)} %get-tuple-element.15), channel_id=1, source_target_pairs={{0,3},{1,2},{2,1},{3,0},{4,7},{5,6},{6,5},{7,4},{8,11},{9,10},{10,... | collective-permute-start | bytes 294920 | tf_op jit(solution)/shard_map/ppermute | solution.py:48
  11.9 1.1 %collective-permute-start.5 = (bf16[24,16,128]{2,1,0:T(8,128)(2,1)S(1)}, bf16[24,16,128]{2,1,0:T(8,128)(2,1)S(1)}, u32[]{:S(2)}, u32[]{:S(2)}) collective-permute-start(bf16[24,16,128]{2,1,0:T(8,128)(2,1)S(1)} %get-tuple-element.18), channel_id=1, source_target_pairs={{0,1},{1,0},{2,3},{3,2},{4,5},{5,4},{6,7},{7,6},{8,9},{9,8},{10,11... | collective-permute-start | bytes 294920 | tf_op jit(solution)/shard_map/ppermute | solution.py:48
  13.7 2.0 %shard_map.84.partial_ref = f32[4,24,16,128]{3,2,1,0:T(8,128)S(1)} custom-call(f32[2,4,12,16,128]{4,3,2,1,0:T(8,128)S(1)} %get-tuple-element.12.wide_ref.psi_ref, f32[2,4,12,16,128]{4,3,2,1,0:T(8,128)S(1)} %shard_map.83.side_ref, s32[4]{0:T(128)S(1)} %copy-done.6, s32[4]{0:T(128)S(1)} %copy-done.7, f32[3,2,4]{2,1,0:T(2,128)S(1)} %bitcast.16, ...), custom_call_target="tpu_custom_call" | custom-call | flops 40000000 | bytes 20000000 | tf_op jit(solution)/shard_map/pallas_call | solution.py:269
  17.1 3.3 %shard_map.85.e_ref.r_ref = f32[2,8,128]{2,1,0:T(8,128)S(1)} custom-call(f32[2,4,12,16,128]{4,3,2,1,0:T(8,128)S(1)} %get-tuple-element.12.wide_ref.psi_ref, f32[4,24,16,128]{3,2,1,0:T(8,128)S(1)} %shard_map.84.partial_ref, bf16[24,16,128]{2,1,0:T(8,128)(2,1)S(1)} %collective-permute-done.tb_ref, bf16[24,16,128]{2,1,0:T(8,128)(2,1)S(1)} %collective-permute-done.1.zb_ref, ...), custom_call_target="tpu_custom_call" | custom-call | flops 40000000 | bytes 20000000 | tf_op jit(solution)/shard_map/pallas_call | solution.py:439
  20.6 2.2 %collective-permute-start.10 = (f32[2,8,128]{2,1,0:T(8,128)S(1)}, f32[2,8,128]{2,1,0:T(8,128)S(1)}, u32[]{:S(2)}, u32[]{:S(2)}) collective-permute-start(f32[2,8,128]{2,1,0:T(8,128)S(1)} %shard_map.85.e_ref.r_ref), channel_id=1, source_target_pairs={{0,12},{4,8},{8,4},{12,0},{1,13},{5,9},{9,5},{13,1},{2,14},{6,10},... | collective-permute-start | bytes 24584 | tf_op jit(solution)/shard_map/ppermute | solution.py:48
  22.7 3.0 %collective-permute-start.9 = (f32[2,8,128]{2,1,0:T(8,128)S(1)}, f32[2,8,128]{2,1,0:T(8,128)S(1)}, u32[]{:S(2)}, u32[]{:S(2)}) collective-permute-start(f32[2,8,128]{2,1,0:T(8,128)S(1)} %shard_map.85.e_ref.r_ref), channel_id=1, source_target_pairs={{0,3},{1,2},{2,1},{3,0},{4,7},{5,6},{6,5},{7,4},{8,11},{9,10},{10,... | collective-permute-start | bytes 24584 | tf_op jit(solution)/shard_map/ppermute | solution.py:48
  26.4 1.7 %shard_map.86.operator_ref = f32[9,3,24,8,128]{4,3,2,1,0:T(8,128)S(1)} custom-call(f32[432,8,24]{2,1,0:T(8,128)S(1)} %bitcast.13), custom_call_target="tpu_custom_call" | custom-call | tf_op jit(solution)/shard_map/pallas_call | solution.py:298
  28.2 1.3 %collective-permute-done.8.ta = f32[2,8,128]{2,1,0:T(8,128)S(1)} collective-permute-done((f32[2,8,128]{2,1,0:T(8,128)S(1)}, f32[2,8,128]{2,1,0:T(8,128)S(1)}, u32[]{:S(2)}, u32[]{:S(2)}) %collective-permute-start.8) | collective-permute-done | bytes 8224 | tf_op jit(solution)/shard_map/ppermute | solution.py:48
  30.2 2.8 %collective-permute-start.16 = (f32[2,8,128]{2,1,0:T(8,128)S(1)}, f32[2,8,128]{2,1,0:T(8,128)S(1)}, u32[]{:S(2)}, u32[]{:S(2)}) collective-permute-start(f32[2,8,128]{2,1,0:T(8,128)S(1)} %shard_map.87.e_ref), channel_id=1, source_target_pairs={{0,12},{4,8},{8,4},{12,0},{1,13},{5,9},{9,5},{13,1},{2,14},{6,10},... | collective-permute-start | bytes 24584 | tf_op jit(solution)/shard_map/ppermute | solution.py:48
  33.0 1.6 %collective-permute-start.15 = (f32[2,8,128]{2,1,0:T(8,128)S(1)}, f32[2,8,128]{2,1,0:T(8,128)S(1)}, u32[]{:S(2)}, u32[]{:S(2)}) collective-permute-start(f32[2,8,128]{2,1,0:T(8,128)S(1)} %shard_map.87.e_ref), channel_id=1, source_target_pairs={{0,3},{1,2},{2,1},{3,0},{4,7},{5,6},{6,5},{7,4},{8,11},{9,10},{10,... | collective-permute-start | bytes 24584 | tf_op jit(solution)/shard_map/ppermute | solution.py:48
  34.8 1.0 %collective-permute-done.17.tb = f32[2,8,128]{2,1,0:T(8,128)S(1)} collective-permute-done((f32[2,8,128]{2,1,0:T(8,128)S(1)}, f32[2,8,128]{2,1,0:T(8,128)S(1)}, u32[]{:S(2)}, u32[]{:S(2)}) %collective-permute-start.17) | collective-permute-done | bytes 8224 | tf_op jit(solution)/shard_map/ppermute | solution.py:48
  35.9 1.7 %collective-permute-done.15.xb = f32[2,8,128]{2,1,0:T(8,128)S(1)} collective-permute-done((f32[2,8,128]{2,1,0:T(8,128)S(1)}, f32[2,8,128]{2,1,0:T(8,128)S(1)}, u32[]{:S(2)}, u32[]{:S(2)}) %collective-permute-start.15) | collective-permute-done | bytes 8224 | tf_op jit(solution)/shard_map/ppermute | solution.py:48
  38.8 1.2 %collective-permute-start.23 = (f32[2,8,128]{2,1,0:T(8,128)S(1)}, f32[2,8,128]{2,1,0:T(8,128)S(1)}, u32[]{:S(2)}, u32[]{:S(2)}) collective-permute-start(f32[2,8,128]{2,1,0:T(8,128)S(1)} %shard_map.88.e_ref), channel_id=1, source_target_pairs={{0,112},{16,32},{32,16},{48,64},{64,48},{80,96},{96,80},{112,0},{1... | collective-permute-start | bytes 24584 | tf_op jit(solution)/shard_map/ppermute | solution.py:48
  39.9 2.6 %collective-permute-start.22 = (f32[2,8,128]{2,1,0:T(8,128)S(1)}, f32[2,8,128]{2,1,0:T(8,128)S(1)}, u32[]{:S(2)}, u32[]{:S(2)}) collective-permute-start(f32[2,8,128]{2,1,0:T(8,128)S(1)} %shard_map.88.e_ref), channel_id=1, source_target_pairs={{0,12},{4,8},{8,4},{12,0},{1,13},{5,9},{9,5},{13,1},{2,14},{6,10},... | collective-permute-start | bytes 24584 | tf_op jit(solution)/shard_map/ppermute | solution.py:48
  42.6 1.2 %collective-permute-start.21 = (f32[2,8,128]{2,1,0:T(8,128)S(1)}, f32[2,8,128]{2,1,0:T(8,128)S(1)}, u32[]{:S(2)}, u32[]{:S(2)}) collective-permute-start(f32[2,8,128]{2,1,0:T(8,128)S(1)} %shard_map.88.e_ref), channel_id=1, source_target_pairs={{0,3},{1,2},{2,1},{3,0},{4,7},{5,6},{6,5},{7,4},{8,11},{9,10},{10,... | collective-permute-start | bytes 24584 | tf_op jit(solution)/shard_map/ppermute | solution.py:48
  44.8 2.3 %collective-permute-done.21.xb = f32[2,8,128]{2,1,0:T(8,128)S(1)} collective-permute-done((f32[2,8,128]{2,1,0:T(8,128)S(1)}, f32[2,8,128]{2,1,0:T(8,128)S(1)}, u32[]{:S(2)}, u32[]{:S(2)}) %collective-permute-start.21) | collective-permute-done | bytes 8224 | tf_op jit(solution)/shard_map/ppermute | solution.py:48
  48.0 1.5 %collective-permute-start.29 = (f32[2,8,128]{2,1,0:T(8,128)S(1)}, f32[2,8,128]{2,1,0:T(8,128)S(1)}, u32[]{:S(2)}, u32[]{:S(2)}) collective-permute-start(f32[2,8,128]{2,1,0:T(8,128)S(1)} %shard_map.89.e_ref), channel_id=1, source_target_pairs={{0,112},{16,32},{32,16},{48,64},{64,48},{80,96},{96,80},{112,0},{1... | collective-permute-start | bytes 24584 | tf_op jit(solution)/shard_map/ppermute | solution.py:48
  49.5 1.8 %collective-permute-start.28 = (f32[2,8,128]{2,1,0:T(8,128)S(1)}, f32[2,8,128]{2,1,0:T(8,128)S(1)}, u32[]{:S(2)}, u32[]{:S(2)}) collective-permute-start(f32[2,8,128]{2,1,0:T(8,128)S(1)} %shard_map.89.e_ref), channel_id=1, source_target_pairs={{0,12},{4,8},{8,4},{12,0},{1,13},{5,9},{9,5},{13,1},{2,14},{6,10},... | collective-permute-start | bytes 24584 | tf_op jit(solution)/shard_map/ppermute | solution.py:48
  51.4 1.6 %collective-permute-start.27 = (f32[2,8,128]{2,1,0:T(8,128)S(1)}, f32[2,8,128]{2,1,0:T(8,128)S(1)}, u32[]{:S(2)}, u32[]{:S(2)}) collective-permute-start(f32[2,8,128]{2,1,0:T(8,128)S(1)} %shard_map.89.e_ref), channel_id=1, source_target_pairs={{0,3},{1,2},{2,1},{3,0},{4,7},{5,6},{6,5},{7,4},{8,11},{9,10},{10,... | collective-permute-start | bytes 24584 | tf_op jit(solution)/shard_map/ppermute | solution.py:48
  54.4 1.5 %collective-permute-done.27.xb = f32[2,8,128]{2,1,0:T(8,128)S(1)} collective-permute-done((f32[2,8,128]{2,1,0:T(8,128)S(1)}, f32[2,8,128]{2,1,0:T(8,128)S(1)}, u32[]{:S(2)}, u32[]{:S(2)}) %collective-permute-start.27) | collective-permute-done | bytes 8224 | tf_op jit(solution)/shard_map/ppermute | solution.py:48
  56.6 3.1 %shard_map.90 = f32[2,4,12,16,128]{4,3,2,1,0:T(8,128)} custom-call(f32[2,8,128]{2,1,0:T(8,128)S(1)} %shard_map.89.e_ref, f32[2,8,128]{2,1,0:T(8,128)S(1)} %collective-permute-done.24.xa, f32[2,8,128]{2,1,0:T(8,128)S(1)} %collective-permute-done.25.za, f32[2,8,128]{2,1,0:T(8,128)S(1)} %collective-permute-done.26.ta, ...), custom_call_target="tpu_custom_call" | custom-call | tf_op jit(solution)/shard_map/pallas_call | solution.py:568
  (61 shorter events, 10.2 us)
Async XLA Ops:
  1.9 10.0 %collective-permute-start = (bf16[24,16,128]{2,1,0:T(8,128)(2,1)S(1)}, bf16[24,16,128]{2,1,0:T(8,128)(2,1)S(1)}, u32[]{:S(2)}, u32[]{:S(2)}) collective-permute-start(bf16[24,16,128]{2,1,0:T(8,128)(2,1)S(1)} %get-tuple-element.13), channel_id=1, source_target_pairs={{0,112},{16,32},{32,16},{48,64},{64,48},{80,96},{96,80},{112,0},{1... | collective-permute-start | bytes 294920 | tf_op jit(solution)/shard_map/ppermute | solution.py:48
  7.1 8.6 %collective-permute-start.1 = (bf16[24,16,128]{2,1,0:T(8,128)(2,1)S(1)}, bf16[24,16,128]{2,1,0:T(8,128)(2,1)S(1)}, u32[]{:S(2)}, u32[]{:S(2)}) collective-permute-start(bf16[24,16,128]{2,1,0:T(8,128)(2,1)S(1)} %get-tuple-element.14), channel_id=1, source_target_pairs={{0,12},{4,8},{8,4},{12,0},{1,13},{5,9},{9,5},{13,1},{2,14},{6,10},... | collective-permute-start | bytes 294920 | tf_op jit(solution)/shard_map/ppermute | solution.py:48
  9.9 6.5 %collective-permute-start.2 = (bf16[24,16,128]{2,1,0:T(8,128)(2,1)S(1)}, bf16[24,16,128]{2,1,0:T(8,128)(2,1)S(1)}, u32[]{:S(2)}, u32[]{:S(2)}) collective-permute-start(bf16[24,16,128]{2,1,0:T(8,128)(2,1)S(1)} %get-tuple-element.15), channel_id=1, source_target_pairs={{0,3},{1,2},{2,1},{3,0},{4,7},{5,6},{6,5},{7,4},{8,11},{9,10},{10,... | collective-permute-start | bytes 294920 | tf_op jit(solution)/shard_map/ppermute | solution.py:48
  11.7 5.4 %collective-permute-start.3 = (bf16[24,16,128]{2,1,0:T(8,128)(2,1)S(1)}, bf16[24,16,128]{2,1,0:T(8,128)(2,1)S(1)}, u32[]{:S(2)}, u32[]{:S(2)}) collective-permute-start(bf16[24,16,128]{2,1,0:T(8,128)(2,1)S(1)} %get-tuple-element.16), channel_id=1, source_target_pairs={{0,16},{16,0},{32,48},{48,32},{64,80},{80,64},{96,112},{112,96},{1... | collective-permute-start | bytes 294920 | tf_op jit(solution)/shard_map/ppermute | solution.py:48
  11.7 5.4 %collective-permute-start.4 = (bf16[24,16,128]{2,1,0:T(8,128)(2,1)S(1)}, bf16[24,16,128]{2,1,0:T(8,128)(2,1)S(1)}, u32[]{:S(2)}, u32[]{:S(2)}) collective-permute-start(bf16[24,16,128]{2,1,0:T(8,128)(2,1)S(1)} %get-tuple-element.17), channel_id=1, source_target_pairs={{0,4},{4,0},{8,12},{12,8},{1,5},{5,1},{9,13},{13,9},{2,6},{6,2},{1... | collective-permute-start | bytes 294920 | tf_op jit(solution)/shard_map/ppermute | solution.py:48
  11.9 5.2 %collective-permute-start.5 = (bf16[24,16,128]{2,1,0:T(8,128)(2,1)S(1)}, bf16[24,16,128]{2,1,0:T(8,128)(2,1)S(1)}, u32[]{:S(2)}, u32[]{:S(2)}) collective-permute-start(bf16[24,16,128]{2,1,0:T(8,128)(2,1)S(1)} %get-tuple-element.18), channel_id=1, source_target_pairs={{0,1},{1,0},{2,3},{3,2},{4,5},{5,4},{6,7},{7,6},{8,9},{9,8},{10,11... | collective-permute-start | bytes 294920 | tf_op jit(solution)/shard_map/ppermute | solution.py:48
  20.4 5.8 %collective-permute-start.11 = (f32[2,8,128]{2,1,0:T(8,128)S(1)}, f32[2,8,128]{2,1,0:T(8,128)S(1)}, u32[]{:S(2)}, u32[]{:S(2)}) collective-permute-start(f32[2,8,128]{2,1,0:T(8,128)S(1)} %shard_map.85.e_ref.r_ref), channel_id=1, source_target_pairs={{0,112},{16,32},{32,16},{48,64},{64,48},{80,96},{96,80},{112,0},{1... | collective-permute-start | bytes 24584 | tf_op jit(solution)/shard_map/ppermute | solution.py:48
  20.6 7.6 %collective-permute-start.10 = (f32[2,8,128]{2,1,0:T(8,128)S(1)}, f32[2,8,128]{2,1,0:T(8,128)S(1)}, u32[]{:S(2)}, u32[]{:S(2)}) collective-permute-start(f32[2,8,128]{2,1,0:T(8,128)S(1)} %shard_map.85.e_ref.r_ref), channel_id=1, source_target_pairs={{0,12},{4,8},{8,4},{12,0},{1,13},{5,9},{9,5},{13,1},{2,14},{6,10},... | collective-permute-start | bytes 24584 | tf_op jit(solution)/shard_map/ppermute | solution.py:48
  22.7 5.4 %collective-permute-start.9 = (f32[2,8,128]{2,1,0:T(8,128)S(1)}, f32[2,8,128]{2,1,0:T(8,128)S(1)}, u32[]{:S(2)}, u32[]{:S(2)}) collective-permute-start(f32[2,8,128]{2,1,0:T(8,128)S(1)} %shard_map.85.e_ref.r_ref), channel_id=1, source_target_pairs={{0,3},{1,2},{2,1},{3,0},{4,7},{5,6},{6,5},{7,4},{8,11},{9,10},{10,... | collective-permute-start | bytes 24584 | tf_op jit(solution)/shard_map/ppermute | solution.py:48
  25.8 3.7 %collective-permute-start.8 = (f32[2,8,128]{2,1,0:T(8,128)S(1)}, f32[2,8,128]{2,1,0:T(8,128)S(1)}, u32[]{:S(2)}, u32[]{:S(2)}) collective-permute-start(f32[2,8,128]{2,1,0:T(8,128)S(1)} %shard_map.85.e_ref.r_ref), channel_id=1, source_target_pairs={{0,16},{16,0},{32,48},{48,32},{64,80},{80,64},{96,112},{112,96},{1... | collective-permute-start | bytes 24584 | tf_op jit(solution)/shard_map/ppermute | solution.py:48
  30.0 5.8 %collective-permute-start.17 = (f32[2,8,128]{2,1,0:T(8,128)S(1)}, f32[2,8,128]{2,1,0:T(8,128)S(1)}, u32[]{:S(2)}, u32[]{:S(2)}) collective-permute-start(f32[2,8,128]{2,1,0:T(8,128)S(1)} %shard_map.87.e_ref), channel_id=1, source_target_pairs={{0,112},{16,32},{32,16},{48,64},{64,48},{80,96},{96,80},{112,0},{1... | collective-permute-start | bytes 24584 | tf_op jit(solution)/shard_map/ppermute | solution.py:48
  30.2 5.6 %collective-permute-start.16 = (f32[2,8,128]{2,1,0:T(8,128)S(1)}, f32[2,8,128]{2,1,0:T(8,128)S(1)}, u32[]{:S(2)}, u32[]{:S(2)}) collective-permute-start(f32[2,8,128]{2,1,0:T(8,128)S(1)} %shard_map.87.e_ref), channel_id=1, source_target_pairs={{0,12},{4,8},{8,4},{12,0},{1,13},{5,9},{9,5},{13,1},{2,14},{6,10},... | collective-permute-start | bytes 24584 | tf_op jit(solution)/shard_map/ppermute | solution.py:48
  33.0 4.6 %collective-permute-start.15 = (f32[2,8,128]{2,1,0:T(8,128)S(1)}, f32[2,8,128]{2,1,0:T(8,128)S(1)}, u32[]{:S(2)}, u32[]{:S(2)}) collective-permute-start(f32[2,8,128]{2,1,0:T(8,128)S(1)} %shard_map.87.e_ref), channel_id=1, source_target_pairs={{0,3},{1,2},{2,1},{3,0},{4,7},{5,6},{6,5},{7,4},{8,11},{9,10},{10,... | collective-permute-start | bytes 24584 | tf_op jit(solution)/shard_map/ppermute | solution.py:48
  34.6 3.7 %collective-permute-start.13 = (f32[2,8,128]{2,1,0:T(8,128)S(1)}, f32[2,8,128]{2,1,0:T(8,128)S(1)}, u32[]{:S(2)}, u32[]{:S(2)}) collective-permute-start(f32[2,8,128]{2,1,0:T(8,128)S(1)} %shard_map.87.e_ref), channel_id=1, source_target_pairs={{0,4},{4,0},{8,12},{12,8},{1,5},{5,1},{9,13},{13,9},{2,6},{6,2},{1... | collective-permute-start | bytes 24584 | tf_op jit(solution)/shard_map/ppermute | solution.py:48
  38.8 5.8 %collective-permute-start.23 = (f32[2,8,128]{2,1,0:T(8,128)S(1)}, f32[2,8,128]{2,1,0:T(8,128)S(1)}, u32[]{:S(2)}, u32[]{:S(2)}) collective-permute-start(f32[2,8,128]{2,1,0:T(8,128)S(1)} %shard_map.88.e_ref), channel_id=1, source_target_pairs={{0,112},{16,32},{32,16},{48,64},{64,48},{80,96},{96,80},{112,0},{1... | collective-permute-start | bytes 24584 | tf_op jit(solution)/shard_map/ppermute | solution.py:48
  39.9 4.9 %collective-permute-start.22 = (f32[2,8,128]{2,1,0:T(8,128)S(1)}, f32[2,8,128]{2,1,0:T(8,128)S(1)}, u32[]{:S(2)}, u32[]{:S(2)}) collective-permute-start(f32[2,8,128]{2,1,0:T(8,128)S(1)} %shard_map.88.e_ref), channel_id=1, source_target_pairs={{0,12},{4,8},{8,4},{12,0},{1,13},{5,9},{9,5},{13,1},{2,14},{6,10},... | collective-permute-start | bytes 24584 | tf_op jit(solution)/shard_map/ppermute | solution.py:48
  42.6 4.6 %collective-permute-start.21 = (f32[2,8,128]{2,1,0:T(8,128)S(1)}, f32[2,8,128]{2,1,0:T(8,128)S(1)}, u32[]{:S(2)}, u32[]{:S(2)}) collective-permute-start(f32[2,8,128]{2,1,0:T(8,128)S(1)} %shard_map.88.e_ref), channel_id=1, source_target_pairs={{0,3},{1,2},{2,1},{3,0},{4,7},{5,6},{6,5},{7,4},{8,11},{9,10},{10,... | collective-permute-start | bytes 24584 | tf_op jit(solution)/shard_map/ppermute | solution.py:48
  43.8 3.7 %collective-permute-start.20 = (f32[2,8,128]{2,1,0:T(8,128)S(1)}, f32[2,8,128]{2,1,0:T(8,128)S(1)}, u32[]{:S(2)}, u32[]{:S(2)}) collective-permute-start(f32[2,8,128]{2,1,0:T(8,128)S(1)} %shard_map.88.e_ref), channel_id=1, source_target_pairs={{0,16},{16,0},{32,48},{48,32},{64,80},{80,64},{96,112},{112,96},{1... | collective-permute-start | bytes 24584 | tf_op jit(solution)/shard_map/ppermute | solution.py:48
  43.8 3.7 %collective-permute-start.19 = (f32[2,8,128]{2,1,0:T(8,128)S(1)}, f32[2,8,128]{2,1,0:T(8,128)S(1)}, u32[]{:S(2)}, u32[]{:S(2)}) collective-permute-start(f32[2,8,128]{2,1,0:T(8,128)S(1)} %shard_map.88.e_ref), channel_id=1, source_target_pairs={{0,4},{4,0},{8,12},{12,8},{1,5},{5,1},{9,13},{13,9},{2,6},{6,2},{1... | collective-permute-start | bytes 24584 | tf_op jit(solution)/shard_map/ppermute | solution.py:48
  48.0 5.8 %collective-permute-start.29 = (f32[2,8,128]{2,1,0:T(8,128)S(1)}, f32[2,8,128]{2,1,0:T(8,128)S(1)}, u32[]{:S(2)}, u32[]{:S(2)}) collective-permute-start(f32[2,8,128]{2,1,0:T(8,128)S(1)} %shard_map.89.e_ref), channel_id=1, source_target_pairs={{0,112},{16,32},{32,16},{48,64},{64,48},{80,96},{96,80},{112,0},{1... | collective-permute-start | bytes 24584 | tf_op jit(solution)/shard_map/ppermute | solution.py:48
  49.5 4.9 %collective-permute-start.28 = (f32[2,8,128]{2,1,0:T(8,128)S(1)}, f32[2,8,128]{2,1,0:T(8,128)S(1)}, u32[]{:S(2)}, u32[]{:S(2)}) collective-permute-start(f32[2,8,128]{2,1,0:T(8,128)S(1)} %shard_map.89.e_ref), channel_id=1, source_target_pairs={{0,12},{4,8},{8,4},{12,0},{1,13},{5,9},{9,5},{13,1},{2,14},{6,10},... | collective-permute-start | bytes 24584 | tf_op jit(solution)/shard_map/ppermute | solution.py:48
  51.4 4.6 %collective-permute-start.27 = (f32[2,8,128]{2,1,0:T(8,128)S(1)}, f32[2,8,128]{2,1,0:T(8,128)S(1)}, u32[]{:S(2)}, u32[]{:S(2)}) collective-permute-start(f32[2,8,128]{2,1,0:T(8,128)S(1)} %shard_map.89.e_ref), channel_id=1, source_target_pairs={{0,3},{1,2},{2,1},{3,0},{4,7},{5,6},{6,5},{7,4},{8,11},{9,10},{10,... | collective-permute-start | bytes 24584 | tf_op jit(solution)/shard_map/ppermute | solution.py:48
  52.9 3.7 %collective-permute-start.26 = (f32[2,8,128]{2,1,0:T(8,128)S(1)}, f32[2,8,128]{2,1,0:T(8,128)S(1)}, u32[]{:S(2)}, u32[]{:S(2)}) collective-permute-start(f32[2,8,128]{2,1,0:T(8,128)S(1)} %shard_map.89.e_ref), channel_id=1, source_target_pairs={{0,16},{16,0},{32,48},{48,32},{64,80},{80,64},{96,112},{112,96},{1... | collective-permute-start | bytes 24584 | tf_op jit(solution)/shard_map/ppermute | solution.py:48
  52.9 3.7 %collective-permute-start.25 = (f32[2,8,128]{2,1,0:T(8,128)S(1)}, f32[2,8,128]{2,1,0:T(8,128)S(1)}, u32[]{:S(2)}, u32[]{:S(2)}) collective-permute-start(f32[2,8,128]{2,1,0:T(8,128)S(1)} %shard_map.89.e_ref), channel_id=1, source_target_pairs={{0,4},{4,0},{8,12},{12,8},{1,5},{5,1},{9,13},{13,9},{2,6},{6,2},{1... | collective-permute-start | bytes 24584 | tf_op jit(solution)/shard_map/ppermute | solution.py:48
  (14 other events, 97.6 us)

commit v5 on v4

--- a/solution.py
+++ b/solution.py
@@ -218,6 +218,7 @@
     wide_ref, side_ref, when_ref, spin_ref, wall_ref, links_ref, clover_ref, out_ref,
 ):
     first_time = lax.axis_index("ta") * BLOCK
+    upper = row_index(HALF) >= 4
 
     def rhs(r, carry):
         when = when_ref[r]
@@ -238,6 +239,16 @@
                     for s in range(2)
                 ]
                 hop(3, sign, field, link_loader(links_ref, 6 + side, low), total)
+            sign = -1.0 if half == 0 else 1.0
+            turned = [
+                mapped(
+                    lambda p: pltpu.roll(p, 4, 0),
+                    projected(0, sign, lambda part, c, start=start: wide_ref[part, r, c, start : start + HALF, :]),
+                )
+                for start in (0, HALF)
+            ]
+            field = mapped(lambda a, b: jnp.where(upper, b, a), *turned)
+            hop(0, sign, field, link_loader(links_ref, half, low), total)
             at_wall = first_time + 2 * half + row_index(HALF) // BLOCK == when
             for chirality in range(2):
                 values = [(load(0, 6 * chirality + i), load(1, 6 * chirality + i)) for i in range(6)]
@@ -305,7 +316,7 @@
 
 
 def fine_kernel(
-    wide_ref, partial_ref, tb_ref, zb_ref, xb_ref, ta_ref, za_ref, xa_ref, links_ref, near_ref,
+    wide_ref, partial_ref, xb_ref, tb_ref, zb_ref, ta_ref, za_ref, xa_ref, links_ref, near_ref,
     out_ref, tedge, zedge, xedge, residual, rows_ref,
 ):
     even = [is_even(axis) for axis in ("ta", "gz", "xy")]
@@ -351,17 +362,13 @@
                 return load
 
             total = [[[None, None] for _ in range(3)] for _ in range(4)]
-            for side, sign in enumerate((-1.0, 1.0)):
-                def turned(start):
-                    return mapped(lambda p: pltpu.roll(p, 4, 0), projected(0, sign, loader(start)))
-
-                edge = table(lambda slot: tedge[side, slot, r])
-                if side == 0:
-                    lower_part, upper_part = (turned(0), turned(8)) if half == 0 else (turned(8), edge)
-                else:
-                    lower_part, upper_part = (edge, turned(0)) if half == 0 else (turned(0), turned(8))
-                field = mapped(lambda a, b: jnp.where(upper, b, a), lower_part, upper_part)
-                hop(0, sign, field, link_loader(links_ref, side, low), total)
+            side = 1 if half == 0 else 0
+            sign = 1.0 if half == 0 else -1.0
+            turned = mapped(lambda p: pltpu.roll(p, 4, 0), projected(0, sign, loader(low)))
+            edge = table(lambda slot: tedge[side, slot, r])
+            lower_part, upper_part = (edge, turned) if half == 0 else (turned, edge)
+            field = mapped(lambda a, b: jnp.where(upper, b, a), lower_part, upper_part)
+            hop(0, sign, field, link_loader(links_ref, side, low), total)
             for side, sign in enumerate((-1.0, 1.0)):
                 row = 4 * r + 2 * half
                 first = table(lambda slot: zedge[side, slot, pl.ds(row, 1), :])
@@ -450,7 +457,7 @@
         ],
         compiler_params=vmem_params(24),
         cost_estimate=pl.CostEstimate(flops=40_000_000, bytes_accessed=20_000_000, transcendentals=0),
-    )(wide, partial, *[halos[i] for i in (1, 3, 5, 0, 2, 4)], links, near)
+    )(wide, partial, *[halos[i] for i in (5, 1, 3, 0, 2, 4)], links, near)
 
 
 def merge(low, high, width, inside):

time: 60.8 us -> 59.6 us (0.980)
  starting transfers between devices: 32.1 us -> 31.3 us
    ppermute x30, starting transfers between devices: 32.1 us -> 31.3 us  [swap(): return lax.ppermute(value, axis, pairs)]
  transfers between devices with their start and end apart: 30 -> 30, of which waited for: 15 -> 14; matrix products, arithmetic and copies ran while one was open for 0% -> 0% of each run, Pallas kernels for 7% -> 8%
where the time goes in v5:
time: 59.6 us; the launch traced here: 58.9 us
  starting transfers between devices  31.3 us (53%)
  Pallas kernels  13.3 us (22%)
  waiting for transfers between devices  13 us (22%)
  local copies, waits for them, and re-layouts  1.12 us (2%)
    ppermute x30, starting transfers between devices, swap(): return lax.ppermute(value, axis, pairs)  31.3 us
    ppermute x30, waiting for transfers between devices, swap(): return lax.ppermute(value, axis, pairs)  13 us
    pallas_call x1, Pallas kernels, last(): pl.pallas_call(last_kernel, out_shape=jax.ShapeDtypeStruct((2, 4, 12, ROW...  3.11 us
    pallas_call x1, Pallas kernels, fine(): pl.pallas_call(fine_kernel, out_shape=jax.ShapeDtypeStruct((2, HALF, LANE...  3.06 us
    pallas_call x1, Pallas kernels, centre(): pl.pallas_call(centre_kernel, out_shape=jax.ShapeDtypeStruct((4, 24, ROWS...  2.22 us
    pallas_call x1, Pallas kernels, spread(): pl.pallas_call(spread_kernel, out_shape=jax.ShapeDtypeStruct((9, 3, 24, H...  1.71 us
    pallas_call x3, Pallas kernels, coarse(): pl.pallas_call(coarse_kernel, out_shape=jax.ShapeDtypeStruct((2, HALF, LA...  1.7 us
  transfers between devices with their start and end apart: 30, of which 14 were waited for; matrix products, arithmetic and copies ran while one was open for 0% of the time, Pallas kernels for 8%

profile of v5, /device:TPU:0, one launch (start us, length us, event | category | flops | bytes accessed | tf_op | source)
XLA Modules:
  0.0 58.9 jit_solution(15682080581089439743)
XLA Ops:
  0.0 1.1 %copy-done.4 = bf16[2,4,12,4,4,128]{5,4,3,2,1,0:T(4,128)(2,1)S(1)} copy-done((bf16[2,4,12,4,4,128]{5,4,3,2,1,0:T(4,128)(2,1)S(1)}, bf16[2,4,12,4,4,128]{5,4,3,2,1,0:T(4,128)(2,1)}, u32[]{:S(2)}) %copy-start.4) | copy-done | bytes 393240
  1.9 2.8 %collective-permute-start = (bf16[24,16,128]{2,1,0:T(8,128)(2,1)S(1)}, bf16[24,16,128]{2,1,0:T(8,128)(2,1)S(1)}, u32[]{:S(2)}, u32[]{:S(2)}) collective-permute-start(bf16[24,16,128]{2,1,0:T(8,128)(2,1)S(1)} %get-tuple-element.13), channel_id=1, source_target_pairs={{0,3},{1,2},{2,1},{3,0},{4,7},{5,6},{6,5},{7,4},{8,11},{9,10},{10,... | collective-permute-start | bytes 294920 | tf_op jit(solution)/shard_map/ppermute | solution.py:48
  4.7 4.2 %collective-permute-start.1 = (bf16[24,16,128]{2,1,0:T(8,128)(2,1)S(1)}, bf16[24,16,128]{2,1,0:T(8,128)(2,1)S(1)}, u32[]{:S(2)}, u32[]{:S(2)}) collective-permute-start(bf16[24,16,128]{2,1,0:T(8,128)(2,1)S(1)} %get-tuple-element.14), channel_id=1, source_target_pairs={{0,112},{16,32},{32,16},{48,64},{64,48},{80,96},{96,80},{112,0},{1... | collective-permute-start | bytes 294920 | tf_op jit(solution)/shard_map/ppermute | solution.py:48
  8.9 2.8 %collective-permute-start.2 = (bf16[24,16,128]{2,1,0:T(8,128)(2,1)S(1)}, bf16[24,16,128]{2,1,0:T(8,128)(2,1)S(1)}, u32[]{:S(2)}, u32[]{:S(2)}) collective-permute-start(bf16[24,16,128]{2,1,0:T(8,128)(2,1)S(1)} %get-tuple-element.15), channel_id=1, source_target_pairs={{0,12},{4,8},{8,4},{12,0},{1,13},{5,9},{9,5},{13,1},{2,14},{6,10},... | collective-permute-start | bytes 294920 | tf_op jit(solution)/shard_map/ppermute | solution.py:48
  12.6 2.2 %shard_map.84.partial_ref = f32[4,24,16,128]{3,2,1,0:T(8,128)S(1)} custom-call(f32[2,4,12,16,128]{4,3,2,1,0:T(8,128)S(1)} %get-tuple-element.12.wide_ref.psi_ref, f32[2,4,12,16,128]{4,3,2,1,0:T(8,128)S(1)} %shard_map.83.side_ref, s32[4]{0:T(128)S(1)} %copy-done.6, s32[4]{0:T(128)S(1)} %copy-done.7, f32[3,2,4]{2,1,0:T(2,128)S(1)} %bitcast.16, ...), custom_call_target="tpu_custom_call" | custom-call | flops 40000000 | bytes 20000000 | tf_op jit(solution)/shard_map/pallas_call | solution.py:280
  15.2 1.3 %collective-permute-done.3.ta_ref = bf16[24,16,128]{2,1,0:T(8,128)(2,1)S(1)} collective-permute-done((bf16[24,16,128]{2,1,0:T(8,128)(2,1)S(1)}, bf16[24,16,128]{2,1,0:T(8,128)(2,1)S(1)}, u32[]{:S(2)}, u32[]{:S(2)}) %collective-permute-start.3) | collective-permute-done | bytes 98336 | tf_op jit(solution)/shard_map/ppermute | solution.py:48
  16.5 3.1 %shard_map.85.e_ref.r_ref = f32[2,8,128]{2,1,0:T(8,128)S(1)} custom-call(f32[2,4,12,16,128]{4,3,2,1,0:T(8,128)S(1)} %get-tuple-element.12.wide_ref.psi_ref, f32[4,24,16,128]{3,2,1,0:T(8,128)S(1)} %shard_map.84.partial_ref, bf16[24,16,128]{2,1,0:T(8,128)(2,1)S(1)} %collective-permute-done.xb_ref, bf16[24,16,128]{2,1,0:T(8,128)(2,1)S(1)} %collective-permute-done.1.tb_ref, ...), custom_call_target="tpu_custom_call" | custom-call | flops 40000000 | bytes 20000000 | tf_op jit(solution)/shard_map/pallas_call | solution.py:446
  20.0 2.8 %collective-permute-start.10 = (f32[2,8,128]{2,1,0:T(8,128)S(1)}, f32[2,8,128]{2,1,0:T(8,128)S(1)}, u32[]{:S(2)}, u32[]{:S(2)}) collective-permute-start(f32[2,8,128]{2,1,0:T(8,128)S(1)} %shard_map.85.e_ref.r_ref), channel_id=1, source_target_pairs={{0,12},{4,8},{8,4},{12,0},{1,13},{5,9},{9,5},{13,1},{2,14},{6,10},... | collective-permute-start | bytes 24584 | tf_op jit(solution)/shard_map/ppermute | solution.py:48
  22.8 2.3 %collective-permute-start.9 = (f32[2,8,128]{2,1,0:T(8,128)S(1)}, f32[2,8,128]{2,1,0:T(8,128)S(1)}, u32[]{:S(2)}, u32[]{:S(2)}) collective-permute-start(f32[2,8,128]{2,1,0:T(8,128)S(1)} %shard_map.85.e_ref.r_ref), channel_id=1, source_target_pairs={{0,3},{1,2},{2,1},{3,0},{4,7},{5,6},{6,5},{7,4},{8,11},{9,10},{10,... | collective-permute-start | bytes 24584 | tf_op jit(solution)/shard_map/ppermute | solution.py:48
  25.9 1.7 %shard_map.86.operator_ref = f32[9,3,24,8,128]{4,3,2,1,0:T(8,128)S(1)} custom-call(f32[432,8,24]{2,1,0:T(8,128)S(1)} %bitcast.13), custom_call_target="tpu_custom_call" | custom-call | tf_op jit(solution)/shard_map/pallas_call | solution.py:309
  27.6 1.1 %collective-permute-done.8.ta = f32[2,8,128]{2,1,0:T(8,128)S(1)} collective-permute-done((f32[2,8,128]{2,1,0:T(8,128)S(1)}, f32[2,8,128]{2,1,0:T(8,128)S(1)}, u32[]{:S(2)}, u32[]{:S(2)}) %collective-permute-start.8) | collective-permute-done | bytes 8224 | tf_op jit(solution)/shard_map/ppermute | solution.py:48
  29.3 1.1 %collective-permute-start.17 = (f32[2,8,128]{2,1,0:T(8,128)S(1)}, f32[2,8,128]{2,1,0:T(8,128)S(1)}, u32[]{:S(2)}, u32[]{:S(2)}) collective-permute-start(f32[2,8,128]{2,1,0:T(8,128)S(1)} %shard_map.87.e_ref), channel_id=1, source_target_pairs={{0,112},{16,32},{32,16},{48,64},{64,48},{80,96},{96,80},{112,0},{1... | collective-permute-start | bytes 24584 | tf_op jit(solution)/shard_map/ppermute | solution.py:48
  30.4 1.9 %collective-permute-start.16 = (f32[2,8,128]{2,1,0:T(8,128)S(1)}, f32[2,8,128]{2,1,0:T(8,128)S(1)}, u32[]{:S(2)}, u32[]{:S(2)}) collective-permute-start(f32[2,8,128]{2,1,0:T(8,128)S(1)} %shard_map.87.e_ref), channel_id=1, source_target_pairs={{0,12},{4,8},{8,4},{12,0},{1,13},{5,9},{9,5},{13,1},{2,14},{6,10},... | collective-permute-start | bytes 24584 | tf_op jit(solution)/shard_map/ppermute | solution.py:48
  32.2 1.9 %collective-permute-start.15 = (f32[2,8,128]{2,1,0:T(8,128)S(1)}, f32[2,8,128]{2,1,0:T(8,128)S(1)}, u32[]{:S(2)}, u32[]{:S(2)}) collective-permute-start(f32[2,8,128]{2,1,0:T(8,128)S(1)} %shard_map.87.e_ref), channel_id=1, source_target_pairs={{0,3},{1,2},{2,1},{3,0},{4,7},{5,6},{6,5},{7,4},{8,11},{9,10},{10,... | collective-permute-start | bytes 24584 | tf_op jit(solution)/shard_map/ppermute | solution.py:48
  35.3 1.5 %collective-permute-done.15.xb = f32[2,8,128]{2,1,0:T(8,128)S(1)} collective-permute-done((f32[2,8,128]{2,1,0:T(8,128)S(1)}, f32[2,8,128]{2,1,0:T(8,128)S(1)}, u32[]{:S(2)}, u32[]{:S(2)}) %collective-permute-start.15) | collective-permute-done | bytes 8224 | tf_op jit(solution)/shard_map/ppermute | solution.py:48
  39.1 2.8 %collective-permute-start.22 = (f32[2,8,128]{2,1,0:T(8,128)S(1)}, f32[2,8,128]{2,1,0:T(8,128)S(1)}, u32[]{:S(2)}, u32[]{:S(2)}) collective-permute-start(f32[2,8,128]{2,1,0:T(8,128)S(1)} %shard_map.88.e_ref), channel_id=1, source_target_pairs={{0,12},{4,8},{8,4},{12,0},{1,13},{5,9},{9,5},{13,1},{2,14},{6,10},... | collective-permute-start | bytes 24584 | tf_op jit(solution)/shard_map/ppermute | solution.py:48
  41.8 1.2 %collective-permute-start.21 = (f32[2,8,128]{2,1,0:T(8,128)S(1)}, f32[2,8,128]{2,1,0:T(8,128)S(1)}, u32[]{:S(2)}, u32[]{:S(2)}) collective-permute-start(f32[2,8,128]{2,1,0:T(8,128)S(1)} %shard_map.88.e_ref), channel_id=1, source_target_pairs={{0,3},{1,2},{2,1},{3,0},{4,7},{5,6},{6,5},{7,4},{8,11},{9,10},{10,... | collective-permute-start | bytes 24584 | tf_op jit(solution)/shard_map/ppermute | solution.py:48
  43.1 1.1 %collective-permute-done.23.tb = f32[2,8,128]{2,1,0:T(8,128)S(1)} collective-permute-done((f32[2,8,128]{2,1,0:T(8,128)S(1)}, f32[2,8,128]{2,1,0:T(8,128)S(1)}, u32[]{:S(2)}, u32[]{:S(2)}) %collective-permute-start.23) | collective-permute-done | bytes 8224 | tf_op jit(solution)/shard_map/ppermute | solution.py:48
  44.1 2.3 %collective-permute-done.21.xb = f32[2,8,128]{2,1,0:T(8,128)S(1)} collective-permute-done((f32[2,8,128]{2,1,0:T(8,128)S(1)}, f32[2,8,128]{2,1,0:T(8,128)S(1)}, u32[]{:S(2)}, u32[]{:S(2)}) %collective-permute-start.21) | collective-permute-done | bytes 8224 | tf_op jit(solution)/shard_map/ppermute | solution.py:48
  47.3 1.6 %collective-permute-start.29 = (f32[2,8,128]{2,1,0:T(8,128)S(1)}, f32[2,8,128]{2,1,0:T(8,128)S(1)}, u32[]{:S(2)}, u32[]{:S(2)}) collective-permute-start(f32[2,8,128]{2,1,0:T(8,128)S(1)} %shard_map.89.e_ref), channel_id=1, source_target_pairs={{0,112},{16,32},{32,16},{48,64},{64,48},{80,96},{96,80},{112,0},{1... | collective-permute-start | bytes 24584 | tf_op jit(solution)/shard_map/ppermute | solution.py:48
  48.9 2.0 %collective-permute-start.28 = (f32[2,8,128]{2,1,0:T(8,128)S(1)}, f32[2,8,128]{2,1,0:T(8,128)S(1)}, u32[]{:S(2)}, u32[]{:S(2)}) collective-permute-start(f32[2,8,128]{2,1,0:T(8,128)S(1)} %shard_map.89.e_ref), channel_id=1, source_target_pairs={{0,12},{4,8},{8,4},{12,0},{1,13},{5,9},{9,5},{13,1},{2,14},{6,10},... | collective-permute-start | bytes 24584 | tf_op jit(solution)/shard_map/ppermute | solution.py:48
  50.9 1.2 %collective-permute-start.27 = (f32[2,8,128]{2,1,0:T(8,128)S(1)}, f32[2,8,128]{2,1,0:T(8,128)S(1)}, u32[]{:S(2)}, u32[]{:S(2)}) collective-permute-start(f32[2,8,128]{2,1,0:T(8,128)S(1)} %shard_map.89.e_ref), channel_id=1, source_target_pairs={{0,3},{1,2},{2,1},{3,0},{4,7},{5,6},{6,5},{7,4},{8,11},{9,10},{10,... | collective-permute-start | bytes 24584 | tf_op jit(solution)/shard_map/ppermute | solution.py:48
  53.8 1.7 %collective-permute-done.27.xb = f32[2,8,128]{2,1,0:T(8,128)S(1)} collective-permute-done((f32[2,8,128]{2,1,0:T(8,128)S(1)}, f32[2,8,128]{2,1,0:T(8,128)S(1)}, u32[]{:S(2)}, u32[]{:S(2)}) %collective-permute-start.27) | collective-permute-done | bytes 8224 | tf_op jit(solution)/shard_map/ppermute | solution.py:48
  55.8 3.1 %shard_map.90 = f32[2,4,12,16,128]{4,3,2,1,0:T(8,128)} custom-call(f32[2,8,128]{2,1,0:T(8,128)S(1)} %shard_map.89.e_ref, f32[2,8,128]{2,1,0:T(8,128)S(1)} %collective-permute-done.24.xa, f32[2,8,128]{2,1,0:T(8,128)S(1)} %collective-permute-done.25.za, f32[2,8,128]{2,1,0:T(8,128)S(1)} %collective-permute-done.26.ta, ...), custom_call_target="tpu_custom_call" | custom-call | tf_op jit(solution)/shard_map/pallas_call | solution.py:575
  (61 shorter events, 10.2 us)
Async XLA Ops:
  1.9 9.9 %collective-permute-start = (bf16[24,16,128]{2,1,0:T(8,128)(2,1)S(1)}, bf16[24,16,128]{2,1,0:T(8,128)(2,1)S(1)}, u32[]{:S(2)}, u32[]{:S(2)}) collective-permute-start(bf16[24,16,128]{2,1,0:T(8,128)(2,1)S(1)} %get-tuple-element.13), channel_id=1, source_target_pairs={{0,3},{1,2},{2,1},{3,0},{4,7},{5,6},{6,5},{7,4},{8,11},{9,10},{10,... | collective-permute-start | bytes 294920 | tf_op jit(solution)/shard_map/ppermute | solution.py:48
  4.7 10.1 %collective-permute-start.1 = (bf16[24,16,128]{2,1,0:T(8,128)(2,1)S(1)}, bf16[24,16,128]{2,1,0:T(8,128)(2,1)S(1)}, u32[]{:S(2)}, u32[]{:S(2)}) collective-permute-start(bf16[24,16,128]{2,1,0:T(8,128)(2,1)S(1)} %get-tuple-element.14), channel_id=1, source_target_pairs={{0,112},{16,32},{32,16},{48,64},{64,48},{80,96},{96,80},{112,0},{1... | collective-permute-start | bytes 294920 | tf_op jit(solution)/shard_map/ppermute | solution.py:48
  8.9 6.3 %collective-permute-start.2 = (bf16[24,16,128]{2,1,0:T(8,128)(2,1)S(1)}, bf16[24,16,128]{2,1,0:T(8,128)(2,1)S(1)}, u32[]{:S(2)}, u32[]{:S(2)}) collective-permute-start(bf16[24,16,128]{2,1,0:T(8,128)(2,1)S(1)} %get-tuple-element.15), channel_id=1, source_target_pairs={{0,12},{4,8},{8,4},{12,0},{1,13},{5,9},{9,5},{13,1},{2,14},{6,10},... | collective-permute-start | bytes 294920 | tf_op jit(solution)/shard_map/ppermute | solution.py:48
  11.6 4.8 %collective-permute-start.3 = (bf16[24,16,128]{2,1,0:T(8,128)(2,1)S(1)}, bf16[24,16,128]{2,1,0:T(8,128)(2,1)S(1)}, u32[]{:S(2)}, u32[]{:S(2)}) collective-permute-start(bf16[24,16,128]{2,1,0:T(8,128)(2,1)S(1)} %get-tuple-element.16), channel_id=1, source_target_pairs={{0,16},{16,0},{32,48},{48,32},{64,80},{80,64},{96,112},{112,96},{1... | collective-permute-start | bytes 294920 | tf_op jit(solution)/shard_map/ppermute | solution.py:48
  11.6 4.8 %collective-permute-start.4 = (bf16[24,16,128]{2,1,0:T(8,128)(2,1)S(1)}, bf16[24,16,128]{2,1,0:T(8,128)(2,1)S(1)}, u32[]{:S(2)}, u32[]{:S(2)}) collective-permute-start(bf16[24,16,128]{2,1,0:T(8,128)(2,1)S(1)} %get-tuple-element.17), channel_id=1, source_target_pairs={{0,4},{4,0},{8,12},{12,8},{1,5},{5,1},{9,13},{13,9},{2,6},{6,2},{1... | collective-permute-start | bytes 294920 | tf_op jit(solution)/shard_map/ppermute | solution.py:48
  11.8 4.6 %collective-permute-start.5 = (bf16[24,16,128]{2,1,0:T(8,128)(2,1)S(1)}, bf16[24,16,128]{2,1,0:T(8,128)(2,1)S(1)}, u32[]{:S(2)}, u32[]{:S(2)}) collective-permute-start(bf16[24,16,128]{2,1,0:T(8,128)(2,1)S(1)} %get-tuple-element.18), channel_id=1, source_target_pairs={{0,1},{1,0},{2,3},{3,2},{4,5},{5,4},{6,7},{7,6},{8,9},{9,8},{10,11... | collective-permute-start | bytes 294920 | tf_op jit(solution)/shard_map/ppermute | solution.py:48
  19.5 5.8 %collective-permute-start.11 = (f32[2,8,128]{2,1,0:T(8,128)S(1)}, f32[2,8,128]{2,1,0:T(8,128)S(1)}, u32[]{:S(2)}, u32[]{:S(2)}) collective-permute-start(f32[2,8,128]{2,1,0:T(8,128)S(1)} %shard_map.85.e_ref.r_ref), channel_id=1, source_target_pairs={{0,112},{16,32},{32,16},{48,64},{64,48},{80,96},{96,80},{112,0},{1... | collective-permute-start | bytes 24584 | tf_op jit(solution)/shard_map/ppermute | solution.py:48
  20.0 7.6 %collective-permute-start.10 = (f32[2,8,128]{2,1,0:T(8,128)S(1)}, f32[2,8,128]{2,1,0:T(8,128)S(1)}, u32[]{:S(2)}, u32[]{:S(2)}) collective-permute-start(f32[2,8,128]{2,1,0:T(8,128)S(1)} %shard_map.85.e_ref.r_ref), channel_id=1, source_target_pairs={{0,12},{4,8},{8,4},{12,0},{1,13},{5,9},{9,5},{13,1},{2,14},{6,10},... | collective-permute-start | bytes 24584 | tf_op jit(solution)/shard_map/ppermute | solution.py:48
  22.8 4.8 %collective-permute-start.9 = (f32[2,8,128]{2,1,0:T(8,128)S(1)}, f32[2,8,128]{2,1,0:T(8,128)S(1)}, u32[]{:S(2)}, u32[]{:S(2)}) collective-permute-start(f32[2,8,128]{2,1,0:T(8,128)S(1)} %shard_map.85.e_ref.r_ref), channel_id=1, source_target_pairs={{0,3},{1,2},{2,1},{3,0},{4,7},{5,6},{6,5},{7,4},{8,11},{9,10},{10,... | collective-permute-start | bytes 24584 | tf_op jit(solution)/shard_map/ppermute | solution.py:48
  25.1 3.7 %collective-permute-start.8 = (f32[2,8,128]{2,1,0:T(8,128)S(1)}, f32[2,8,128]{2,1,0:T(8,128)S(1)}, u32[]{:S(2)}, u32[]{:S(2)}) collective-permute-start(f32[2,8,128]{2,1,0:T(8,128)S(1)} %shard_map.85.e_ref.r_ref), channel_id=1, source_target_pairs={{0,16},{16,0},{32,48},{48,32},{64,80},{80,64},{96,112},{112,96},{1... | collective-permute-start | bytes 24584 | tf_op jit(solution)/shard_map/ppermute | solution.py:48
  29.3 5.8 %collective-permute-start.17 = (f32[2,8,128]{2,1,0:T(8,128)S(1)}, f32[2,8,128]{2,1,0:T(8,128)S(1)}, u32[]{:S(2)}, u32[]{:S(2)}) collective-permute-start(f32[2,8,128]{2,1,0:T(8,128)S(1)} %shard_map.87.e_ref), channel_id=1, source_target_pairs={{0,112},{16,32},{32,16},{48,64},{64,48},{80,96},{96,80},{112,0},{1... | collective-permute-start | bytes 24584 | tf_op jit(solution)/shard_map/ppermute | solution.py:48
  30.4 4.9 %collective-permute-start.16 = (f32[2,8,128]{2,1,0:T(8,128)S(1)}, f32[2,8,128]{2,1,0:T(8,128)S(1)}, u32[]{:S(2)}, u32[]{:S(2)}) collective-permute-start(f32[2,8,128]{2,1,0:T(8,128)S(1)} %shard_map.87.e_ref), channel_id=1, source_target_pairs={{0,12},{4,8},{8,4},{12,0},{1,13},{5,9},{9,5},{13,1},{2,14},{6,10},... | collective-permute-start | bytes 24584 | tf_op jit(solution)/shard_map/ppermute | solution.py:48
  32.2 4.6 %collective-permute-start.15 = (f32[2,8,128]{2,1,0:T(8,128)S(1)}, f32[2,8,128]{2,1,0:T(8,128)S(1)}, u32[]{:S(2)}, u32[]{:S(2)}) collective-permute-start(f32[2,8,128]{2,1,0:T(8,128)S(1)} %shard_map.87.e_ref), channel_id=1, source_target_pairs={{0,3},{1,2},{2,1},{3,0},{4,7},{5,6},{6,5},{7,4},{8,11},{9,10},{10,... | collective-permute-start | bytes 24584 | tf_op jit(solution)/shard_map/ppermute | solution.py:48
  34.1 3.7 %collective-permute-start.14 = (f32[2,8,128]{2,1,0:T(8,128)S(1)}, f32[2,8,128]{2,1,0:T(8,128)S(1)}, u32[]{:S(2)}, u32[]{:S(2)}) collective-permute-start(f32[2,8,128]{2,1,0:T(8,128)S(1)} %shard_map.87.e_ref), channel_id=1, source_target_pairs={{0,16},{16,0},{32,48},{48,32},{64,80},{80,64},{96,112},{112,96},{1... | collective-permute-start | bytes 24584 | tf_op jit(solution)/shard_map/ppermute | solution.py:48
  38.3 5.8 %collective-permute-start.23 = (f32[2,8,128]{2,1,0:T(8,128)S(1)}, f32[2,8,128]{2,1,0:T(8,128)S(1)}, u32[]{:S(2)}, u32[]{:S(2)}) collective-permute-start(f32[2,8,128]{2,1,0:T(8,128)S(1)} %shard_map.88.e_ref), channel_id=1, source_target_pairs={{0,112},{16,32},{32,16},{48,64},{64,48},{80,96},{96,80},{112,0},{1... | collective-permute-start | bytes 24584 | tf_op jit(solution)/shard_map/ppermute | solution.py:48
  39.1 5.0 %collective-permute-start.22 = (f32[2,8,128]{2,1,0:T(8,128)S(1)}, f32[2,8,128]{2,1,0:T(8,128)S(1)}, u32[]{:S(2)}, u32[]{:S(2)}) collective-permute-start(f32[2,8,128]{2,1,0:T(8,128)S(1)} %shard_map.88.e_ref), channel_id=1, source_target_pairs={{0,12},{4,8},{8,4},{12,0},{1,13},{5,9},{9,5},{13,1},{2,14},{6,10},... | collective-permute-start | bytes 24584 | tf_op jit(solution)/shard_map/ppermute | solution.py:48
  41.8 4.6 %collective-permute-start.21 = (f32[2,8,128]{2,1,0:T(8,128)S(1)}, f32[2,8,128]{2,1,0:T(8,128)S(1)}, u32[]{:S(2)}, u32[]{:S(2)}) collective-permute-start(f32[2,8,128]{2,1,0:T(8,128)S(1)} %shard_map.88.e_ref), channel_id=1, source_target_pairs={{0,3},{1,2},{2,1},{3,0},{4,7},{5,6},{6,5},{7,4},{8,11},{9,10},{10,... | collective-permute-start | bytes 24584 | tf_op jit(solution)/shard_map/ppermute | solution.py:48
  43.1 3.7 %collective-permute-start.20 = (f32[2,8,128]{2,1,0:T(8,128)S(1)}, f32[2,8,128]{2,1,0:T(8,128)S(1)}, u32[]{:S(2)}, u32[]{:S(2)}) collective-permute-start(f32[2,8,128]{2,1,0:T(8,128)S(1)} %shard_map.88.e_ref), channel_id=1, source_target_pairs={{0,16},{16,0},{32,48},{48,32},{64,80},{80,64},{96,112},{112,96},{1... | collective-permute-start | bytes 24584 | tf_op jit(solution)/shard_map/ppermute | solution.py:48
  43.1 3.7 %collective-permute-start.19 = (f32[2,8,128]{2,1,0:T(8,128)S(1)}, f32[2,8,128]{2,1,0:T(8,128)S(1)}, u32[]{:S(2)}, u32[]{:S(2)}) collective-permute-start(f32[2,8,128]{2,1,0:T(8,128)S(1)} %shard_map.88.e_ref), channel_id=1, source_target_pairs={{0,4},{4,0},{8,12},{12,8},{1,5},{5,1},{9,13},{13,9},{2,6},{6,2},{1... | collective-permute-start | bytes 24584 | tf_op jit(solution)/shard_map/ppermute | solution.py:48
  47.3 5.8 %collective-permute-start.29 = (f32[2,8,128]{2,1,0:T(8,128)S(1)}, f32[2,8,128]{2,1,0:T(8,128)S(1)}, u32[]{:S(2)}, u32[]{:S(2)}) collective-permute-start(f32[2,8,128]{2,1,0:T(8,128)S(1)} %shard_map.89.e_ref), channel_id=1, source_target_pairs={{0,112},{16,32},{32,16},{48,64},{64,48},{80,96},{96,80},{112,0},{1... | collective-permute-start | bytes 24584 | tf_op jit(solution)/shard_map/ppermute | solution.py:48
  48.9 4.9 %collective-permute-start.28 = (f32[2,8,128]{2,1,0:T(8,128)S(1)}, f32[2,8,128]{2,1,0:T(8,128)S(1)}, u32[]{:S(2)}, u32[]{:S(2)}) collective-permute-start(f32[2,8,128]{2,1,0:T(8,128)S(1)} %shard_map.89.e_ref), channel_id=1, source_target_pairs={{0,12},{4,8},{8,4},{12,0},{1,13},{5,9},{9,5},{13,1},{2,14},{6,10},... | collective-permute-start | bytes 24584 | tf_op jit(solution)/shard_map/ppermute | solution.py:48
  50.9 4.6 %collective-permute-start.27 = (f32[2,8,128]{2,1,0:T(8,128)S(1)}, f32[2,8,128]{2,1,0:T(8,128)S(1)}, u32[]{:S(2)}, u32[]{:S(2)}) collective-permute-start(f32[2,8,128]{2,1,0:T(8,128)S(1)} %shard_map.89.e_ref), channel_id=1, source_target_pairs={{0,3},{1,2},{2,1},{3,0},{4,7},{5,6},{6,5},{7,4},{8,11},{9,10},{10,... | collective-permute-start | bytes 24584 | tf_op jit(solution)/shard_map/ppermute | solution.py:48
  52.1 3.7 %collective-permute-start.26 = (f32[2,8,128]{2,1,0:T(8,128)S(1)}, f32[2,8,128]{2,1,0:T(8,128)S(1)}, u32[]{:S(2)}, u32[]{:S(2)}) collective-permute-start(f32[2,8,128]{2,1,0:T(8,128)S(1)} %shard_map.89.e_ref), channel_id=1, source_target_pairs={{0,16},{16,0},{32,48},{48,32},{64,80},{80,64},{96,112},{112,96},{1... | collective-permute-start | bytes 24584 | tf_op jit(solution)/shard_map/ppermute | solution.py:48
  52.1 3.7 %collective-permute-start.25 = (f32[2,8,128]{2,1,0:T(8,128)S(1)}, f32[2,8,128]{2,1,0:T(8,128)S(1)}, u32[]{:S(2)}, u32[]{:S(2)}) collective-permute-start(f32[2,8,128]{2,1,0:T(8,128)S(1)} %shard_map.89.e_ref), channel_id=1, source_target_pairs={{0,4},{4,0},{8,12},{12,8},{1,5},{5,1},{9,13},{13,9},{2,6},{6,2},{1... | collective-permute-start | bytes 24584 | tf_op jit(solution)/shard_map/ppermute | solution.py:48
  (14 other events, 92.6 us)

commit v6 on v5

--- a/solution.py
+++ b/solution.py
@@ -432,7 +432,7 @@
                     )
         return carry
 
-    lax.fori_loop(0, 12, vector, 0)
+    lax.fori_loop(0, 12, vector, 0, unroll=2)
     member = ((lane_index(HALF) % NY) // BLOCK == row_index(HALF)).astype(F32)
     for part in range(2):
         out_ref[part] = lax.dot_general(
@@ -564,7 +564,7 @@
             pltpu.make_async_copy(out_ref.at[c, part], out_hbm.at[part, :, c], sems.at[c, part]).start()
         return carry
 
-    lax.fori_loop(0, 12, component, 0)
+    lax.fori_loop(0, 12, component, 0, unroll=2)
     for c in range(12):
         for part in range(2):
             pltpu.make_async_copy(out_ref.at[c, part], out_hbm.at[part, :, c], sems.at[c, part]).wait()

time: 59.6 us -> 59.5 us (level)
  no operation moved by 1% of the time
where the time goes in v6:
time: 59.5 us; the launch traced here: 58.7 us
  starting transfers between devices  31.3 us (53%)
  Pallas kernels  13.1 us (22%)
  waiting for transfers between devices  13 us (22%)
  local copies, waits for them, and re-layouts  1.12 us (2%)
    ppermute x30, starting transfers between devices, swap(): return lax.ppermute(value, axis, pairs)  31.3 us
    ppermute x30, waiting for transfers between devices, swap(): return lax.ppermute(value, axis, pairs)  13 us
    pallas_call x1, Pallas kernels, last(): pl.pallas_call(last_kernel, out_shape=jax.ShapeDtypeStruct((2, 4, 12, ROW...  3.03 us
    pallas_call x1, Pallas kernels, fine(): pl.pallas_call(fine_kernel, out_shape=jax.ShapeDtypeStruct((2, HALF, LANE...  2.98 us
    pallas_call x1, Pallas kernels, centre(): pl.pallas_call(centre_kernel, out_shape=jax.ShapeDtypeStruct((4, 24, ROWS...  2.22 us
    pallas_call x1, Pallas kernels, spread(): pl.pallas_call(spread_kernel, out_shape=jax.ShapeDtypeStruct((9, 3, 24, H...  1.71 us
    pallas_call x3, Pallas kernels, coarse(): pl.pallas_call(coarse_kernel, out_shape=jax.ShapeDtypeStruct((2, HALF, LA...  1.7 us
  transfers between devices with their start and end apart: 30, of which 14 were waited for; matrix products, arithmetic and copies ran while one was open for 0% of the time, Pallas kernels for 8%

profile of v6, /device:TPU:0, one launch (start us, length us, event | category | flops | bytes accessed | tf_op | source)
XLA Modules:
  0.0 58.7 jit_solution(11153528572166339658)
XLA Ops:
  0.0 1.1 %copy-done.4 = bf16[2,4,12,4,4,128]{5,4,3,2,1,0:T(4,128)(2,1)S(1)} copy-done((bf16[2,4,12,4,4,128]{5,4,3,2,1,0:T(4,128)(2,1)S(1)}, bf16[2,4,12,4,4,128]{5,4,3,2,1,0:T(4,128)(2,1)}, u32[]{:S(2)}) %copy-start.4) | copy-done | bytes 393240
  1.9 2.8 %collective-permute-start = (bf16[24,16,128]{2,1,0:T(8,128)(2,1)S(1)}, bf16[24,16,128]{2,1,0:T(8,128)(2,1)S(1)}, u32[]{:S(2)}, u32[]{:S(2)}) collective-permute-start(bf16[24,16,128]{2,1,0:T(8,128)(2,1)S(1)} %get-tuple-element.13), channel_id=1, source_target_pairs={{0,3},{1,2},{2,1},{3,0},{4,7},{5,6},{6,5},{7,4},{8,11},{9,10},{10,... | collective-permute-start | bytes 294920 | tf_op jit(solution)/shard_map/ppermute | solution.py:48
  4.7 4.2 %collective-permute-start.1 = (bf16[24,16,128]{2,1,0:T(8,128)(2,1)S(1)}, bf16[24,16,128]{2,1,0:T(8,128)(2,1)S(1)}, u32[]{:S(2)}, u32[]{:S(2)}) collective-permute-start(bf16[24,16,128]{2,1,0:T(8,128)(2,1)S(1)} %get-tuple-element.14), channel_id=1, source_target_pairs={{0,112},{16,32},{32,16},{48,64},{64,48},{80,96},{96,80},{112,0},{1... | collective-permute-start | bytes 294920 | tf_op jit(solution)/shard_map/ppermute | solution.py:48
  8.9 2.8 %collective-permute-start.2 = (bf16[24,16,128]{2,1,0:T(8,128)(2,1)S(1)}, bf16[24,16,128]{2,1,0:T(8,128)(2,1)S(1)}, u32[]{:S(2)}, u32[]{:S(2)}) collective-permute-start(bf16[24,16,128]{2,1,0:T(8,128)(2,1)S(1)} %get-tuple-element.15), channel_id=1, source_target_pairs={{0,12},{4,8},{8,4},{12,0},{1,13},{5,9},{9,5},{13,1},{2,14},{6,10},... | collective-permute-start | bytes 294920 | tf_op jit(solution)/shard_map/ppermute | solution.py:48
  12.6 2.2 %shard_map.84.partial_ref = f32[4,24,16,128]{3,2,1,0:T(8,128)S(1)} custom-call(f32[2,4,12,16,128]{4,3,2,1,0:T(8,128)S(1)} %get-tuple-element.12.wide_ref.psi_ref, f32[2,4,12,16,128]{4,3,2,1,0:T(8,128)S(1)} %shard_map.83.side_ref, s32[4]{0:T(128)S(1)} %copy-done.6, s32[4]{0:T(128)S(1)} %copy-done.7, f32[3,2,4]{2,1,0:T(2,128)S(1)} %bitcast.16, ...), custom_call_target="tpu_custom_call" | custom-call | flops 40000000 | bytes 20000000 | tf_op jit(solution)/shard_map/pallas_call | solution.py:280
  15.2 1.3 %collective-permute-done.3.ta_ref = bf16[24,16,128]{2,1,0:T(8,128)(2,1)S(1)} collective-permute-done((bf16[24,16,128]{2,1,0:T(8,128)(2,1)S(1)}, bf16[24,16,128]{2,1,0:T(8,128)(2,1)S(1)}, u32[]{:S(2)}, u32[]{:S(2)}) %collective-permute-start.3) | collective-permute-done | bytes 98336 | tf_op jit(solution)/shard_map/ppermute | solution.py:48
  16.5 3.0 %shard_map.85.e_ref.r_ref = f32[2,8,128]{2,1,0:T(8,128)S(1)} custom-call(f32[2,4,12,16,128]{4,3,2,1,0:T(8,128)S(1)} %get-tuple-element.12.wide_ref.psi_ref, f32[4,24,16,128]{3,2,1,0:T(8,128)S(1)} %shard_map.84.partial_ref, bf16[24,16,128]{2,1,0:T(8,128)(2,1)S(1)} %collective-permute-done.xb_ref, bf16[24,16,128]{2,1,0:T(8,128)(2,1)S(1)} %collective-permute-done.1.tb_ref, ...), custom_call_target="tpu_custom_call" | custom-call | flops 40000000 | bytes 20000000 | tf_op jit(solution)/shard_map/pallas_call | solution.py:446
  19.9 2.8 %collective-permute-start.10 = (f32[2,8,128]{2,1,0:T(8,128)S(1)}, f32[2,8,128]{2,1,0:T(8,128)S(1)}, u32[]{:S(2)}, u32[]{:S(2)}) collective-permute-start(f32[2,8,128]{2,1,0:T(8,128)S(1)} %shard_map.85.e_ref.r_ref), channel_id=1, source_target_pairs={{0,12},{4,8},{8,4},{12,0},{1,13},{5,9},{9,5},{13,1},{2,14},{6,10},... | collective-permute-start | bytes 24584 | tf_op jit(solution)/shard_map/ppermute | solution.py:48
  22.7 2.3 %collective-permute-start.9 = (f32[2,8,128]{2,1,0:T(8,128)S(1)}, f32[2,8,128]{2,1,0:T(8,128)S(1)}, u32[]{:S(2)}, u32[]{:S(2)}) collective-permute-start(f32[2,8,128]{2,1,0:T(8,128)S(1)} %shard_map.85.e_ref.r_ref), channel_id=1, source_target_pairs={{0,3},{1,2},{2,1},{3,0},{4,7},{5,6},{6,5},{7,4},{8,11},{9,10},{10,... | collective-permute-start | bytes 24584 | tf_op jit(solution)/shard_map/ppermute | solution.py:48
  25.8 1.7 %shard_map.86.operator_ref = f32[9,3,24,8,128]{4,3,2,1,0:T(8,128)S(1)} custom-call(f32[432,8,24]{2,1,0:T(8,128)S(1)} %bitcast.13), custom_call_target="tpu_custom_call" | custom-call | tf_op jit(solution)/shard_map/pallas_call | solution.py:309
  27.5 1.1 %collective-permute-done.8.ta = f32[2,8,128]{2,1,0:T(8,128)S(1)} collective-permute-done((f32[2,8,128]{2,1,0:T(8,128)S(1)}, f32[2,8,128]{2,1,0:T(8,128)S(1)}, u32[]{:S(2)}, u32[]{:S(2)}) %collective-permute-start.8) | collective-permute-done | bytes 8224 | tf_op jit(solution)/shard_map/ppermute | solution.py:48
  29.2 1.1 %collective-permute-start.17 = (f32[2,8,128]{2,1,0:T(8,128)S(1)}, f32[2,8,128]{2,1,0:T(8,128)S(1)}, u32[]{:S(2)}, u32[]{:S(2)}) collective-permute-start(f32[2,8,128]{2,1,0:T(8,128)S(1)} %shard_map.87.e_ref), channel_id=1, source_target_pairs={{0,112},{16,32},{32,16},{48,64},{64,48},{80,96},{96,80},{112,0},{1... | collective-permute-start | bytes 24584 | tf_op jit(solution)/shard_map/ppermute | solution.py:48
  30.3 1.9 %collective-permute-start.16 = (f32[2,8,128]{2,1,0:T(8,128)S(1)}, f32[2,8,128]{2,1,0:T(8,128)S(1)}, u32[]{:S(2)}, u32[]{:S(2)}) collective-permute-start(f32[2,8,128]{2,1,0:T(8,128)S(1)} %shard_map.87.e_ref), channel_id=1, source_target_pairs={{0,12},{4,8},{8,4},{12,0},{1,13},{5,9},{9,5},{13,1},{2,14},{6,10},... | collective-permute-start | bytes 24584 | tf_op jit(solution)/shard_map/ppermute | solution.py:48
  32.2 1.9 %collective-permute-start.15 = (f32[2,8,128]{2,1,0:T(8,128)S(1)}, f32[2,8,128]{2,1,0:T(8,128)S(1)}, u32[]{:S(2)}, u32[]{:S(2)}) collective-permute-start(f32[2,8,128]{2,1,0:T(8,128)S(1)} %shard_map.87.e_ref), channel_id=1, source_target_pairs={{0,3},{1,2},{2,1},{3,0},{4,7},{5,6},{6,5},{7,4},{8,11},{9,10},{10,... | collective-permute-start | bytes 24584 | tf_op jit(solution)/shard_map/ppermute | solution.py:48
  35.2 1.5 %collective-permute-done.15.xb = f32[2,8,128]{2,1,0:T(8,128)S(1)} collective-permute-done((f32[2,8,128]{2,1,0:T(8,128)S(1)}, f32[2,8,128]{2,1,0:T(8,128)S(1)}, u32[]{:S(2)}, u32[]{:S(2)}) %collective-permute-start.15) | collective-permute-done | bytes 8224 | tf_op jit(solution)/shard_map/ppermute | solution.py:48
  39.0 2.8 %collective-permute-start.22 = (f32[2,8,128]{2,1,0:T(8,128)S(1)}, f32[2,8,128]{2,1,0:T(8,128)S(1)}, u32[]{:S(2)}, u32[]{:S(2)}) collective-permute-start(f32[2,8,128]{2,1,0:T(8,128)S(1)} %shard_map.88.e_ref), channel_id=1, source_target_pairs={{0,12},{4,8},{8,4},{12,0},{1,13},{5,9},{9,5},{13,1},{2,14},{6,10},... | collective-permute-start | bytes 24584 | tf_op jit(solution)/shard_map/ppermute | solution.py:48
  41.8 1.2 %collective-permute-start.21 = (f32[2,8,128]{2,1,0:T(8,128)S(1)}, f32[2,8,128]{2,1,0:T(8,128)S(1)}, u32[]{:S(2)}, u32[]{:S(2)}) collective-permute-start(f32[2,8,128]{2,1,0:T(8,128)S(1)} %shard_map.88.e_ref), channel_id=1, source_target_pairs={{0,3},{1,2},{2,1},{3,0},{4,7},{5,6},{6,5},{7,4},{8,11},{9,10},{10,... | collective-permute-start | bytes 24584 | tf_op jit(solution)/shard_map/ppermute | solution.py:48
  43.0 1.1 %collective-permute-done.23.tb = f32[2,8,128]{2,1,0:T(8,128)S(1)} collective-permute-done((f32[2,8,128]{2,1,0:T(8,128)S(1)}, f32[2,8,128]{2,1,0:T(8,128)S(1)}, u32[]{:S(2)}, u32[]{:S(2)}) %collective-permute-start.23) | collective-permute-done | bytes 8224 | tf_op jit(solution)/shard_map/ppermute | solution.py:48
  44.0 2.3 %collective-permute-done.21.xb = f32[2,8,128]{2,1,0:T(8,128)S(1)} collective-permute-done((f32[2,8,128]{2,1,0:T(8,128)S(1)}, f32[2,8,128]{2,1,0:T(8,128)S(1)}, u32[]{:S(2)}, u32[]{:S(2)}) %collective-permute-start.21) | collective-permute-done | bytes 8224 | tf_op jit(solution)/shard_map/ppermute | solution.py:48
  47.2 1.6 %collective-permute-start.29 = (f32[2,8,128]{2,1,0:T(8,128)S(1)}, f32[2,8,128]{2,1,0:T(8,128)S(1)}, u32[]{:S(2)}, u32[]{:S(2)}) collective-permute-start(f32[2,8,128]{2,1,0:T(8,128)S(1)} %shard_map.89.e_ref), channel_id=1, source_target_pairs={{0,112},{16,32},{32,16},{48,64},{64,48},{80,96},{96,80},{112,0},{1... | collective-permute-start | bytes 24584 | tf_op jit(solution)/shard_map/ppermute | solution.py:48
  48.8 2.0 %collective-permute-start.28 = (f32[2,8,128]{2,1,0:T(8,128)S(1)}, f32[2,8,128]{2,1,0:T(8,128)S(1)}, u32[]{:S(2)}, u32[]{:S(2)}) collective-permute-start(f32[2,8,128]{2,1,0:T(8,128)S(1)} %shard_map.89.e_ref), channel_id=1, source_target_pairs={{0,12},{4,8},{8,4},{12,0},{1,13},{5,9},{9,5},{13,1},{2,14},{6,10},... | collective-permute-start | bytes 24584 | tf_op jit(solution)/shard_map/ppermute | solution.py:48
  50.8 1.2 %collective-permute-start.27 = (f32[2,8,128]{2,1,0:T(8,128)S(1)}, f32[2,8,128]{2,1,0:T(8,128)S(1)}, u32[]{:S(2)}, u32[]{:S(2)}) collective-permute-start(f32[2,8,128]{2,1,0:T(8,128)S(1)} %shard_map.89.e_ref), channel_id=1, source_target_pairs={{0,3},{1,2},{2,1},{3,0},{4,7},{5,6},{6,5},{7,4},{8,11},{9,10},{10,... | collective-permute-start | bytes 24584 | tf_op jit(solution)/shard_map/ppermute | solution.py:48
  53.7 1.7 %collective-permute-done.27.xb = f32[2,8,128]{2,1,0:T(8,128)S(1)} collective-permute-done((f32[2,8,128]{2,1,0:T(8,128)S(1)}, f32[2,8,128]{2,1,0:T(8,128)S(1)}, u32[]{:S(2)}, u32[]{:S(2)}) %collective-permute-start.27) | collective-permute-done | bytes 8224 | tf_op jit(solution)/shard_map/ppermute | solution.py:48
  55.7 3.0 %shard_map.90 = f32[2,4,12,16,128]{4,3,2,1,0:T(8,128)} custom-call(f32[2,8,128]{2,1,0:T(8,128)S(1)} %shard_map.89.e_ref, f32[2,8,128]{2,1,0:T(8,128)S(1)} %collective-permute-done.24.xa, f32[2,8,128]{2,1,0:T(8,128)S(1)} %collective-permute-done.25.za, f32[2,8,128]{2,1,0:T(8,128)S(1)} %collective-permute-done.26.ta, ...), custom_call_target="tpu_custom_call" | custom-call | tf_op jit(solution)/shard_map/pallas_call | solution.py:575
  (61 shorter events, 10.2 us)
Async XLA Ops:
  1.9 9.9 %collective-permute-start = (bf16[24,16,128]{2,1,0:T(8,128)(2,1)S(1)}, bf16[24,16,128]{2,1,0:T(8,128)(2,1)S(1)}, u32[]{:S(2)}, u32[]{:S(2)}) collective-permute-start(bf16[24,16,128]{2,1,0:T(8,128)(2,1)S(1)} %get-tuple-element.13), channel_id=1, source_target_pairs={{0,3},{1,2},{2,1},{3,0},{4,7},{5,6},{6,5},{7,4},{8,11},{9,10},{10,... | collective-permute-start | bytes 294920 | tf_op jit(solution)/shard_map/ppermute | solution.py:48
  4.7 10.1 %collective-permute-start.1 = (bf16[24,16,128]{2,1,0:T(8,128)(2,1)S(1)}, bf16[24,16,128]{2,1,0:T(8,128)(2,1)S(1)}, u32[]{:S(2)}, u32[]{:S(2)}) collective-permute-start(bf16[24,16,128]{2,1,0:T(8,128)(2,1)S(1)} %get-tuple-element.14), channel_id=1, source_target_pairs={{0,112},{16,32},{32,16},{48,64},{64,48},{80,96},{96,80},{112,0},{1... | collective-permute-start | bytes 294920 | tf_op jit(solution)/shard_map/ppermute | solution.py:48
  8.9 6.3 %collective-permute-start.2 = (bf16[24,16,128]{2,1,0:T(8,128)(2,1)S(1)}, bf16[24,16,128]{2,1,0:T(8,128)(2,1)S(1)}, u32[]{:S(2)}, u32[]{:S(2)}) collective-permute-start(bf16[24,16,128]{2,1,0:T(8,128)(2,1)S(1)} %get-tuple-element.15), channel_id=1, source_target_pairs={{0,12},{4,8},{8,4},{12,0},{1,13},{5,9},{9,5},{13,1},{2,14},{6,10},... | collective-permute-start | bytes 294920 | tf_op jit(solution)/shard_map/ppermute | solution.py:48
  11.6 4.8 %collective-permute-start.3 = (bf16[24,16,128]{2,1,0:T(8,128)(2,1)S(1)}, bf16[24,16,128]{2,1,0:T(8,128)(2,1)S(1)}, u32[]{:S(2)}, u32[]{:S(2)}) collective-permute-start(bf16[24,16,128]{2,1,0:T(8,128)(2,1)S(1)} %get-tuple-element.16), channel_id=1, source_target_pairs={{0,16},{16,0},{32,48},{48,32},{64,80},{80,64},{96,112},{112,96},{1... | collective-permute-start | bytes 294920 | tf_op jit(solution)/shard_map/ppermute | solution.py:48
  11.6 4.8 %collective-permute-start.4 = (bf16[24,16,128]{2,1,0:T(8,128)(2,1)S(1)}, bf16[24,16,128]{2,1,0:T(8,128)(2,1)S(1)}, u32[]{:S(2)}, u32[]{:S(2)}) collective-permute-start(bf16[24,16,128]{2,1,0:T(8,128)(2,1)S(1)} %get-tuple-element.17), channel_id=1, source_target_pairs={{0,4},{4,0},{8,12},{12,8},{1,5},{5,1},{9,13},{13,9},{2,6},{6,2},{1... | collective-permute-start | bytes 294920 | tf_op jit(solution)/shard_map/ppermute | solution.py:48
  11.8 4.6 %collective-permute-start.5 = (bf16[24,16,128]{2,1,0:T(8,128)(2,1)S(1)}, bf16[24,16,128]{2,1,0:T(8,128)(2,1)S(1)}, u32[]{:S(2)}, u32[]{:S(2)}) collective-permute-start(bf16[24,16,128]{2,1,0:T(8,128)(2,1)S(1)} %get-tuple-element.18), channel_id=1, source_target_pairs={{0,1},{1,0},{2,3},{3,2},{4,5},{5,4},{6,7},{7,6},{8,9},{9,8},{10,11... | collective-permute-start | bytes 294920 | tf_op jit(solution)/shard_map/ppermute | solution.py:48
  19.5 5.8 %collective-permute-start.11 = (f32[2,8,128]{2,1,0:T(8,128)S(1)}, f32[2,8,128]{2,1,0:T(8,128)S(1)}, u32[]{:S(2)}, u32[]{:S(2)}) collective-permute-start(f32[2,8,128]{2,1,0:T(8,128)S(1)} %shard_map.85.e_ref.r_ref), channel_id=1, source_target_pairs={{0,112},{16,32},{32,16},{48,64},{64,48},{80,96},{96,80},{112,0},{1... | collective-permute-start | bytes 24584 | tf_op jit(solution)/shard_map/ppermute | solution.py:48
  19.9 7.6 %collective-permute-start.10 = (f32[2,8,128]{2,1,0:T(8,128)S(1)}, f32[2,8,128]{2,1,0:T(8,128)S(1)}, u32[]{:S(2)}, u32[]{:S(2)}) collective-permute-start(f32[2,8,128]{2,1,0:T(8,128)S(1)} %shard_map.85.e_ref.r_ref), channel_id=1, source_target_pairs={{0,12},{4,8},{8,4},{12,0},{1,13},{5,9},{9,5},{13,1},{2,14},{6,10},... | collective-permute-start | bytes 24584 | tf_op jit(solution)/shard_map/ppermute | solution.py:48
  22.7 4.8 %collective-permute-start.9 = (f32[2,8,128]{2,1,0:T(8,128)S(1)}, f32[2,8,128]{2,1,0:T(8,128)S(1)}, u32[]{:S(2)}, u32[]{:S(2)}) collective-permute-start(f32[2,8,128]{2,1,0:T(8,128)S(1)} %shard_map.85.e_ref.r_ref), channel_id=1, source_target_pairs={{0,3},{1,2},{2,1},{3,0},{4,7},{5,6},{6,5},{7,4},{8,11},{9,10},{10,... | collective-permute-start | bytes 24584 | tf_op jit(solution)/shard_map/ppermute | solution.py:48
  25.0 3.7 %collective-permute-start.8 = (f32[2,8,128]{2,1,0:T(8,128)S(1)}, f32[2,8,128]{2,1,0:T(8,128)S(1)}, u32[]{:S(2)}, u32[]{:S(2)}) collective-permute-start(f32[2,8,128]{2,1,0:T(8,128)S(1)} %shard_map.85.e_ref.r_ref), channel_id=1, source_target_pairs={{0,16},{16,0},{32,48},{48,32},{64,80},{80,64},{96,112},{112,96},{1... | collective-permute-start | bytes 24584 | tf_op jit(solution)/shard_map/ppermute | solution.py:48
  25.0 3.7 %collective-permute-start.7 = (f32[2,8,128]{2,1,0:T(8,128)S(1)}, f32[2,8,128]{2,1,0:T(8,128)S(1)}, u32[]{:S(2)}, u32[]{:S(2)}) collective-permute-start(f32[2,8,128]{2,1,0:T(8,128)S(1)} %shard_map.85.e_ref.r_ref), channel_id=1, source_target_pairs={{0,4},{4,0},{8,12},{12,8},{1,5},{5,1},{9,13},{13,9},{2,6},{6,2},{1... | collective-permute-start | bytes 24584 | tf_op jit(solution)/shard_map/ppermute | solution.py:48
  29.2 5.8 %collective-permute-start.17 = (f32[2,8,128]{2,1,0:T(8,128)S(1)}, f32[2,8,128]{2,1,0:T(8,128)S(1)}, u32[]{:S(2)}, u32[]{:S(2)}) collective-permute-start(f32[2,8,128]{2,1,0:T(8,128)S(1)} %shard_map.87.e_ref), channel_id=1, source_target_pairs={{0,112},{16,32},{32,16},{48,64},{64,48},{80,96},{96,80},{112,0},{1... | collective-permute-start | bytes 24584 | tf_op jit(solution)/shard_map/ppermute | solution.py:48
  30.3 4.9 %collective-permute-start.16 = (f32[2,8,128]{2,1,0:T(8,128)S(1)}, f32[2,8,128]{2,1,0:T(8,128)S(1)}, u32[]{:S(2)}, u32[]{:S(2)}) collective-permute-start(f32[2,8,128]{2,1,0:T(8,128)S(1)} %shard_map.87.e_ref), channel_id=1, source_target_pairs={{0,12},{4,8},{8,4},{12,0},{1,13},{5,9},{9,5},{13,1},{2,14},{6,10},... | collective-permute-start | bytes 24584 | tf_op jit(solution)/shard_map/ppermute | solution.py:48
  32.2 4.6 %collective-permute-start.15 = (f32[2,8,128]{2,1,0:T(8,128)S(1)}, f32[2,8,128]{2,1,0:T(8,128)S(1)}, u32[]{:S(2)}, u32[]{:S(2)}) collective-permute-start(f32[2,8,128]{2,1,0:T(8,128)S(1)} %shard_map.87.e_ref), channel_id=1, source_target_pairs={{0,3},{1,2},{2,1},{3,0},{4,7},{5,6},{6,5},{7,4},{8,11},{9,10},{10,... | collective-permute-start | bytes 24584 | tf_op jit(solution)/shard_map/ppermute | solution.py:48
  38.2 5.8 %collective-permute-start.23 = (f32[2,8,128]{2,1,0:T(8,128)S(1)}, f32[2,8,128]{2,1,0:T(8,128)S(1)}, u32[]{:S(2)}, u32[]{:S(2)}) collective-permute-start(f32[2,8,128]{2,1,0:T(8,128)S(1)} %shard_map.88.e_ref), channel_id=1, source_target_pairs={{0,112},{16,32},{32,16},{48,64},{64,48},{80,96},{96,80},{112,0},{1... | collective-permute-start | bytes 24584 | tf_op jit(solution)/shard_map/ppermute | solution.py:48
  39.0 5.0 %collective-permute-start.22 = (f32[2,8,128]{2,1,0:T(8,128)S(1)}, f32[2,8,128]{2,1,0:T(8,128)S(1)}, u32[]{:S(2)}, u32[]{:S(2)}) collective-permute-start(f32[2,8,128]{2,1,0:T(8,128)S(1)} %shard_map.88.e_ref), channel_id=1, source_target_pairs={{0,12},{4,8},{8,4},{12,0},{1,13},{5,9},{9,5},{13,1},{2,14},{6,10},... | collective-permute-start | bytes 24584 | tf_op jit(solution)/shard_map/ppermute | solution.py:48
  41.8 4.6 %collective-permute-start.21 = (f32[2,8,128]{2,1,0:T(8,128)S(1)}, f32[2,8,128]{2,1,0:T(8,128)S(1)}, u32[]{:S(2)}, u32[]{:S(2)}) collective-permute-start(f32[2,8,128]{2,1,0:T(8,128)S(1)} %shard_map.88.e_ref), channel_id=1, source_target_pairs={{0,3},{1,2},{2,1},{3,0},{4,7},{5,6},{6,5},{7,4},{8,11},{9,10},{10,... | collective-permute-start | bytes 24584 | tf_op jit(solution)/shard_map/ppermute | solution.py:48
  43.0 3.7 %collective-permute-start.20 = (f32[2,8,128]{2,1,0:T(8,128)S(1)}, f32[2,8,128]{2,1,0:T(8,128)S(1)}, u32[]{:S(2)}, u32[]{:S(2)}) collective-permute-start(f32[2,8,128]{2,1,0:T(8,128)S(1)} %shard_map.88.e_ref), channel_id=1, source_target_pairs={{0,16},{16,0},{32,48},{48,32},{64,80},{80,64},{96,112},{112,96},{1... | collective-permute-start | bytes 24584 | tf_op jit(solution)/shard_map/ppermute | solution.py:48
  43.0 3.7 %collective-permute-start.19 = (f32[2,8,128]{2,1,0:T(8,128)S(1)}, f32[2,8,128]{2,1,0:T(8,128)S(1)}, u32[]{:S(2)}, u32[]{:S(2)}) collective-permute-start(f32[2,8,128]{2,1,0:T(8,128)S(1)} %shard_map.88.e_ref), channel_id=1, source_target_pairs={{0,4},{4,0},{8,12},{12,8},{1,5},{5,1},{9,13},{13,9},{2,6},{6,2},{1... | collective-permute-start | bytes 24584 | tf_op jit(solution)/shard_map/ppermute | solution.py:48
  47.2 5.8 %collective-permute-start.29 = (f32[2,8,128]{2,1,0:T(8,128)S(1)}, f32[2,8,128]{2,1,0:T(8,128)S(1)}, u32[]{:S(2)}, u32[]{:S(2)}) collective-permute-start(f32[2,8,128]{2,1,0:T(8,128)S(1)} %shard_map.89.e_ref), channel_id=1, source_target_pairs={{0,112},{16,32},{32,16},{48,64},{64,48},{80,96},{96,80},{112,0},{1... | collective-permute-start | bytes 24584 | tf_op jit(solution)/shard_map/ppermute | solution.py:48
  48.8 4.9 %collective-permute-start.28 = (f32[2,8,128]{2,1,0:T(8,128)S(1)}, f32[2,8,128]{2,1,0:T(8,128)S(1)}, u32[]{:S(2)}, u32[]{:S(2)}) collective-permute-start(f32[2,8,128]{2,1,0:T(8,128)S(1)} %shard_map.89.e_ref), channel_id=1, source_target_pairs={{0,12},{4,8},{8,4},{12,0},{1,13},{5,9},{9,5},{13,1},{2,14},{6,10},... | collective-permute-start | bytes 24584 | tf_op jit(solution)/shard_map/ppermute | solution.py:48
  50.8 4.6 %collective-permute-start.27 = (f32[2,8,128]{2,1,0:T(8,128)S(1)}, f32[2,8,128]{2,1,0:T(8,128)S(1)}, u32[]{:S(2)}, u32[]{:S(2)}) collective-permute-start(f32[2,8,128]{2,1,0:T(8,128)S(1)} %shard_map.89.e_ref), channel_id=1, source_target_pairs={{0,3},{1,2},{2,1},{3,0},{4,7},{5,6},{6,5},{7,4},{8,11},{9,10},{10,... | collective-permute-start | bytes 24584 | tf_op jit(solution)/shard_map/ppermute | solution.py:48
  52.0 3.7 %collective-permute-start.26 = (f32[2,8,128]{2,1,0:T(8,128)S(1)}, f32[2,8,128]{2,1,0:T(8,128)S(1)}, u32[]{:S(2)}, u32[]{:S(2)}) collective-permute-start(f32[2,8,128]{2,1,0:T(8,128)S(1)} %shard_map.89.e_ref), channel_id=1, source_target_pairs={{0,16},{16,0},{32,48},{48,32},{64,80},{80,64},{96,112},{112,96},{1... | collective-permute-start | bytes 24584 | tf_op jit(solution)/shard_map/ppermute | solution.py:48
  52.0 3.7 %collective-permute-start.25 = (f32[2,8,128]{2,1,0:T(8,128)S(1)}, f32[2,8,128]{2,1,0:T(8,128)S(1)}, u32[]{:S(2)}, u32[]{:S(2)}) collective-permute-start(f32[2,8,128]{2,1,0:T(8,128)S(1)} %shard_map.89.e_ref), channel_id=1, source_target_pairs={{0,4},{4,0},{8,12},{12,8},{1,5},{5,1},{9,13},{13,9},{2,6},{6,2},{1... | collective-permute-start | bytes 24584 | tf_op jit(solution)/shard_map/ppermute | solution.py:48
  (14 other events, 92.5 us)
